TPU v7x, 1024 devices: a whole 4x4x32 slice. The times are simulated.
1024 devices in a mesh: dp: 16 (over x, z_hi), space: 64 (over y, z_lo, core).
Axes of the slice: x: 4, y: 4, z: 32 (z_hi: 4, z_lo: 8; z = z_hi * 8 + z_lo), core: 2. Of those that a mesh axis runs over, the one named last changes fastest.
Arguments:
- volume: bfloat16 [16, 128, 8, 64, 128], P('dp', 'space'), may hold values from -6 to 6
- weight: bfloat16 [3, 3, 3, 64, 128], replicated, may hold values from -0.15625 to 0.15625
- cotangent: bfloat16 [16, 64, 4, 64, 128], P('dp', 'space'), may hold values from -6 to 6
Outputs:
- output: bfloat16 [16, 64, 4, 64, 128], P('dp', 'space')
- grad_volume: bfloat16 [16, 128, 8, 64, 128], P('dp', 'space')
- grad_weight: float32 [3, 3, 3, 64, 128], replicated
All inputs are finite; a program needn't handle non-finite values.
Results may differ from a plain program's by a relative error of at most 0.0034.
Values may be sent and summed in bfloat16 or wider, within the bound.
No kernel may reach another device: no remote copies, remote signals or barrier semaphores. Data moves between devices by JAX's collectives and lax.ppermute only.
A program may use at most 32 MiB of HBM per device.

v0:
```python
import math

import jax
import jax.numpy as jnp
from jax import lax
from jax.sharding import PartitionSpec as P


def passed_along(value, axis, steps):
    count = lax.axis_size(axis)
    first, last = (max(0, -steps), min(count, count - steps))
    return lax.ppermute(value, axis, [(source, source + steps) for source in range(first, last)])


def tap_patches(planes, rows_out):
    channels = planes.shape[3]
    half_width = channels // 2
    padded = jnp.pad(planes, ((0, 0), (1, 0), (1, 0), (0, 0)))
    pieces = []
    for depth_tap in range(3):
        for height_tap in range(3):
            strided = padded[depth_tap, height_tap : height_tap + 2 * rows_out : 2]
            pieces.append(strided[:, 1:, :])
            pieces.append(strided[:, :-1, half_width:])
    patches = jnp.concatenate(pieces, axis=-1)
    return patches.reshape(rows_out * patches.shape[1], patches.shape[2])


def weight_matrix(weight):
    joined = jnp.concatenate([weight[:, :, 1], weight[:, :, 2], weight[:, :, 0]], axis=2)
    return joined.reshape(-1, weight.shape[4])


def spread(grads, rows_out, pairs, cin):
    shaped = grads.reshape(rows_out, pairs, 3, 3 * cin)
    current = shaped[..., : 2 * cin]
    leftward = shaped[..., 2 * cin :]
    left_pair = jnp.concatenate([jnp.zeros_like(leftward), leftward], axis=-1)
    moved = jnp.pad(left_pair[:, 1:], ((0, 0), (0, 1), (0, 0), (0, 0)))
    per_row = current + moved
    even_rows = per_row[:, :, 1]
    odd_rows = per_row[:, :, 2] + jnp.pad(per_row[1:, :, 0], ((0, 1), (0, 0), (0, 0)))
    return jnp.stack([even_rows, odd_rows], axis=1).reshape(2 * rows_out, pairs, 2 * cin)


def shards(volume, weight, cotangent):
    local = volume[0]
    rows_out = cotangent.shape[2]
    pairs = cotangent.shape[3]
    cout = cotangent.shape[4]
    cin = weight.shape[3]
    rim = passed_along(local[1:2], "space", 1)
    planes = jnp.concatenate([rim, local], axis=0)
    patches = tap_patches(planes, rows_out)
    matrix = weight_matrix(weight)
    result = jnp.dot(patches, matrix, preferred_element_type=jnp.float32)
    output = result.astype(jnp.bfloat16).reshape(1, 1, rows_out, pairs, cout)
    grad_rows = cotangent.reshape(rows_out * pairs, cout)
    local_terms = lax.dot_general(
        patches, grad_rows, (((0,), (0,)), ((), ())), preferred_element_type=jnp.float32
    )
    per_depth = matrix.reshape(3, -1, cout)

    def backward_tap(rows_in, depth_tap):
        return lax.dot_general(
            rows_in,
            per_depth[depth_tap],
            (((1,), (1,)), ((), ())),
            preferred_element_type=jnp.float32,
        )

    spill = spread(backward_tap(grad_rows, 0), rows_out, pairs, cin)
    incoming = passed_along(spill, "space", -1)
    first_plane = spread(backward_tap(grad_rows, 1), rows_out, pairs, cin)
    second_plane = spread(backward_tap(grad_rows, 2), rows_out, pairs, cin) + incoming
    grad_volume = jnp.stack([first_plane, second_plane])[None].astype(jnp.bfloat16)
    blocks = local_terms.reshape(3, 3, 3, cin, cout)
    arranged = jnp.stack([blocks[:, :, 2], blocks[:, :, 0], blocks[:, :, 1]], axis=2)
    summed = lax.psum(arranged, ("dp", "space"))
    factor = 1.0 / math.sqrt(lax.axis_size("dp") * lax.axis_size("space") * rows_out * pairs)
    return (output, grad_volume, summed * factor)


def solution(mesh):
    return jax.shard_map(
        shards,
        mesh=mesh,
        in_specs=(P("dp", "space", None, None, None), P(), P("dp", "space", None, None, None)),
        out_specs=(P("dp", "space", None, None, None), P("dp", "space", None, None, None), P()),
        check_vma=False,
    )
```

profile of v0, /device:TPU:1, one launch (start us, length us, event | category | flops | bytes accessed | tf_op | source)
XLA Modules:
  0.0 940.6 jit_solution(15648577681022171018)
XLA Ops:
  7.2 1.1 slice_bitcast_fusion.2
  8.4 0.2 convolution_bitcast_fusion
  8.6 0.2 copy.34
  8.9 0.4 reshape.83
  9.4 0.3 pad_slice_fusion
  9.8 0.1 slice_add_fusion
  9.9 0.2 fusion.12
  10.3 16.2 %collective-permute-start.1 = (f32[8,64,128]{2,1,0:T(8,128)S(1)}, f32[8,64,128]{2,1,0:T(8,128)S(1)}, u32[]{:S(2)}, u32[]{:S(2)}) collective-permute-start(f32[8,64,128]{2,1,0:T(8,128)S(1)} %bitcast.121), channel_id=1, source_target_pairs={{1,0},{2,1},{3,2},{4,3},{5,4},{6,5},{7,6},{8,7},{9,8},{10,9},{11,1... | collective-permute-start | bytes 786440 | tf_op jit(solution)/shard_map/ppermute | solution.py:12
  26.5 0.7 slice_bitcast_fusion.3
  27.2 1.9 collective-permute-start
  29.1 0.2 convolution_bitcast_fusion.1
  29.3 0.2 copy.30
  29.6 0.4 reshape.81
  30.1 0.3 pad_slice_fusion.1
  30.5 0.1 slice_add_fusion.1
  30.6 0.2 fusion.11
  30.9 0.2 convolution_bitcast_fusion.2
  31.2 0.2 copy.26
  31.4 0.4 reshape.80
  31.9 0.3 pad_slice_fusion.2
  32.3 0.1 slice_add_fusion.2
  32.4 0.1 slice.248
  32.7 0.1 slice.247
  33.0 1.0 fusion.5
  35.2 0.5 concatenate.27
  35.7 0.6 copy.38
  36.3 0.4 fusion.14
  36.7 1.0 pad_maximum_fusion
  37.8 1.0 convolution_convert_fusion
  38.8 0.7 pad_maximum_fusion.4
  39.6 892.0 %all-reduce.12.cloned.1.call-done = f32[3,3,3,64,128]{4,3,2,1,0:T(8,128)} async-done(((f32[3,3,3,64,128]{4,3,2,1,0:T(8,128)}), f32[3,3,3,64,128]{4,3,2,1,0:T(8,128)}) %all-reduce.12.cloned.1.call-update) | async-done | bytes 884752 | tf_op jit(solution)/shard_map/psum | solution.py:79
  931.6 2.2 broadcast_multiply_fusion
  (48 shorter events, 1.9 us)
Async XLA Ops:
  7.2 1.2 copy-start
  7.2 924.4 %all-reduce.12.cloned.1.call-start = ((), (), s32[]{:S(2)}) async-start(), calls=%async_computation | async-start | bytes 1769472 | tf_op jit(solution)/shard_map/psum | solution.py:79
  10.3 16.2 %copy-start.1 = (bf16[1,2,8,64,128]{4,3,2,1,0:T(8,128)(2,1)S(1)}, bf16[1,2,8,64,128]{4,3,2,1,0:T(8,128)(2,1)}, u32[]{:S(2)}) copy-start(bf16[1,2,8,64,128]{4,3,2,1,0:T(8,128)(2,1)} %param.3) | copy-start | bytes 786436
  10.3 28.5 %collective-permute-start.1 = (f32[8,64,128]{2,1,0:T(8,128)S(1)}, f32[8,64,128]{2,1,0:T(8,128)S(1)}, u32[]{:S(2)}, u32[]{:S(2)}) collective-permute-start(f32[8,64,128]{2,1,0:T(8,128)S(1)} %bitcast.121), channel_id=1, source_target_pairs={{1,0},{2,1},{3,2},{4,3},{5,4},{6,5},{7,6},{8,7},{9,8},{10,9},{11,1... | collective-permute-start | bytes 786440 | tf_op jit(solution)/shard_map/ppermute | solution.py:12
  27.2 5.8 collective-permute-start
Sparse Core Ops, SparseCore 0:
  37.9 893.6 all-reduce.11
where the time goes:
time: 941 us
  waiting for transfers between devices  892 us (95%)
  starting transfers between devices  18.1 us (2%)
  between operations  14.5 us (2%)
    psum x1, waiting for transfers between devices, shards(): summed = lax.psum(arranged, ('dp', 'space'))  892 us
  transfers between devices with their start and end apart: 3, of which 1 were waited for; matrix products, arithmetic and copies ran while one was open for 1% of the time, Pallas kernels for 0%

commit v1 on v0

v1 whole, which is shorter than its diff:
```python
import math

import jax
import jax.numpy as jnp
from jax import lax
from jax.experimental import pallas as pl
from jax.experimental.pallas import tpu as pltpu
from jax.sharding import PartitionSpec as P

DP = ("x", "zh")
SPACE = ("y", "zl", "c")
PLANE = ("x", "y", "c")
SIZES = (4, 4, 4, 8, 2)
VMEM_BYTES = 16 << 20


def passed_along(value, axes, steps):
    count = math.prod(lax.axis_size(axis) for axis in axes)
    first, last = (max(0, -steps), min(count, count - steps))
    return lax.ppermute(value, axes, [(source, source + steps) for source in range(first, last)])


def exchange(value, axes):
    return lax.all_to_all(value, axes, 0, 0, tiled=True)


def with_next_pair(cells, pairs):
    wide = cells.astype(jnp.float32)
    rows = wide.shape[0]
    row = lax.broadcasted_iota(jnp.int32, wide.shape, 0)
    ahead = jnp.where(row % pairs == pairs - 1, 0.0, pltpu.roll(wide, rows - 1, 0))
    return jnp.concatenate([cells, ahead.astype(jnp.bfloat16)], axis=1)


def from_previous_pair(wide, pairs):
    row = lax.broadcasted_iota(jnp.int32, wide.shape, 0)
    return jnp.where(row % pairs == 0, 0.0, pltpu.roll(wide, 1, 0))


def plane_rows(plane, rows_out):
    even = jnp.concatenate([plane[2 * b] for b in range(rows_out)], axis=0)
    odd = jnp.concatenate([plane[2 * b + 1] for b in range(rows_out)], axis=0)
    return even, odd


def tap_weight(weight, depth_tap, height_tap):
    taps = weight[depth_tap, height_tap]
    pair = jnp.concatenate([taps[1], taps[2]], axis=0)
    left = jnp.concatenate([jnp.zeros_like(taps[0]), taps[0]], axis=0)
    return jnp.concatenate([pair, left], axis=1)


def forward_dot(rows, weight):
    return lax.dot_general(
        rows, weight, (((1,), (0,)), ((), ())), preferred_element_type=jnp.float32
    )


def backward_dot(rows, weight):
    return lax.dot_general(
        rows, weight, (((1,), (1,)), ((), ())), preferred_element_type=jnp.float32
    )


def kernel_dot(rows, grads):
    return lax.dot_general(
        rows, grads, (((0,), (0,)), ((), ())), preferred_element_type=jnp.float32
    )


def store_kernel_terms(terms_ref, depth_tap, plane, grads, rows_out, pairs, cin, cout):
    even, odd = plane_rows(plane, rows_out)
    kept = (rows_out - 1) * pairs
    products = (
        kernel_dot(odd[:kept], grads[pairs:]),
        kernel_dot(even, grads),
        kernel_dot(odd, grads),
    )
    for height_tap in range(3):
        product = products[height_tap]
        base = (depth_tap * 3 + height_tap) * 3 * cin
        terms_ref[base : base + cin] = product[cin:, cout:]
        terms_ref[base + cin : base + 3 * cin] = product[:, :cout]


def forward_terms(plane, weight, depth_tap, rows_out, pairs):
    even, odd = plane_rows(plane, rows_out)
    lifted = jnp.concatenate([jnp.zeros_like(odd[:pairs]), odd[: (rows_out - 1) * pairs]], axis=0)
    return (
        forward_dot(lifted, tap_weight(weight, depth_tap, 0))
        + forward_dot(even, tap_weight(weight, depth_tap, 1))
        + forward_dot(odd, tap_weight(weight, depth_tap, 2))
    )


def backward_terms(grads, weight, depth_tap, pairs):
    raised = jnp.concatenate([grads[pairs:], jnp.zeros_like(grads[:pairs])], axis=0)
    even = backward_dot(grads, tap_weight(weight, depth_tap, 1))
    odd = backward_dot(grads, tap_weight(weight, depth_tap, 2)) + backward_dot(
        raised, tap_weight(weight, depth_tap, 0)
    )
    return even, odd


def own_kernel(local_ref, grads_ref, weight_ref, terms_ref, forward_ref, first_ref, second_ref):
    rows_out, pairs, cout = grads_ref.shape
    cin = weight_ref.shape[3]
    grads = with_next_pair(grads_ref[...].reshape(rows_out * pairs, cout), pairs)
    for depth_tap in (1, 2):
        plane = local_ref[depth_tap - 1]
        store_kernel_terms(terms_ref, depth_tap - 1, plane, grads, rows_out, pairs, cin, cout)
    forward_ref[...] = forward_terms(local_ref[0], weight_ref, 1, rows_out, pairs) + forward_terms(
        local_ref[1], weight_ref, 2, rows_out, pairs
    )
    even, odd = backward_terms(grads, weight_ref, 1, pairs)
    for b in range(rows_out):
        first_ref[2 * b] = even[b * pairs : (b + 1) * pairs].astype(jnp.bfloat16)
        first_ref[2 * b + 1] = odd[b * pairs : (b + 1) * pairs].astype(jnp.bfloat16)
    even, odd = backward_terms(grads, weight_ref, 2, pairs)
    second_ref[0] = even
    second_ref[1] = odd


def joined_kernel(local_ref, later_ref, terms_ref, chunks_ref, scratch_ref):
    rows_out, pairs, cout = later_ref.shape
    cin = local_ref.shape[3] // 2
    count, rows, _ = chunks_ref.shape
    total = 27 * cin
    step = total // count
    later = with_next_pair(later_ref[...].reshape(rows_out * pairs, cout), pairs)
    store_kernel_terms(scratch_ref, 0, local_ref[1], later, rows_out, pairs, cin, cout)
    scratch_ref[9 * cin : total] = terms_ref[...]
    scratch_ref[total:] = jnp.zeros((scratch_ref.shape[0] - total, cout), jnp.float32)
    for index in range(count):
        chunks_ref[index] = scratch_ref[index * step : index * step + rows].astype(chunks_ref.dtype)


def finish_kernel(
    rim_ref, later_ref, weight_ref, forward_ref, first_ref, second_ref, output_ref, grad_ref
):
    rows_out, pairs, cout = later_ref.shape
    later = with_next_pair(later_ref[...].reshape(rows_out * pairs, cout), pairs)
    total = forward_ref[...] + forward_terms(rim_ref[0], weight_ref, 0, rows_out, pairs)
    result = total[:, :cout] + from_previous_pair(total[:, cout:], pairs)
    output_ref[...] = result.astype(jnp.bfloat16).reshape(output_ref.shape)
    even, odd = backward_terms(later, weight_ref, 0, pairs)
    even = (even + second_ref[0]).astype(jnp.bfloat16)
    odd = (odd + second_ref[1]).astype(jnp.bfloat16)
    grad_ref[0] = first_ref[...]
    for b in range(rows_out):
        grad_ref[1, 2 * b] = even[b * pairs : (b + 1) * pairs]
        grad_ref[1, 2 * b + 1] = odd[b * pairs : (b + 1) * pairs]


def spread_kernel(step, factor, chunks_ref, grad_ref):
    for index in range(chunks_ref.shape[0]):
        block = chunks_ref[index].astype(jnp.float32)[:step]
        grad_ref[index * step : (index + 1) * step] = block * factor


def shards(volume, weight, cotangent):
    local = volume[0]
    grads = cotangent[0, 0]
    rows_out, pairs, cout = grads.shape
    cin = weight.shape[3]
    total = 27 * cin
    cells = rows_out * pairs
    count = math.prod(lax.axis_size(axis) for axis in PLANE)
    step = total // count
    rows = -(-step // 8) * 8
    devices = math.prod(lax.axis_size(axis) for axis in DP + SPACE)
    factor = 1.0 / math.sqrt(devices * cells)

    later = passed_along(grads, SPACE, -1)
    rim = passed_along(local[1:2], SPACE, 1)
    terms, forward, first, second = pl.pallas_call(
        own_kernel,
        out_shape=(
            jax.ShapeDtypeStruct((18 * cin, cout), jnp.float32),
            jax.ShapeDtypeStruct((cells, 2 * cout), jnp.float32),
            jax.ShapeDtypeStruct((2 * rows_out, pairs, 2 * cin), jnp.bfloat16),
            jax.ShapeDtypeStruct((2, cells, 2 * cin), jnp.float32),
        ),
        cost_estimate=pl.CostEstimate(flops=300_000_000, bytes_accessed=2_000_000, transcendentals=0),
        compiler_params=pltpu.CompilerParams(vmem_limit_bytes=VMEM_BYTES),
        name="own",
    )(local, grads, weight)
    chunks = pl.pallas_call(
        joined_kernel,
        out_shape=jax.ShapeDtypeStruct((count, rows, cout), jnp.bfloat16),
        scratch_shapes=[pltpu.VMEM((total + 8, cout), jnp.float32)],
        cost_estimate=pl.CostEstimate(flops=60_000_000, bytes_accessed=1_000_000, transcendentals=0),
        compiler_params=pltpu.CompilerParams(vmem_limit_bytes=VMEM_BYTES),
        name="joined",
    )(local, later, terms)

    piece = jnp.sum(exchange(chunks, PLANE).astype(jnp.float32), axis=0)
    for axis in ("zl", "zh"):
        copies = jnp.broadcast_to(piece[None], (lax.axis_size(axis), rows, cout))
        piece = jnp.sum(exchange(copies, (axis,)), axis=0)
    copies = jnp.broadcast_to(piece.astype(jnp.bfloat16)[None], (count, rows, cout))
    gathered = exchange(copies, PLANE)

    output, grad_volume = pl.pallas_call(
        finish_kernel,
        out_shape=(
            jax.ShapeDtypeStruct((rows_out, pairs, cout), jnp.bfloat16),
            jax.ShapeDtypeStruct((2, 2 * rows_out, pairs, 2 * cin), jnp.bfloat16),
        ),
        cost_estimate=pl.CostEstimate(flops=100_000_000, bytes_accessed=1_000_000, transcendentals=0),
        compiler_params=pltpu.CompilerParams(vmem_limit_bytes=VMEM_BYTES),
        name="finish",
    )(rim, later, weight, forward, first, second)
    grad_weight = pl.pallas_call(
        lambda chunks_ref, grad_ref: spread_kernel(step, factor, chunks_ref, grad_ref),
        out_shape=jax.ShapeDtypeStruct((total, cout), jnp.float32),
        compiler_params=pltpu.CompilerParams(vmem_limit_bytes=VMEM_BYTES),
        name="spread_out",
    )(gathered)
    return (output[None, None], grad_volume[None], grad_weight.reshape(weight.shape))


def solution(mesh):
    fine = jax.sharding.Mesh(mesh.devices.reshape(SIZES), DP + SPACE)
    split = P(DP, SPACE, None, None, None)
    return jax.shard_map(
        shards,
        mesh=fine,
        in_specs=(split, P(), split),
        out_specs=(split, split, P()),
        check_vma=False,
    )
```

time: 941 us -> 127 us (0.13)
  the two profiles are of different devices: /device:TPU:1 before, /device:TPU:8 now
where the time goes in v1:
time: 127 us; the launch traced here: 126 us
  blocking collectives  87.2 us (69%)
  starting transfers between devices  19.9 us (16%)
  waiting for transfers between devices  11.7 us (9%)
  local copies, waits for them, and re-layouts  3.67 us (3%)
  Pallas kernels  3.01 us (2%)
    all_to_all x3, blocking collectives, exchange(): return lax.all_to_all(value, axes, 0, 0, tiled=True)  87.2 us
    ppermute x2, starting transfers between devices, passed_along(): lax.ppermute(value, axes, [(source, source + steps) for source in range(f...  14.5 us
    ppermute x2, waiting for transfers between devices, passed_along(): lax.ppermute(value, axes, [(source, source + steps) for source in range(f...  11.7 us
    all_to_all x1, starting transfers between devices, exchange(): return lax.all_to_all(value, axes, 0, 0, tiled=True)  5.32 us
    unnamed x10, local copies, waits for them, and re-layouts  2.8 us
  transfers between devices with their start and end apart: 3, of which 1 were waited for; matrix products, arithmetic and copies ran while one was open for 0% of the time, Pallas kernels for 1%

profile of v1, /device:TPU:8, one launch (start us, length us, event | category | flops | bytes accessed | tf_op | source)
XLA Modules:
  0.0 126.3 jit_solution(16313900588375949120)
XLA Ops:
  0.6 12.5 %collective-permute-start.1 = (bf16[4,64,128]{2,1,0:T(8,128)(2,1)}, bf16[4,64,128]{2,1,0:T(8,128)(2,1)S(1)}, u32[]{:S(2)}, u32[]{:S(2)}) collective-permute-start(bf16[4,64,128]{2,1,0:T(8,128)(2,1)} %bitcast.9), channel_id=1, source_target_pairs={{1,0},{2,1},{3,2},{4,3},{5,4},{6,5},{7,6},{8,7},{9,8},{10,9},{11,1... | collective-permute-start | bytes 196616 | tf_op jit(solution)/shard_map/ppermute | solution.py:20
  13.1 0.0 copy-start
  13.1 0.9 copy-done
  14.1 0.0 copy-start.2
  14.1 1.0 copy-done.2
  15.1 0.0 copy-start.4
  15.1 0.8 copy-done.4
  15.9 0.7 own.1
  16.6 0.0 collective-permute-done.1.later_ref
  16.7 0.3 joined.1
  16.9 16.9 %all_to_all.20 = bf16[32,56,128]{2,1,0:T(8,128)(2,1)S(1)} all-to-all(bf16[32,56,128]{2,1,0:T(8,128)(2,1)S(1)} %joined.1), channel_id=1, replica_groups=mesh['x'=4,'zh'=4,'y'=4,'zl'=8,'c'=2] {'x','y','c'}, dimensions={0} | all-to-all | bytes 917504 | tf_op jit(solution)/shard_map/all_to_all | solution.py:24
  33.9 0.1 convert_reduce_fusion
  34.0 24.3 %all_to_all.21 = f32[8,56,128]{2,1,0:T(8,128)S(1)} all-to-all(f32[8,56,128]{2,1,0:T(8,128)S(1)} %broadcast_in_dim.12), channel_id=1, replica_groups=mesh['x'=4,'zh'=4,'y'=4,'zl'=8,'c'=2] {'zl'}, dimensions={0} | all-to-all | bytes 458752 | tf_op jit(solution)/shard_map/all_to_all | solution.py:24
  58.3 46.0 %all_to_all.22 = f32[4,56,128]{2,1,0:T(8,128)S(1)} all-to-all(f32[4,56,128]{2,1,0:T(8,128)S(1)} %broadcast_in_dim.13), channel_id=1, replica_groups=mesh['x'=4,'zh'=4,'y'=4,'zl'=8,'c'=2] {'zh'}, dimensions={0} | all-to-all | bytes 229376 | tf_op jit(solution)/shard_map/all_to_all | solution.py:24
  104.3 0.8 broadcast_in_dim.28
  105.1 0.0 copy-start.1
  105.1 0.0 copy-start.3
  105.1 5.3 %all-to-all-start.3 = ((bf16[32,56,128]{2,1,0:T(8,128)(2,1)}), bf16[32,56,128]{2,1,0:T(8,128)(2,1)S(1)}, u32[]{:S(2)}, u32[]{:S(2)}) async-start(bf16[32,56,128]{2,1,0:T(8,128)(2,1)} %broadcast_in_dim.28), calls=%async_computation.3 | async-start | bytes 917504 | tf_op jit(solution)/shard_map/all_to_all | solution.py:24
  110.4 0.0 copy-done.1
  110.5 2.1 %collective-permute-start = (bf16[1,8,64,128]{3,2,1,0:T(8,128)(2,1)S(1)}, bf16[1,8,64,128]{3,2,1,0:T(8,128)(2,1)S(1)}, u32[]{:S(2)}, u32[]{:S(2)}) collective-permute-start(bf16[1,8,64,128]{3,2,1,0:T(8,128)(2,1)S(1)} %slice_bitcast_fusion), channel_id=1, source_target_pairs={{0,1},{1,2},{2,3},{3,4},{4,5},{5,6},{6,7},{7,8},{8,9},{9,10},{10,1... | collective-permute-start | bytes 393224 | tf_op jit(solution)/shard_map/ppermute | solution.py:20
  112.5 11.7 %collective-permute-done.rim_ref = bf16[1,8,64,128]{3,2,1,0:T(8,128)(2,1)S(1)} collective-permute-done((bf16[1,8,64,128]{3,2,1,0:T(8,128)(2,1)S(1)}, bf16[1,8,64,128]{3,2,1,0:T(8,128)(2,1)S(1)}, u32[]{:S(2)}, u32[]{:S(2)}) %collective-permute-start) | collective-permute-done | bytes 131104 | tf_op jit(solution)/shard_map/ppermute | solution.py:20
  124.2 0.0 copy-done.3
  124.2 1.1 finish.1
  125.3 0.0 all-to-all-done.3.chunks_ref
  125.3 1.0 spread_out.1
  (5 shorter events, 0.1 us)
Async XLA Ops:
  0.6 16.0 %collective-permute-start.1 = (bf16[4,64,128]{2,1,0:T(8,128)(2,1)}, bf16[4,64,128]{2,1,0:T(8,128)(2,1)S(1)}, u32[]{:S(2)}, u32[]{:S(2)}) collective-permute-start(bf16[4,64,128]{2,1,0:T(8,128)(2,1)} %bitcast.9), channel_id=1, source_target_pairs={{1,0},{2,1},{3,2},{4,3},{5,4},{6,5},{7,6},{8,7},{9,8},{10,9},{11,1... | collective-permute-start | bytes 196616 | tf_op jit(solution)/shard_map/ppermute | solution.py:20
  13.1 1.0 copy-start
  14.1 1.0 copy-start.2
  15.1 0.8 copy-start.4
  105.1 5.3 %copy-start.1 = (bf16[1,2,8,64,128]{4,3,2,1,0:T(8,128)(2,1)S(1)}, bf16[1,2,8,64,128]{4,3,2,1,0:T(8,128)(2,1)}, u32[]{:S(2)}) copy-start(bf16[1,2,8,64,128]{4,3,2,1,0:T(8,128)(2,1)} %param.3) | copy-start | bytes 786436
  105.1 19.2 %copy-start.3 = (bf16[3,3,3,64,128]{4,3,2,1,0:T(8,128)(2,1)S(1)}, bf16[3,3,3,64,128]{4,3,2,1,0:T(8,128)(2,1)}, u32[]{:S(2)}) copy-start(bf16[3,3,3,64,128]{4,3,2,1,0:T(8,128)(2,1)} %weight_ref.3) | copy-start | bytes 1327108
  105.1 20.2 %all-to-all-start.3 = ((bf16[32,56,128]{2,1,0:T(8,128)(2,1)}), bf16[32,56,128]{2,1,0:T(8,128)(2,1)S(1)}, u32[]{:S(2)}, u32[]{:S(2)}) async-start(bf16[32,56,128]{2,1,0:T(8,128)(2,1)} %broadcast_in_dim.28), calls=%async_computation.3 | async-start | bytes 917504 | tf_op jit(solution)/shard_map/all_to_all | solution.py:24
  110.5 13.8 %collective-permute-start = (bf16[1,8,64,128]{3,2,1,0:T(8,128)(2,1)S(1)}, bf16[1,8,64,128]{3,2,1,0:T(8,128)(2,1)S(1)}, u32[]{:S(2)}, u32[]{:S(2)}) collective-permute-start(bf16[1,8,64,128]{3,2,1,0:T(8,128)(2,1)S(1)} %slice_bitcast_fusion), channel_id=1, source_target_pairs={{0,1},{1,2},{2,3},{3,4},{4,5},{5,6},{6,7},{7,8},{8,9},{9,10},{10,1... | collective-permute-start | bytes 393224 | tf_op jit(solution)/shard_map/ppermute | solution.py:20

commit v2 on v1

--- a/solution.py
+++ b/solution.py
@@ -8,9 +8,9 @@
 from jax.sharding import PartitionSpec as P
 
 DP = ("x", "zh")
-SPACE = ("y", "zl", "c")
-PLANE = ("x", "y", "c")
-SIZES = (4, 4, 4, 8, 2)
+SPACE = ("y", "zn", "ze", "c")
+SLAB = ("x", "y", "ze", "c")
+SIZES = (4, 4, 4, 4, 2, 2)
 VMEM_BYTES = 16 << 20
 
 
@@ -22,6 +22,11 @@
 
 def exchange(value, axes):
     return lax.all_to_all(value, axes, 0, 0, tiled=True)
+
+
+def summed_over(piece, axis):
+    copies = jnp.broadcast_to(piece[None], (lax.axis_size(axis), *piece.shape))
+    return jnp.sum(exchange(copies, (axis,)), axis=0)
 
 
 def with_next_pair(cells, pairs):
@@ -165,14 +170,13 @@
     cin = weight.shape[3]
     total = 27 * cin
     cells = rows_out * pairs
-    count = math.prod(lax.axis_size(axis) for axis in PLANE)
+    count = math.prod(lax.axis_size(axis) for axis in SLAB)
     step = total // count
     rows = -(-step // 8) * 8
     devices = math.prod(lax.axis_size(axis) for axis in DP + SPACE)
     factor = 1.0 / math.sqrt(devices * cells)
 
     later = passed_along(grads, SPACE, -1)
-    rim = passed_along(local[1:2], SPACE, 1)
     terms, forward, first, second = pl.pallas_call(
         own_kernel,
         out_shape=(
@@ -194,12 +198,11 @@
         name="joined",
     )(local, later, terms)
 
-    piece = jnp.sum(exchange(chunks, PLANE).astype(jnp.float32), axis=0)
-    for axis in ("zl", "zh"):
-        copies = jnp.broadcast_to(piece[None], (lax.axis_size(axis), rows, cout))
-        piece = jnp.sum(exchange(copies, (axis,)), axis=0)
-    copies = jnp.broadcast_to(piece.astype(jnp.bfloat16)[None], (count, rows, cout))
-    gathered = exchange(copies, PLANE)
+    piece = jnp.sum(exchange(chunks, SLAB).astype(jnp.float32), axis=0)
+    piece = summed_over(piece, "zn")
+    piece, plane = lax.optimization_barrier((piece, local[1:2]))
+    rim = passed_along(plane, SPACE, 1)
+    piece = summed_over(piece, "zh")
 
     output, grad_volume = pl.pallas_call(
         finish_kernel,
@@ -211,6 +214,9 @@
         compiler_params=pltpu.CompilerParams(vmem_limit_bytes=VMEM_BYTES),
         name="finish",
     )(rim, later, weight, forward, first, second)
+    piece, output, grad_volume = lax.optimization_barrier((piece, output, grad_volume))
+    copies = jnp.broadcast_to(piece.astype(jnp.bfloat16)[None], (count, rows, cout))
+    gathered = exchange(copies, SLAB)
     grad_weight = pl.pallas_call(
         lambda chunks_ref, grad_ref: spread_kernel(step, factor, chunks_ref, grad_ref),
         out_shape=jax.ShapeDtypeStruct((total, cout), jnp.float32),

time: 127 us -> 122 us (0.961)
  the two profiles are of different devices: /device:TPU:8 before, /device:TPU:1 now
where the time goes in v2:
time: 122 us
  starting transfers between devices  49.4 us (40%)
  blocking collectives  39.3 us (32%)
  waiting for transfers between devices  24.9 us (20%)
  local copies, waits for them, and re-layouts  4.15 us (3%)
  Pallas kernels  3.02 us (2%)
    all_to_all x2, blocking collectives, exchange(): return lax.all_to_all(value, axes, 0, 0, tiled=True)  39.3 us
    all_to_all x2, starting transfers between devices, exchange(): return lax.all_to_all(value, axes, 0, 0, tiled=True)  29.4 us
    all_to_all x2, waiting for transfers between devices, exchange(): return lax.all_to_all(value, axes, 0, 0, tiled=True)  22.2 us
    ppermute x2, starting transfers between devices, passed_along(): lax.ppermute(value, axes, [(source, source + steps) for source in range(f...  20 us
    unnamed x10, local copies, waits for them, and re-layouts  2.8 us
    ppermute x2, waiting for transfers between devices, passed_along(): lax.ppermute(value, axes, [(source, source + steps) for source in range(f...  2.77 us
  transfers between devices with their start and end apart: 4, of which 3 were waited for; matrix products, arithmetic and copies ran while one was open for 0% of the time, Pallas kernels for 1%

profile of v2, /device:TPU:1, one launch (start us, length us, event | category | flops | bytes accessed | tf_op | source)
XLA Modules:
  0.0 121.6 jit_solution(18301934780483658808)
XLA Ops:
  0.6 16.1 %collective-permute-start = (bf16[4,64,128]{2,1,0:T(8,128)(2,1)}, bf16[4,64,128]{2,1,0:T(8,128)(2,1)S(1)}, u32[]{:S(2)}, u32[]{:S(2)}) collective-permute-start(bf16[4,64,128]{2,1,0:T(8,128)(2,1)} %bitcast.9), channel_id=1, source_target_pairs={{1,0},{2,1},{3,2},{4,3},{5,4},{6,5},{7,6},{8,7},{9,8},{10,9},{11,1... | collective-permute-start | bytes 196616 | tf_op jit(solution)/shard_map/ppermute | solution.py:20
  16.7 0.0 copy-start
  16.7 0.9 copy-done
  17.7 0.0 copy-start.2
  17.7 1.0 copy-done.2
  18.7 0.0 copy-start.4
  18.7 0.8 copy-done.4
  19.5 0.7 own.1
  20.2 0.0 collective-permute-done.later_ref
  20.2 0.3 joined.1
  20.5 18.1 %all_to_all.20 = bf16[64,32,128]{2,1,0:T(8,128)(2,1)S(1)} all-to-all(bf16[64,32,128]{2,1,0:T(8,128)(2,1)S(1)} %joined.1), channel_id=1, replica_groups=mesh['x'=4,'zh'=4,'y'=4,'zn'=4,'ze'=2,'c'=2] {'x','y','ze','c'}, dimensions={0} | all-to-all | bytes 1048576 | tf_op jit(solution)/shard_map/all_to_all | solution.py:24
  38.6 0.0 copy-start.1
  38.6 0.1 convert_reduce_fusion
  38.7 0.0 copy-start.3
  38.7 0.6 broadcast_in_dim.10
  39.4 8.8 %all-to-all-start.1 = ((f32[4,32,128]{2,1,0:T(8,128)}), f32[4,32,128]{2,1,0:T(8,128)S(1)}, u32[]{:S(2)}, u32[]{:S(2)}) async-start(f32[4,32,128]{2,1,0:T(8,128)} %broadcast_in_dim.10), calls=%async_computation.1 | async-start | bytes 131072 | tf_op jit(solution)/shard_map/all_to_all | solution.py:24
  48.2 0.0 copy-done.1
  48.2 8.5 %all-to-all-done.1 = f32[4,32,128]{2,1,0:T(8,128)S(1)} async-done(((f32[4,32,128]{2,1,0:T(8,128)}), f32[4,32,128]{2,1,0:T(8,128)S(1)}, u32[]{:S(2)}, u32[]{:S(2)}) %all-to-all-start.1) | async-done | bytes 65568 | tf_op jit(solution)/shard_map/all_to_all | solution.py:24
  56.7 0.6 broadcast_in_dim.11
  57.3 20.6 %all-to-all-start.2 = ((f32[4,32,128]{2,1,0:T(8,128)}), f32[4,32,128]{2,1,0:T(8,128)S(1)}, u32[]{:S(2)}, u32[]{:S(2)}) async-start(f32[4,32,128]{2,1,0:T(8,128)} %broadcast_in_dim.11), calls=%async_computation.2 | async-start | bytes 131072 | tf_op jit(solution)/shard_map/all_to_all | solution.py:24
  77.9 3.9 %collective-permute-start.1 = (bf16[1,8,64,128]{3,2,1,0:T(8,128)(2,1)S(1)}, bf16[1,8,64,128]{3,2,1,0:T(8,128)(2,1)S(1)}, u32[]{:S(2)}, u32[]{:S(2)}) collective-permute-start(bf16[1,8,64,128]{3,2,1,0:T(8,128)(2,1)S(1)} %slice_bitcast_fusion), channel_id=1, source_target_pairs={{0,1},{1,2},{2,3},{3,4},{4,5},{5,6},{6,7},{7,8},{8,9},{9,10},{10,1... | collective-permute-start | bytes 393224 | tf_op jit(solution)/shard_map/ppermute | solution.py:20
  81.8 2.8 %collective-permute-done.1.rim_ref = bf16[1,8,64,128]{3,2,1,0:T(8,128)(2,1)S(1)} collective-permute-done((bf16[1,8,64,128]{3,2,1,0:T(8,128)(2,1)S(1)}, bf16[1,8,64,128]{3,2,1,0:T(8,128)(2,1)S(1)}, u32[]{:S(2)}, u32[]{:S(2)}) %collective-permute-start.1) | collective-permute-done | bytes 131104 | tf_op jit(solution)/shard_map/ppermute | solution.py:20
  84.6 0.0 copy-done.3
  84.6 1.1 finish.1
  85.7 13.7 %all-to-all-done.2 = f32[4,32,128]{2,1,0:T(8,128)S(1)} async-done(((f32[4,32,128]{2,1,0:T(8,128)}), f32[4,32,128]{2,1,0:T(8,128)S(1)}, u32[]{:S(2)}, u32[]{:S(2)}) %all-to-all-start.2) | async-done | bytes 65568 | tf_op jit(solution)/shard_map/all_to_all | solution.py:24
  99.4 0.1 broadcast_in_dim.28
  99.5 21.1 %all_to_all.21.chunks_ref = bf16[64,32,128]{2,1,0:T(8,128)(2,1)S(1)} all-to-all(bf16[64,32,128]{2,1,0:T(8,128)(2,1)S(1)} %broadcast_in_dim.28), channel_id=1, replica_groups=mesh['x'=4,'zh'=4,'y'=4,'zn'=4,'ze'=2,'c'=2] {'x','y','ze','c'}, dimensions={0} | all-to-all | bytes 1048576 | tf_op jit(solution)/shard_map/all_to_all | solution.py:24
  120.6 1.0 spread_out.1
  (3 shorter events, 0.0 us)
Async XLA Ops:
  0.6 19.6 %collective-permute-start = (bf16[4,64,128]{2,1,0:T(8,128)(2,1)}, bf16[4,64,128]{2,1,0:T(8,128)(2,1)S(1)}, u32[]{:S(2)}, u32[]{:S(2)}) collective-permute-start(bf16[4,64,128]{2,1,0:T(8,128)(2,1)} %bitcast.9), channel_id=1, source_target_pairs={{1,0},{2,1},{3,2},{4,3},{5,4},{6,5},{7,6},{8,7},{9,8},{10,9},{11,1... | collective-permute-start | bytes 196616 | tf_op jit(solution)/shard_map/ppermute | solution.py:20
  16.7 1.0 copy-start
  17.7 1.0 copy-start.2
  18.7 0.8 copy-start.4
  38.6 9.6 %copy-start.1 = (bf16[1,2,8,64,128]{4,3,2,1,0:T(8,128)(2,1)S(1)}, bf16[1,2,8,64,128]{4,3,2,1,0:T(8,128)(2,1)}, u32[]{:S(2)}) copy-start(bf16[1,2,8,64,128]{4,3,2,1,0:T(8,128)(2,1)} %param.3) | copy-start | bytes 786436
  38.7 45.9 %copy-start.3 = (bf16[3,3,3,64,128]{4,3,2,1,0:T(8,128)(2,1)S(1)}, bf16[3,3,3,64,128]{4,3,2,1,0:T(8,128)(2,1)}, u32[]{:S(2)}) copy-start(bf16[3,3,3,64,128]{4,3,2,1,0:T(8,128)(2,1)} %weight_ref.3) | copy-start | bytes 1327108
  39.4 17.3 %all-to-all-start.1 = ((f32[4,32,128]{2,1,0:T(8,128)}), f32[4,32,128]{2,1,0:T(8,128)S(1)}, u32[]{:S(2)}, u32[]{:S(2)}) async-start(f32[4,32,128]{2,1,0:T(8,128)} %broadcast_in_dim.10), calls=%async_computation.1 | async-start | bytes 131072 | tf_op jit(solution)/shard_map/all_to_all | solution.py:24
  57.3 42.0 %all-to-all-start.2 = ((f32[4,32,128]{2,1,0:T(8,128)}), f32[4,32,128]{2,1,0:T(8,128)S(1)}, u32[]{:S(2)}, u32[]{:S(2)}) async-start(f32[4,32,128]{2,1,0:T(8,128)} %broadcast_in_dim.11), calls=%async_computation.2 | async-start | bytes 131072 | tf_op jit(solution)/shard_map/all_to_all | solution.py:24
  77.9 6.7 %collective-permute-start.1 = (bf16[1,8,64,128]{3,2,1,0:T(8,128)(2,1)S(1)}, bf16[1,8,64,128]{3,2,1,0:T(8,128)(2,1)S(1)}, u32[]{:S(2)}, u32[]{:S(2)}) collective-permute-start(bf16[1,8,64,128]{3,2,1,0:T(8,128)(2,1)S(1)} %slice_bitcast_fusion), channel_id=1, source_target_pairs={{0,1},{1,2},{2,3},{3,4},{4,5},{5,6},{6,7},{7,8},{8,9},{9,10},{10,1... | collective-permute-start | bytes 393224 | tf_op jit(solution)/shard_map/ppermute | solution.py:20

commit v3 on v2

--- a/solution.py
+++ b/solution.py
@@ -24,9 +24,10 @@
     return lax.all_to_all(value, axes, 0, 0, tiled=True)
 
 
-def summed_over(piece, axis):
-    copies = jnp.broadcast_to(piece[None], (lax.axis_size(axis), *piece.shape))
-    return jnp.sum(exchange(copies, (axis,)), axis=0)
+def swapped_sum(piece, axis, distance):
+    count = lax.axis_size(axis)
+    pairs = [(source, source ^ distance) for source in range(count)]
+    return piece + lax.ppermute(piece, axis, pairs)
 
 
 def with_next_pair(cells, pairs):
@@ -177,6 +178,7 @@
     factor = 1.0 / math.sqrt(devices * cells)
 
     later = passed_along(grads, SPACE, -1)
+    rim = passed_along(local[1:2], SPACE, 1)
     terms, forward, first, second = pl.pallas_call(
         own_kernel,
         out_shape=(
@@ -199,10 +201,11 @@
     )(local, later, terms)
 
     piece = jnp.sum(exchange(chunks, SLAB).astype(jnp.float32), axis=0)
-    piece = summed_over(piece, "zn")
-    piece, plane = lax.optimization_barrier((piece, local[1:2]))
-    rim = passed_along(plane, SPACE, 1)
-    piece = summed_over(piece, "zh")
+    for axis in ("zn", "zh"):
+        for bit in range(lax.axis_size(axis).bit_length() - 1):
+            piece = swapped_sum(piece, axis, 1 << bit)
+        if axis == "zn":
+            piece, rim = lax.optimization_barrier((piece, rim))
 
     output, grad_volume = pl.pallas_call(
         finish_kernel,
@@ -214,7 +217,6 @@
         compiler_params=pltpu.CompilerParams(vmem_limit_bytes=VMEM_BYTES),
         name="finish",
     )(rim, later, weight, forward, first, second)
-    piece, output, grad_volume = lax.optimization_barrier((piece, output, grad_volume))
     copies = jnp.broadcast_to(piece.astype(jnp.bfloat16)[None], (count, rows, cout))
     gathered = exchange(copies, SLAB)
     grad_weight = pl.pallas_call(

time: 122 us -> 118 us (0.967)
  blocking collectives: 39.3 us -> 0 us
  starting transfers between devices: 49.4 us -> 77.2 us
  waiting for transfers between devices: 24.9 us -> 31.7 us
    ppermute x0 -> x4, starting transfers between devices: none -> 42.3 us  [swapped_sum(): return piece + lax.ppermute(piece, axis, pairs)]
    all_to_all x2 -> x0, blocking collectives: 39.3 us -> none  [exchange(): return lax.all_to_all(value, axes, 0, 0, tiled=True)]
    all_to_all x2, starting transfers between devices: 29.4 us -> 15.3 us  [exchange(): return lax.all_to_all(value, axes, 0, 0, tiled=True)]
    ppermute x0 -> x4, waiting for transfers between devices: none -> 10.8 us  [swapped_sum(): return piece + lax.ppermute(piece, axis, pairs)]
    ppermute x2, waiting for transfers between devices: 2.77 us -> 0.01 us  [passed_along(): lax.ppermute(value, axes, [(source, source + steps) for source in range(f...]
    broadcast_in_dim x2 -> x0, local copies, waits for them, and re-layouts: 1.27 us -> none  [summed_over(): copies = jnp.broadcast_to(piece[None], (lax.axis_size(axis), *piece.shape))]
    all_to_all x2, waiting for transfers between devices: 22.2 us -> 20.9 us  [exchange(): return lax.all_to_all(value, axes, 0, 0, tiled=True)]
  transfers between devices with their start and end apart: 4 -> 8, of which waited for: 3 -> 6; matrix products, arithmetic and copies ran while one was open for 0% -> 0% of each run, Pallas kernels for 1% -> 2%
where the time goes in v3:
time: 118 us; the launch traced here: 117 us
  starting transfers between devices  77.2 us (65%)
  waiting for transfers between devices  31.7 us (27%)
  Pallas kernels  3.83 us (3%)
  local copies, waits for them, and re-layouts  3.68 us (3%)
    ppermute x4, starting transfers between devices, swapped_sum(): return piece + lax.ppermute(piece, axis, pairs)  42.3 us
    all_to_all x2, waiting for transfers between devices, exchange(): return lax.all_to_all(value, axes, 0, 0, tiled=True)  20.9 us
    ppermute x2, starting transfers between devices, passed_along(): lax.ppermute(value, axes, [(source, source + steps) for source in range(f...  19.6 us
    all_to_all x2, starting transfers between devices, exchange(): return lax.all_to_all(value, axes, 0, 0, tiled=True)  15.3 us
    ppermute x4, waiting for transfers between devices, swapped_sum(): return piece + lax.ppermute(piece, axis, pairs)  10.8 us
    unnamed x10, local copies, waits for them, and re-layouts  2.8 us
  transfers between devices with their start and end apart: 8, of which 6 were waited for; matrix products, arithmetic and copies ran while one was open for 0% of the time, Pallas kernels for 2%

profile of v3, /device:TPU:1, one launch (start us, length us, event | category | flops | bytes accessed | tf_op | source)
XLA Modules:
  0.0 117.3 jit_solution(16062268305098446594)
XLA Ops:
  0.6 16.1 %collective-permute-start = (bf16[4,64,128]{2,1,0:T(8,128)(2,1)}, bf16[4,64,128]{2,1,0:T(8,128)(2,1)S(1)}, u32[]{:S(2)}, u32[]{:S(2)}) collective-permute-start(bf16[4,64,128]{2,1,0:T(8,128)(2,1)} %bitcast.9), channel_id=1, source_target_pairs={{1,0},{2,1},{3,2},{4,3},{5,4},{6,5},{7,6},{8,7},{9,8},{10,9},{11,1... | collective-permute-start | bytes 196616 | tf_op jit(solution)/shard_map/ppermute | solution.py:20
  16.7 0.0 copy-start
  16.7 0.9 copy-done
  17.7 0.0 copy-start.2
  17.7 1.0 copy-done.2
  18.7 0.0 copy-start.4
  18.7 0.8 copy-done.4
  19.5 0.7 own.1
  20.2 0.0 collective-permute-done.later_ref
  20.2 1.1 joined.1
  21.3 0.0 copy-start.1
  21.3 5.7 %all-to-all-start = ((bf16[64,32,128]{2,1,0:T(8,128)(2,1)}), bf16[64,32,128]{2,1,0:T(8,128)(2,1)S(1)}, u32[]{:S(2)}, u32[]{:S(2)}) async-start(bf16[64,32,128]{2,1,0:T(8,128)(2,1)} %joined.1), calls=%async_computation | async-start | bytes 1048576 | tf_op jit(solution)/shard_map/all_to_all | solution.py:24
  27.0 0.0 copy-done.1
  27.0 3.5 %collective-permute-start.3 = (bf16[1,8,64,128]{3,2,1,0:T(8,128)(2,1)S(1)}, bf16[1,8,64,128]{3,2,1,0:T(8,128)(2,1)S(1)}, u32[]{:S(2)}, u32[]{:S(2)}) collective-permute-start(bf16[1,8,64,128]{3,2,1,0:T(8,128)(2,1)S(1)} %slice_bitcast_fusion), channel_id=1, source_target_pairs={{0,1},{1,2},{2,3},{3,4},{4,5},{5,6},{6,7},{7,8},{8,9},{9,10},{10,1... | collective-permute-start | bytes 393224 | tf_op jit(solution)/shard_map/ppermute | solution.py:20
  30.5 9.2 %all-to-all-done = bf16[64,32,128]{2,1,0:T(8,128)(2,1)S(1)} async-done(((bf16[64,32,128]{2,1,0:T(8,128)(2,1)}), bf16[64,32,128]{2,1,0:T(8,128)(2,1)S(1)}, u32[]{:S(2)}, u32[]{:S(2)}) %all-to-all-start) | async-done | bytes 524320 | tf_op jit(solution)/shard_map/all_to_all | solution.py:24
  39.8 0.1 convert_reduce_fusion
  39.9 1.9 %collective-permute-start.1 = (f32[32,128]{1,0:T(8,128)S(1)}, f32[32,128]{1,0:T(8,128)S(1)}, u32[]{:S(2)}, u32[]{:S(2)}) collective-permute-start(f32[32,128]{1,0:T(8,128)S(1)} %convert_reduce_fusion), channel_id=1, source_target_pairs={{0,4},{4,0},{8,12},{12,8},{1,5},{5,1},{9,13},{13,9},{2,6},{6,2},{1... | collective-permute-start | bytes 49160 | tf_op jit(solution)/shard_map/ppermute | solution.py:30
  41.8 3.5 %collective-permute-done.1 = f32[32,128]{1,0:T(8,128)S(1)} collective-permute-done((f32[32,128]{1,0:T(8,128)S(1)}, f32[32,128]{1,0:T(8,128)S(1)}, u32[]{:S(2)}, u32[]{:S(2)}) %collective-permute-start.1) | collective-permute-done | bytes 16416 | tf_op jit(solution)/shard_map/ppermute | solution.py:30
  45.2 7.1 %collective-permute-start.2 = (f32[32,128]{1,0:T(8,128)S(1)}, f32[32,128]{1,0:T(8,128)S(1)}, u32[]{:S(2)}, u32[]{:S(2)}) collective-permute-start(f32[32,128]{1,0:T(8,128)S(1)} %add.12), channel_id=1, source_target_pairs={{0,8},{4,12},{8,0},{12,4},{1,9},{5,13},{9,1},{13,5},{2,10},{6,14},... | collective-permute-start | bytes 49160 | tf_op jit(solution)/shard_map/ppermute | solution.py:30
  52.4 1.2 %collective-permute-done.2 = f32[32,128]{1,0:T(8,128)S(1)} collective-permute-done((f32[32,128]{1,0:T(8,128)S(1)}, f32[32,128]{1,0:T(8,128)S(1)}, u32[]{:S(2)}, u32[]{:S(2)}) %collective-permute-start.2) | collective-permute-done | bytes 16416 | tf_op jit(solution)/shard_map/ppermute | solution.py:30
  53.6 0.0 collective-permute-done.3.rim_ref
  53.6 15.4 %collective-permute-start.4 = (f32[32,128]{1,0:T(8,128)S(1)}, f32[32,128]{1,0:T(8,128)S(1)}, u32[]{:S(2)}, u32[]{:S(2)}) collective-permute-start(f32[32,128]{1,0:T(8,128)S(1)} %add.13), channel_id=1, source_target_pairs={{0,64},{64,0},{128,192},{192,128},{1,65},{65,1},{129,193},{193,129... | collective-permute-start | bytes 49160 | tf_op jit(solution)/shard_map/ppermute | solution.py:30
  69.1 1.1 collective-permute-done.4
  70.2 17.8 %collective-permute-start.5 = (f32[32,128]{1,0:T(8,128)S(1)}, f32[32,128]{1,0:T(8,128)S(1)}, u32[]{:S(2)}, u32[]{:S(2)}) collective-permute-start(f32[32,128]{1,0:T(8,128)S(1)} %add.14), channel_id=1, source_target_pairs={{0,128},{64,192},{128,0},{192,64},{1,129},{65,193},{129,1},{193,65... | collective-permute-start | bytes 49160 | tf_op jit(solution)/shard_map/ppermute | solution.py:30
  88.0 5.0 %collective-permute-done.5 = f32[32,128]{1,0:T(8,128)S(1)} collective-permute-done((f32[32,128]{1,0:T(8,128)S(1)}, f32[32,128]{1,0:T(8,128)S(1)}, u32[]{:S(2)}, u32[]{:S(2)}) %collective-permute-start.5) | collective-permute-done | bytes 16416 | tf_op jit(solution)/shard_map/ppermute | solution.py:30
  93.0 0.9 broadcast_in_dim.14
  93.9 0.0 copy-start.3
  93.9 9.7 %all-to-all-start.1 = ((bf16[64,32,128]{2,1,0:T(8,128)(2,1)}), bf16[64,32,128]{2,1,0:T(8,128)(2,1)S(1)}, u32[]{:S(2)}, u32[]{:S(2)}) async-start(bf16[64,32,128]{2,1,0:T(8,128)(2,1)} %broadcast_in_dim.14), calls=%async_computation.1 | async-start | bytes 1048576 | tf_op jit(solution)/shard_map/all_to_all | solution.py:24
  103.5 0.0 copy-done.3
  103.6 1.1 finish.1
  104.6 11.7 %all-to-all-done.1.chunks_ref = bf16[64,32,128]{2,1,0:T(8,128)(2,1)S(1)} async-done(((bf16[64,32,128]{2,1,0:T(8,128)(2,1)}), bf16[64,32,128]{2,1,0:T(8,128)(2,1)S(1)}, u32[]{:S(2)}, u32[]{:S(2)}) %all-to-all-start.1) | async-done | bytes 524320 | tf_op jit(solution)/shard_map/all_to_all | solution.py:24
  116.3 1.0 spread_out.1
  (5 shorter events, 0.0 us)
Async XLA Ops:
  0.6 19.6 %collective-permute-start = (bf16[4,64,128]{2,1,0:T(8,128)(2,1)}, bf16[4,64,128]{2,1,0:T(8,128)(2,1)S(1)}, u32[]{:S(2)}, u32[]{:S(2)}) collective-permute-start(bf16[4,64,128]{2,1,0:T(8,128)(2,1)} %bitcast.9), channel_id=1, source_target_pairs={{1,0},{2,1},{3,2},{4,3},{5,4},{6,5},{7,6},{8,7},{9,8},{10,9},{11,1... | collective-permute-start | bytes 196616 | tf_op jit(solution)/shard_map/ppermute | solution.py:20
  16.7 1.0 copy-start
  17.7 1.0 copy-start.2
  18.7 0.8 copy-start.4
  21.3 5.7 %copy-start.1 = (bf16[1,2,8,64,128]{4,3,2,1,0:T(8,128)(2,1)S(1)}, bf16[1,2,8,64,128]{4,3,2,1,0:T(8,128)(2,1)}, u32[]{:S(2)}) copy-start(bf16[1,2,8,64,128]{4,3,2,1,0:T(8,128)(2,1)} %param.3) | copy-start | bytes 786436
  21.3 18.5 %all-to-all-start = ((bf16[64,32,128]{2,1,0:T(8,128)(2,1)}), bf16[64,32,128]{2,1,0:T(8,128)(2,1)S(1)}, u32[]{:S(2)}, u32[]{:S(2)}) async-start(bf16[64,32,128]{2,1,0:T(8,128)(2,1)} %joined.1), calls=%async_computation | async-start | bytes 1048576 | tf_op jit(solution)/shard_map/all_to_all | solution.py:24
  27.0 26.6 %collective-permute-start.3 = (bf16[1,8,64,128]{3,2,1,0:T(8,128)(2,1)S(1)}, bf16[1,8,64,128]{3,2,1,0:T(8,128)(2,1)S(1)}, u32[]{:S(2)}, u32[]{:S(2)}) collective-permute-start(bf16[1,8,64,128]{3,2,1,0:T(8,128)(2,1)S(1)} %slice_bitcast_fusion), channel_id=1, source_target_pairs={{0,1},{1,2},{2,3},{3,4},{4,5},{5,6},{6,7},{7,8},{8,9},{9,10},{10,1... | collective-permute-start | bytes 393224 | tf_op jit(solution)/shard_map/ppermute | solution.py:20
  39.9 5.4 %collective-permute-start.1 = (f32[32,128]{1,0:T(8,128)S(1)}, f32[32,128]{1,0:T(8,128)S(1)}, u32[]{:S(2)}, u32[]{:S(2)}) collective-permute-start(f32[32,128]{1,0:T(8,128)S(1)} %convert_reduce_fusion), channel_id=1, source_target_pairs={{0,4},{4,0},{8,12},{12,8},{1,5},{5,1},{9,13},{13,9},{2,6},{6,2},{1... | collective-permute-start | bytes 49160 | tf_op jit(solution)/shard_map/ppermute | solution.py:30
  45.2 8.4 %collective-permute-start.2 = (f32[32,128]{1,0:T(8,128)S(1)}, f32[32,128]{1,0:T(8,128)S(1)}, u32[]{:S(2)}, u32[]{:S(2)}) collective-permute-start(f32[32,128]{1,0:T(8,128)S(1)} %add.12), channel_id=1, source_target_pairs={{0,8},{4,12},{8,0},{12,4},{1,9},{5,13},{9,1},{13,5},{2,10},{6,14},... | collective-permute-start | bytes 49160 | tf_op jit(solution)/shard_map/ppermute | solution.py:30
  53.6 16.6 %collective-permute-start.4 = (f32[32,128]{1,0:T(8,128)S(1)}, f32[32,128]{1,0:T(8,128)S(1)}, u32[]{:S(2)}, u32[]{:S(2)}) collective-permute-start(f32[32,128]{1,0:T(8,128)S(1)} %add.13), channel_id=1, source_target_pairs={{0,64},{64,0},{128,192},{192,128},{1,65},{65,1},{129,193},{193,129... | collective-permute-start | bytes 49160 | tf_op jit(solution)/shard_map/ppermute | solution.py:30
  70.2 22.8 %collective-permute-start.5 = (f32[32,128]{1,0:T(8,128)S(1)}, f32[32,128]{1,0:T(8,128)S(1)}, u32[]{:S(2)}, u32[]{:S(2)}) collective-permute-start(f32[32,128]{1,0:T(8,128)S(1)} %add.14), channel_id=1, source_target_pairs={{0,128},{64,192},{128,0},{192,64},{1,129},{65,193},{129,1},{193,65... | collective-permute-start | bytes 49160 | tf_op jit(solution)/shard_map/ppermute | solution.py:30
  93.9 9.7 %copy-start.3 = (bf16[3,3,3,64,128]{4,3,2,1,0:T(8,128)(2,1)S(1)}, bf16[3,3,3,64,128]{4,3,2,1,0:T(8,128)(2,1)}, u32[]{:S(2)}) copy-start(bf16[3,3,3,64,128]{4,3,2,1,0:T(8,128)(2,1)} %weight_ref.3) | copy-start | bytes 1327108
  93.9 22.5 %all-to-all-start.1 = ((bf16[64,32,128]{2,1,0:T(8,128)(2,1)}), bf16[64,32,128]{2,1,0:T(8,128)(2,1)S(1)}, u32[]{:S(2)}, u32[]{:S(2)}) async-start(bf16[64,32,128]{2,1,0:T(8,128)(2,1)} %broadcast_in_dim.14), calls=%async_computation.1 | async-start | bytes 1048576 | tf_op jit(solution)/shard_map/all_to_all | solution.py:24

commit v4 on v2

--- a/solution.py
+++ b/solution.py
@@ -10,6 +10,7 @@
 DP = ("x", "zh")
 SPACE = ("y", "zn", "ze", "c")
 SLAB = ("x", "y", "ze", "c")
+LINE = ("zh", "zn")
 SIZES = (4, 4, 4, 4, 2, 2)
 VMEM_BYTES = 16 << 20
 
@@ -22,11 +23,6 @@
 
 def exchange(value, axes):
     return lax.all_to_all(value, axes, 0, 0, tiled=True)
-
-
-def summed_over(piece, axis):
-    copies = jnp.broadcast_to(piece[None], (lax.axis_size(axis), *piece.shape))
-    return jnp.sum(exchange(copies, (axis,)), axis=0)
 
 
 def with_next_pair(cells, pairs):
@@ -199,10 +195,11 @@
     )(local, later, terms)
 
     piece = jnp.sum(exchange(chunks, SLAB).astype(jnp.float32), axis=0)
-    piece = summed_over(piece, "zn")
     piece, plane = lax.optimization_barrier((piece, local[1:2]))
     rim = passed_along(plane, SPACE, 1)
-    piece = summed_over(piece, "zh")
+    lines = math.prod(lax.axis_size(axis) for axis in LINE)
+    copies = jnp.broadcast_to(piece[None], (lines, rows, cout))
+    piece = jnp.sum(exchange(copies, LINE), axis=0)
 
     output, grad_volume = pl.pallas_call(
         finish_kernel,

time: 122 us -> 121 us (level)
  waiting for transfers between devices: 24.9 us -> 47.1 us
  blocking collectives: 39.3 us -> 18.4 us
  starting transfers between devices: 49.4 us -> 46.4 us
    all_to_all x2 -> x1, blocking collectives: 39.3 us -> 18.4 us  [exchange(): return lax.all_to_all(value, axes, 0, 0, tiled=True)]
    ppermute x2, waiting for transfers between devices: 2.77 us -> 18.5 us  [passed_along(): lax.ppermute(value, axes, [(source, source + steps) for source in range(f...]
    all_to_all x2, waiting for transfers between devices: 22.2 us -> 28.6 us  [exchange(): return lax.all_to_all(value, axes, 0, 0, tiled=True)]
    all_to_all x2, starting transfers between devices: 29.4 us -> 27.9 us  [exchange(): return lax.all_to_all(value, axes, 0, 0, tiled=True)]
    ppermute x2, starting transfers between devices: 20 us -> 18.6 us  [passed_along(): lax.ppermute(value, axes, [(source, source + steps) for source in range(f...]
where the time goes in v4:
time: 121 us; the launch traced here: 120 us
  waiting for transfers between devices  47.1 us (39%)
  starting transfers between devices  46.4 us (38%)
  blocking collectives  18.4 us (15%)
  Pallas kernels  3.82 us (3%)
  local copies, waits for them, and re-layouts  3.61 us (3%)
    all_to_all x2, waiting for transfers between devices, exchange(): return lax.all_to_all(value, axes, 0, 0, tiled=True)  28.6 us
    all_to_all x2, starting transfers between devices, exchange(): return lax.all_to_all(value, axes, 0, 0, tiled=True)  27.9 us
    ppermute x2, starting transfers between devices, passed_along(): lax.ppermute(value, axes, [(source, source + steps) for source in range(f...  18.6 us
    ppermute x2, waiting for transfers between devices, passed_along(): lax.ppermute(value, axes, [(source, source + steps) for source in range(f...  18.5 us
    all_to_all x1, blocking collectives, exchange(): return lax.all_to_all(value, axes, 0, 0, tiled=True)  18.4 us
    unnamed x10, local copies, waits for them, and re-layouts  2.8 us
  transfers between devices with their start and end apart: 4, of which 3 were waited for; matrix products, arithmetic and copies ran while one was open for 0% of the time, Pallas kernels for 1%

profile of v4, /device:TPU:1, one launch (start us, length us, event | category | flops | bytes accessed | tf_op | source)
XLA Modules:
  0.0 120.2 jit_solution(3874688964501673000)
XLA Ops:
  0.6 16.1 %collective-permute-start = (bf16[4,64,128]{2,1,0:T(8,128)(2,1)}, bf16[4,64,128]{2,1,0:T(8,128)(2,1)S(1)}, u32[]{:S(2)}, u32[]{:S(2)}) collective-permute-start(bf16[4,64,128]{2,1,0:T(8,128)(2,1)} %bitcast.9), channel_id=1, source_target_pairs={{1,0},{2,1},{3,2},{4,3},{5,4},{6,5},{7,6},{8,7},{9,8},{10,9},{11,1... | collective-permute-start | bytes 196616 | tf_op jit(solution)/shard_map/ppermute | solution.py:21
  16.7 0.0 copy-start
  16.7 0.9 copy-done
  17.7 0.0 copy-start.2
  17.7 1.0 copy-done.2
  18.7 0.0 copy-start.4
  18.7 0.8 copy-done.4
  19.5 0.7 own.1
  20.2 0.0 collective-permute-done.later_ref
  20.2 1.1 joined.1
  21.3 0.0 copy-start.1
  21.3 5.7 %all-to-all-start = ((bf16[64,32,128]{2,1,0:T(8,128)(2,1)}), bf16[64,32,128]{2,1,0:T(8,128)(2,1)S(1)}, u32[]{:S(2)}, u32[]{:S(2)}) async-start(bf16[64,32,128]{2,1,0:T(8,128)(2,1)} %joined.1), calls=%async_computation | async-start | bytes 1048576 | tf_op jit(solution)/shard_map/all_to_all | solution.py:25
  27.0 0.0 copy-done.1
  27.0 12.8 %all-to-all-done = bf16[64,32,128]{2,1,0:T(8,128)(2,1)S(1)} async-done(((bf16[64,32,128]{2,1,0:T(8,128)(2,1)}), bf16[64,32,128]{2,1,0:T(8,128)(2,1)S(1)}, u32[]{:S(2)}, u32[]{:S(2)}) %all-to-all-start) | async-done | bytes 524320 | tf_op jit(solution)/shard_map/all_to_all | solution.py:25
  39.8 0.1 convert_reduce_fusion
  39.9 0.0 copy-start.3
  39.9 0.7 broadcast_in_dim.8
  40.6 22.2 %all-to-all-start.1 = ((f32[16,32,128]{2,1,0:T(8,128)}), f32[16,32,128]{2,1,0:T(8,128)S(1)}, u32[]{:S(2)}, u32[]{:S(2)}) async-start(f32[16,32,128]{2,1,0:T(8,128)} %broadcast_in_dim.8), calls=%async_computation.1 | async-start | bytes 524288 | tf_op jit(solution)/shard_map/all_to_all | solution.py:25
  62.8 2.5 %collective-permute-start.1 = (bf16[1,8,64,128]{3,2,1,0:T(8,128)(2,1)S(1)}, bf16[1,8,64,128]{3,2,1,0:T(8,128)(2,1)S(1)}, u32[]{:S(2)}, u32[]{:S(2)}) collective-permute-start(bf16[1,8,64,128]{3,2,1,0:T(8,128)(2,1)S(1)} %slice_bitcast_fusion), channel_id=1, source_target_pairs={{0,1},{1,2},{2,3},{3,4},{4,5},{5,6},{6,7},{7,8},{8,9},{9,10},{10,1... | collective-permute-start | bytes 393224 | tf_op jit(solution)/shard_map/ppermute | solution.py:21
  65.3 18.5 %collective-permute-done.1.rim_ref = bf16[1,8,64,128]{3,2,1,0:T(8,128)(2,1)S(1)} collective-permute-done((bf16[1,8,64,128]{3,2,1,0:T(8,128)(2,1)S(1)}, bf16[1,8,64,128]{3,2,1,0:T(8,128)(2,1)S(1)}, u32[]{:S(2)}, u32[]{:S(2)}) %collective-permute-start.1) | collective-permute-done | bytes 131104 | tf_op jit(solution)/shard_map/ppermute | solution.py:21
  83.8 0.0 copy-done.3
  83.8 1.1 finish.1
  84.9 15.8 %all-to-all-done.1 = f32[16,32,128]{2,1,0:T(8,128)S(1)} async-done(((f32[16,32,128]{2,1,0:T(8,128)}), f32[16,32,128]{2,1,0:T(8,128)S(1)}, u32[]{:S(2)}, u32[]{:S(2)}) %all-to-all-start.1) | async-done | bytes 262176 | tf_op jit(solution)/shard_map/all_to_all | solution.py:25
  100.8 0.1 broadcast_in_dim.21
  100.8 18.4 %all_to_all.15.chunks_ref = bf16[64,32,128]{2,1,0:T(8,128)(2,1)S(1)} all-to-all(bf16[64,32,128]{2,1,0:T(8,128)(2,1)S(1)} %broadcast_in_dim.21), channel_id=1, replica_groups=mesh['x'=4,'zh'=4,'y'=4,'zn'=4,'ze'=2,'c'=2] {'x','y','ze','c'}, dimensions={0} | all-to-all | bytes 1048576 | tf_op jit(solution)/shard_map/all_to_all | solution.py:25
  119.2 1.0 spread_out.1
  (2 shorter events, 0.0 us)
Async XLA Ops:
  0.6 19.6 %collective-permute-start = (bf16[4,64,128]{2,1,0:T(8,128)(2,1)}, bf16[4,64,128]{2,1,0:T(8,128)(2,1)S(1)}, u32[]{:S(2)}, u32[]{:S(2)}) collective-permute-start(bf16[4,64,128]{2,1,0:T(8,128)(2,1)} %bitcast.9), channel_id=1, source_target_pairs={{1,0},{2,1},{3,2},{4,3},{5,4},{6,5},{7,6},{8,7},{9,8},{10,9},{11,1... | collective-permute-start | bytes 196616 | tf_op jit(solution)/shard_map/ppermute | solution.py:21
  16.7 1.0 copy-start
  17.7 1.0 copy-start.2
  18.7 0.8 copy-start.4
  21.3 5.7 %copy-start.1 = (bf16[1,2,8,64,128]{4,3,2,1,0:T(8,128)(2,1)S(1)}, bf16[1,2,8,64,128]{4,3,2,1,0:T(8,128)(2,1)}, u32[]{:S(2)}) copy-start(bf16[1,2,8,64,128]{4,3,2,1,0:T(8,128)(2,1)} %param.3) | copy-start | bytes 786436
  21.3 18.5 %all-to-all-start = ((bf16[64,32,128]{2,1,0:T(8,128)(2,1)}), bf16[64,32,128]{2,1,0:T(8,128)(2,1)S(1)}, u32[]{:S(2)}, u32[]{:S(2)}) async-start(bf16[64,32,128]{2,1,0:T(8,128)(2,1)} %joined.1), calls=%async_computation | async-start | bytes 1048576 | tf_op jit(solution)/shard_map/all_to_all | solution.py:25
  39.9 44.0 %copy-start.3 = (bf16[3,3,3,64,128]{4,3,2,1,0:T(8,128)(2,1)S(1)}, bf16[3,3,3,64,128]{4,3,2,1,0:T(8,128)(2,1)}, u32[]{:S(2)}) copy-start(bf16[3,3,3,64,128]{4,3,2,1,0:T(8,128)(2,1)} %weight_ref.3) | copy-start | bytes 1327108
  40.6 60.1 %all-to-all-start.1 = ((f32[16,32,128]{2,1,0:T(8,128)}), f32[16,32,128]{2,1,0:T(8,128)S(1)}, u32[]{:S(2)}, u32[]{:S(2)}) async-start(f32[16,32,128]{2,1,0:T(8,128)} %broadcast_in_dim.8), calls=%async_computation.1 | async-start | bytes 524288 | tf_op jit(solution)/shard_map/all_to_all | solution.py:25
  62.8 21.0 %collective-permute-start.1 = (bf16[1,8,64,128]{3,2,1,0:T(8,128)(2,1)S(1)}, bf16[1,8,64,128]{3,2,1,0:T(8,128)(2,1)S(1)}, u32[]{:S(2)}, u32[]{:S(2)}) collective-permute-start(bf16[1,8,64,128]{3,2,1,0:T(8,128)(2,1)S(1)} %slice_bitcast_fusion), channel_id=1, source_target_pairs={{0,1},{1,2},{2,3},{3,4},{4,5},{5,6},{6,7},{7,8},{8,9},{9,10},{10,1... | collective-permute-start | bytes 393224 | tf_op jit(solution)/shard_map/ppermute | solution.py:21

commit v5 on v4

--- a/solution.py
+++ b/solution.py
@@ -173,6 +173,7 @@
     factor = 1.0 / math.sqrt(devices * cells)
 
     later = passed_along(grads, SPACE, -1)
+    rim = passed_along(local[1:2], SPACE, 1)
     terms, forward, first, second = pl.pallas_call(
         own_kernel,
         out_shape=(
@@ -195,11 +196,10 @@
     )(local, later, terms)
 
     piece = jnp.sum(exchange(chunks, SLAB).astype(jnp.float32), axis=0)
-    piece, plane = lax.optimization_barrier((piece, local[1:2]))
-    rim = passed_along(plane, SPACE, 1)
+    piece, rim = lax.optimization_barrier((piece, rim))
     lines = math.prod(lax.axis_size(axis) for axis in LINE)
-    copies = jnp.broadcast_to(piece[None], (lines, rows, cout))
-    piece = jnp.sum(exchange(copies, LINE), axis=0)
+    copies = jnp.broadcast_to(piece.astype(jnp.bfloat16)[None], (lines, rows, cout))
+    piece = jnp.sum(exchange(copies, LINE).astype(jnp.float32), axis=0)
 
     output, grad_volume = pl.pallas_call(
         finish_kernel,

time: 121 us -> 111 us (0.917)
  waiting for transfers between devices: 47.1 us -> 31.7 us
  blocking collectives: 18.4 us -> 23.2 us
    ppermute x2, waiting for transfers between devices: 18.5 us -> 0.01 us  [passed_along(): lax.ppermute(value, axes, [(source, source + steps) for source in range(f...]
    all_to_all x1, blocking collectives: 18.4 us -> 23.2 us  [exchange(): return lax.all_to_all(value, axes, 0, 0, tiled=True)]
    all_to_all x2, waiting for transfers between devices: 28.6 us -> 31.7 us  [exchange(): return lax.all_to_all(value, axes, 0, 0, tiled=True)]
  transfers between devices with their start and end apart: 4 -> 4, of which waited for: 3 -> 2; matrix products, arithmetic and copies ran while one was open for 0% -> 0% of each run, Pallas kernels for 1% -> 2%
where the time goes in v5:
time: 111 us; the launch traced here: 110 us
  starting transfers between devices  47.3 us (43%)
  waiting for transfers between devices  31.7 us (29%)
  blocking collectives  23.2 us (21%)
  Pallas kernels  3.82 us (3%)
  local copies, waits for them, and re-layouts  3.56 us (3%)
    all_to_all x2, waiting for transfers between devices, exchange(): return lax.all_to_all(value, axes, 0, 0, tiled=True)  31.7 us
    all_to_all x2, starting transfers between devices, exchange(): return lax.all_to_all(value, axes, 0, 0, tiled=True)  27.6 us
    all_to_all x1, blocking collectives, exchange(): return lax.all_to_all(value, axes, 0, 0, tiled=True)  23.2 us
    ppermute x2, starting transfers between devices, passed_along(): lax.ppermute(value, axes, [(source, source + steps) for source in range(f...  19.7 us
    unnamed x10, local copies, waits for them, and re-layouts  2.81 us
  transfers between devices with their start and end apart: 4, of which 2 were waited for; matrix products, arithmetic and copies ran while one was open for 0% of the time, Pallas kernels for 2%

profile of v5, /device:TPU:1, one launch (start us, length us, event | category | flops | bytes accessed | tf_op | source)
XLA Modules:
  0.0 110.5 jit_solution(13844363611338601064)
XLA Ops:
  0.6 16.1 %collective-permute-start = (bf16[4,64,128]{2,1,0:T(8,128)(2,1)}, bf16[4,64,128]{2,1,0:T(8,128)(2,1)S(1)}, u32[]{:S(2)}, u32[]{:S(2)}) collective-permute-start(bf16[4,64,128]{2,1,0:T(8,128)(2,1)} %bitcast.9), channel_id=1, source_target_pairs={{1,0},{2,1},{3,2},{4,3},{5,4},{6,5},{7,6},{8,7},{9,8},{10,9},{11,1... | collective-permute-start | bytes 196616 | tf_op jit(solution)/shard_map/ppermute | solution.py:21
  16.7 0.0 copy-start
  16.7 0.9 copy-done
  17.7 0.0 copy-start.2
  17.7 1.0 copy-done.2
  18.7 0.0 copy-start.4
  18.7 0.8 copy-done.4
  19.5 0.7 own.1
  20.2 0.0 collective-permute-done.later_ref
  20.2 1.1 joined.1
  21.3 0.0 copy-start.1
  21.3 5.7 %all-to-all-start = ((bf16[64,32,128]{2,1,0:T(8,128)(2,1)}), bf16[64,32,128]{2,1,0:T(8,128)(2,1)S(1)}, u32[]{:S(2)}, u32[]{:S(2)}) async-start(bf16[64,32,128]{2,1,0:T(8,128)(2,1)} %joined.1), calls=%async_computation | async-start | bytes 1048576 | tf_op jit(solution)/shard_map/all_to_all | solution.py:25
  27.0 0.0 copy-done.1
  27.0 0.0 copy-start.3
  27.0 3.7 %collective-permute-start.1 = (bf16[1,8,64,128]{3,2,1,0:T(8,128)(2,1)S(1)}, bf16[1,8,64,128]{3,2,1,0:T(8,128)(2,1)S(1)}, u32[]{:S(2)}, u32[]{:S(2)}) collective-permute-start(bf16[1,8,64,128]{3,2,1,0:T(8,128)(2,1)S(1)} %slice_bitcast_fusion), channel_id=1, source_target_pairs={{0,1},{1,2},{2,3},{3,4},{4,5},{5,6},{6,7},{7,8},{8,9},{9,10},{10,1... | collective-permute-start | bytes 393224 | tf_op jit(solution)/shard_map/ppermute | solution.py:21
  30.7 9.1 %all-to-all-done = bf16[64,32,128]{2,1,0:T(8,128)(2,1)S(1)} async-done(((bf16[64,32,128]{2,1,0:T(8,128)(2,1)}), bf16[64,32,128]{2,1,0:T(8,128)(2,1)S(1)}, u32[]{:S(2)}, u32[]{:S(2)}) %all-to-all-start) | async-done | bytes 524320 | tf_op jit(solution)/shard_map/all_to_all | solution.py:25
  39.8 0.1 convert_reduce_fusion
  39.9 0.0 collective-permute-done.1.rim_ref
  39.9 0.7 broadcast_in_dim.8
  40.5 21.9 %all-to-all-start.1 = ((bf16[16,32,128]{2,1,0:T(8,128)(2,1)}), bf16[16,32,128]{2,1,0:T(8,128)(2,1)S(1)}, u32[]{:S(2)}, u32[]{:S(2)}) async-start(bf16[16,32,128]{2,1,0:T(8,128)(2,1)} %broadcast_in_dim.8), calls=%async_computation.1 | async-start | bytes 262144 | tf_op jit(solution)/shard_map/all_to_all | solution.py:25
  62.5 0.0 copy-done.3
  62.5 1.1 finish.1
  63.6 22.6 %all-to-all-done.1 = bf16[16,32,128]{2,1,0:T(8,128)(2,1)S(1)} async-done(((bf16[16,32,128]{2,1,0:T(8,128)(2,1)}), bf16[16,32,128]{2,1,0:T(8,128)(2,1)S(1)}, u32[]{:S(2)}, u32[]{:S(2)}) %all-to-all-start.1) | async-done | bytes 131104 | tf_op jit(solution)/shard_map/all_to_all | solution.py:25
  86.2 0.1 broadcast_in_dim.21
  86.3 23.2 %all_to_all.15.chunks_ref = bf16[64,32,128]{2,1,0:T(8,128)(2,1)S(1)} all-to-all(bf16[64,32,128]{2,1,0:T(8,128)(2,1)S(1)} %broadcast_in_dim.21), channel_id=1, replica_groups=mesh['x'=4,'zh'=4,'y'=4,'zn'=4,'ze'=2,'c'=2] {'x','y','ze','c'}, dimensions={0} | all-to-all | bytes 1048576 | tf_op jit(solution)/shard_map/all_to_all | solution.py:25
  109.5 1.0 spread_out.1
  (2 shorter events, 0.0 us)
Async XLA Ops:
  0.6 19.6 %collective-permute-start = (bf16[4,64,128]{2,1,0:T(8,128)(2,1)}, bf16[4,64,128]{2,1,0:T(8,128)(2,1)S(1)}, u32[]{:S(2)}, u32[]{:S(2)}) collective-permute-start(bf16[4,64,128]{2,1,0:T(8,128)(2,1)} %bitcast.9), channel_id=1, source_target_pairs={{1,0},{2,1},{3,2},{4,3},{5,4},{6,5},{7,6},{8,7},{9,8},{10,9},{11,1... | collective-permute-start | bytes 196616 | tf_op jit(solution)/shard_map/ppermute | solution.py:21
  16.7 1.0 copy-start
  17.7 1.0 copy-start.2
  18.7 0.8 copy-start.4
  21.3 5.7 %copy-start.1 = (bf16[1,2,8,64,128]{4,3,2,1,0:T(8,128)(2,1)S(1)}, bf16[1,2,8,64,128]{4,3,2,1,0:T(8,128)(2,1)}, u32[]{:S(2)}) copy-start(bf16[1,2,8,64,128]{4,3,2,1,0:T(8,128)(2,1)} %param.3) | copy-start | bytes 786436
  21.3 18.5 %all-to-all-start = ((bf16[64,32,128]{2,1,0:T(8,128)(2,1)}), bf16[64,32,128]{2,1,0:T(8,128)(2,1)S(1)}, u32[]{:S(2)}, u32[]{:S(2)}) async-start(bf16[64,32,128]{2,1,0:T(8,128)(2,1)} %joined.1), calls=%async_computation | async-start | bytes 1048576 | tf_op jit(solution)/shard_map/all_to_all | solution.py:25
  27.0 35.5 %copy-start.3 = (bf16[3,3,3,64,128]{4,3,2,1,0:T(8,128)(2,1)S(1)}, bf16[3,3,3,64,128]{4,3,2,1,0:T(8,128)(2,1)}, u32[]{:S(2)}) copy-start(bf16[3,3,3,64,128]{4,3,2,1,0:T(8,128)(2,1)} %weight_ref.3) | copy-start | bytes 1327108
  27.0 12.9 %collective-permute-start.1 = (bf16[1,8,64,128]{3,2,1,0:T(8,128)(2,1)S(1)}, bf16[1,8,64,128]{3,2,1,0:T(8,128)(2,1)S(1)}, u32[]{:S(2)}, u32[]{:S(2)}) collective-permute-start(bf16[1,8,64,128]{3,2,1,0:T(8,128)(2,1)S(1)} %slice_bitcast_fusion), channel_id=1, source_target_pairs={{0,1},{1,2},{2,3},{3,4},{4,5},{5,6},{6,7},{7,8},{8,9},{9,10},{10,1... | collective-permute-start | bytes 393224 | tf_op jit(solution)/shard_map/ppermute | solution.py:21
  40.5 45.7 %all-to-all-start.1 = ((bf16[16,32,128]{2,1,0:T(8,128)(2,1)}), bf16[16,32,128]{2,1,0:T(8,128)(2,1)S(1)}, u32[]{:S(2)}, u32[]{:S(2)}) async-start(bf16[16,32,128]{2,1,0:T(8,128)(2,1)} %broadcast_in_dim.8), calls=%async_computation.1 | async-start | bytes 262144 | tf_op jit(solution)/shard_map/all_to_all | solution.py:25

commit v6 on v5

v6 whole, which is shorter than its diff:
```python
import functools
import math

import jax
import jax.numpy as jnp
from jax import lax
from jax.experimental import pallas as pl
from jax.experimental.pallas import tpu as pltpu
from jax.sharding import PartitionSpec as P

DP = ("x", "zh")
SPACE = ("y", "zn", "ze", "c")
SLAB = ("x", "y", "ze", "c")
LINE = ("zh", "zn")
SIZES = (4, 4, 4, 4, 2, 2)
VMEM_BYTES = 16 << 20


def passed_along(value, axes, steps):
    count = math.prod(lax.axis_size(axis) for axis in axes)
    first, last = (max(0, -steps), min(count, count - steps))
    return lax.ppermute(value, axes, [(source, source + steps) for source in range(first, last)])


def exchange(value, axes):
    return lax.all_to_all(value, axes, 0, 0, tiled=True)


def with_next_pair(cells, pairs):
    wide = cells.astype(jnp.float32)
    rows = wide.shape[0]
    row = lax.broadcasted_iota(jnp.int32, wide.shape, 0)
    ahead = jnp.where(row % pairs == pairs - 1, 0.0, pltpu.roll(wide, rows - 1, 0))
    return jnp.concatenate([cells, ahead.astype(jnp.bfloat16)], axis=1)


def from_previous_pair(wide, pairs):
    row = lax.broadcasted_iota(jnp.int32, wide.shape, 0)
    return jnp.where(row % pairs == 0, 0.0, pltpu.roll(wide, 1, 0))


def plane_rows(plane, rows_out):
    even = jnp.concatenate([plane[2 * b] for b in range(rows_out)], axis=0)
    odd = jnp.concatenate([plane[2 * b + 1] for b in range(rows_out)], axis=0)
    return even, odd


def tap_weight(weight, depth_tap, height_tap):
    taps = weight[depth_tap, height_tap]
    pair = jnp.concatenate([taps[1], taps[2]], axis=0)
    left = jnp.concatenate([jnp.zeros_like(taps[0]), taps[0]], axis=0)
    return jnp.concatenate([pair, left], axis=1)


def forward_dot(rows, weight):
    return lax.dot_general(
        rows, weight, (((1,), (0,)), ((), ())), preferred_element_type=jnp.float32
    )


def backward_dot(rows, weight):
    return lax.dot_general(
        rows, weight, (((1,), (1,)), ((), ())), preferred_element_type=jnp.float32
    )


def kernel_dot(rows, grads):
    return lax.dot_general(
        rows, grads, (((0,), (0,)), ((), ())), preferred_element_type=jnp.float32
    )


def store_kernel_terms(terms_ref, base, plane, grads, rows_out, pairs, cin, cout):
    even, odd = plane_rows(plane, rows_out)
    kept = (rows_out - 1) * pairs
    products = (
        kernel_dot(odd[:kept], grads[pairs:]),
        kernel_dot(even, grads),
        kernel_dot(odd, grads),
    )
    for height_tap in range(3):
        product = products[height_tap]
        start = base + height_tap * 3 * cin
        terms_ref[start : start + cin] = product[cin:, cout:].astype(terms_ref.dtype)
        terms_ref[start + cin : start + 3 * cin] = product[:, :cout].astype(terms_ref.dtype)


def forward_terms(plane, weight, depth_tap, rows_out, pairs):
    even, odd = plane_rows(plane, rows_out)
    lifted = jnp.concatenate([jnp.zeros_like(odd[:pairs]), odd[: (rows_out - 1) * pairs]], axis=0)
    return (
        forward_dot(lifted, tap_weight(weight, depth_tap, 0))
        + forward_dot(even, tap_weight(weight, depth_tap, 1))
        + forward_dot(odd, tap_weight(weight, depth_tap, 2))
    )


def backward_terms(grads, weight, depth_tap, pairs):
    raised = jnp.concatenate([grads[pairs:], jnp.zeros_like(grads[:pairs])], axis=0)
    even = backward_dot(grads, tap_weight(weight, depth_tap, 1))
    odd = backward_dot(grads, tap_weight(weight, depth_tap, 2)) + backward_dot(
        raised, tap_weight(weight, depth_tap, 0)
    )
    return even, odd


def own_kernel(local_ref, grads_ref, head_ref, rest_ref, terms_ref):
    rows_out, pairs, cout = grads_ref.shape
    cin = local_ref.shape[3] // 2
    grads = with_next_pair(grads_ref[...].reshape(rows_out * pairs, cout), pairs)
    for plane in range(2):
        store_kernel_terms(
            terms_ref, plane * 9 * cin, local_ref[plane], grads, rows_out, pairs, cin, cout
        )
    kept = head_ref.shape[0]
    head_ref[...] = terms_ref[:kept]
    rest_ref[...] = terms_ref[kept:]


def joined_kernel(step, local_ref, later_ref, rest_ref, chunks_ref, scratch_ref):
    rows_out, pairs, cout = later_ref.shape
    cin = local_ref.shape[3] // 2
    count, rows, _ = chunks_ref.shape
    rest = rest_ref.shape[0]
    total = rest + 9 * cin
    later = with_next_pair(later_ref[...].reshape(rows_out * pairs, cout), pairs)
    scratch_ref[:rest] = rest_ref[...].astype(jnp.float32)
    store_kernel_terms(scratch_ref, rest, local_ref[1], later, rows_out, pairs, cin, cout)
    scratch_ref[total:] = jnp.zeros((scratch_ref.shape[0] - total, cout), jnp.float32)
    for index in range(count):
        chunks_ref[index] = scratch_ref[index * step : index * step + rows].astype(jnp.bfloat16)


def copies_kernel(first_ref, second_ref, copies_ref):
    first = jnp.sum(first_ref[...].astype(jnp.float32), axis=0).astype(jnp.bfloat16)
    second = jnp.sum(second_ref[...].astype(jnp.float32), axis=0).astype(jnp.bfloat16)
    piece = jnp.concatenate([first, second], axis=0)
    for index in range(copies_ref.shape[0]):
        copies_ref[index] = piece


def finish_kernel(
    rim_ref, local_ref, grads_ref, later_ref, weight_ref, output_ref, grad_ref
):
    rows_out, pairs, cout = later_ref.shape
    cells = rows_out * pairs
    grads = with_next_pair(grads_ref[...].reshape(cells, cout), pairs)
    later = with_next_pair(later_ref[...].reshape(cells, cout), pairs)
    total = (
        forward_terms(rim_ref[0], weight_ref, 0, rows_out, pairs)
        + forward_terms(local_ref[0], weight_ref, 1, rows_out, pairs)
        + forward_terms(local_ref[1], weight_ref, 2, rows_out, pairs)
    )
    result = total[:, :cout] + from_previous_pair(total[:, cout:], pairs)
    output_ref[...] = result.astype(jnp.bfloat16).reshape(output_ref.shape)
    spilled = backward_terms(later, weight_ref, 0, pairs)
    own = backward_terms(grads, weight_ref, 2, pairs)
    planes = (
        backward_terms(grads, weight_ref, 1, pairs),
        (spilled[0] + own[0], spilled[1] + own[1]),
    )
    for plane, sides in enumerate(planes):
        for side, values in enumerate(sides):
            rounded = values.astype(jnp.bfloat16)
            for b in range(rows_out):
                grad_ref[plane, 2 * b + side] = rounded[b * pairs : (b + 1) * pairs]


def spread_kernel(head, step, cin, factor, chunks_ref, grad_ref):
    count = chunks_ref.shape[0]
    ahead = 9 * cin
    total = 27 * cin
    for index in range(count):
        block = chunks_ref[index].astype(jnp.float32) * factor
        grad_ref[ahead + index * head : ahead + (index + 1) * head] = block[:head]
        start = ahead + count * head + index * step
        stop = start + step
        below = min(max(total - start, 0), step)
        if below:
            grad_ref[start : start + below] = block[head : head + below]
        if below < step:
            grad_ref[start + below - total : stop - total] = block[head + below : head + step]


def shards(volume, weight, cotangent):
    local = volume[0]
    grads = cotangent[0, 0]
    rows_out, pairs, cout = grads.shape
    cin = weight.shape[3]
    total = 27 * cin
    cells = rows_out * pairs
    count = math.prod(lax.axis_size(axis) for axis in SLAB)
    head = 18 * cin // count // 16 * 16
    step = total // count - head
    rows = -(-step // 16) * 16
    devices = math.prod(lax.axis_size(axis) for axis in DP + SPACE)
    factor = 1.0 / math.sqrt(devices * cells)

    later = passed_along(grads, SPACE, -1)
    rim = passed_along(local[1:2], SPACE, 1)
    kept = count * head
    leaving, rest = pl.pallas_call(
        own_kernel,
        out_shape=(
            jax.ShapeDtypeStruct((kept, cout), jnp.bfloat16),
            jax.ShapeDtypeStruct((18 * cin - kept, cout), jnp.bfloat16),
        ),
        scratch_shapes=[pltpu.VMEM((18 * cin, cout), jnp.bfloat16)],
        cost_estimate=pl.CostEstimate(flops=100_000_000, bytes_accessed=600_000, transcendentals=0),
        compiler_params=pltpu.CompilerParams(vmem_limit_bytes=VMEM_BYTES),
        name="own",
    )(local, grads)
    first = exchange(leaving.reshape(count, head, cout), SLAB)
    chunks = pl.pallas_call(
        functools.partial(joined_kernel, step),
        out_shape=jax.ShapeDtypeStruct((count, rows, cout), jnp.bfloat16),
        scratch_shapes=[pltpu.VMEM((count * step + 16, cout), jnp.float32)],
        cost_estimate=pl.CostEstimate(flops=40_000_000_000, bytes_accessed=600_000, transcendentals=0),
        compiler_params=pltpu.CompilerParams(vmem_limit_bytes=VMEM_BYTES),
        name="joined",
    )(local, later, rest)
    second = exchange(chunks, SLAB)
    first, second, rim = lax.optimization_barrier((first, second, rim))
    lines = math.prod(lax.axis_size(axis) for axis in LINE)
    copies = pl.pallas_call(
        copies_kernel,
        out_shape=jax.ShapeDtypeStruct((lines, head + rows, cout), jnp.bfloat16),
        cost_estimate=pl.CostEstimate(flops=500_000, bytes_accessed=700_000, transcendentals=0),
        compiler_params=pltpu.CompilerParams(vmem_limit_bytes=VMEM_BYTES),
        name="copies",
    )(first, second)
    piece = jnp.sum(exchange(copies, LINE).astype(jnp.float32), axis=0)

    output, grad_volume = pl.pallas_call(
        finish_kernel,
        out_shape=(
            jax.ShapeDtypeStruct((rows_out, pairs, cout), jnp.bfloat16),
            jax.ShapeDtypeStruct((2, 2 * rows_out, pairs, 2 * cin), jnp.bfloat16),
        ),
        cost_estimate=pl.CostEstimate(flops=400_000_000, bytes_accessed=1_500_000, transcendentals=0),
        compiler_params=pltpu.CompilerParams(vmem_limit_bytes=VMEM_BYTES),
        name="finish",
    )(rim, local, grads, later, weight)
    piece, output, grad_volume = lax.optimization_barrier((piece, output, grad_volume))
    copies = jnp.broadcast_to(piece.astype(jnp.bfloat16)[None], (count, head + rows, cout))
    gathered = exchange(copies, SLAB)
    grad_weight = pl.pallas_call(
        functools.partial(spread_kernel, head, step, cin, factor),
        out_shape=jax.ShapeDtypeStruct((total, cout), jnp.float32),
        compiler_params=pltpu.CompilerParams(vmem_limit_bytes=VMEM_BYTES),
        name="spread_out",
    )(gathered)
    return (output[None, None], grad_volume[None], grad_weight.reshape(weight.shape))


def solution(mesh):
    fine = jax.sharding.Mesh(mesh.devices.reshape(SIZES), DP + SPACE)
    split = P(DP, SPACE, None, None, None)
    return jax.shard_map(
        shards,
        mesh=fine,
        in_specs=(split, P(), split),
        out_specs=(split, split, P()),
        check_vma=False,
    )
```

time: 111 us -> 121 us (1.090)
  waiting for transfers between devices: 31.7 us -> 36.3 us
  starting transfers between devices: 47.3 us -> 50.7 us
  blocking collectives: 23.2 us -> 25.8 us
  local copies, waits for them, and re-layouts: 3.56 us -> 1.88 us
  Pallas kernels: 3.82 us -> 5.23 us
    all_to_all x2 -> x3, starting transfers between devices: 27.6 us -> 31 us  [exchange(): return lax.all_to_all(value, axes, 0, 0, tiled=True)]
    all_to_all x2 -> x3, waiting for transfers between devices: 31.7 us -> 34.3 us  [exchange(): return lax.all_to_all(value, axes, 0, 0, tiled=True)]
    all_to_all x1, blocking collectives: 23.2 us -> 25.8 us  [exchange(): return lax.all_to_all(value, axes, 0, 0, tiled=True)]
    ppermute x2, waiting for transfers between devices: 0.01 us -> 1.93 us  [passed_along(): lax.ppermute(value, axes, [(source, source + steps) for source in range(f...]
    pallas_call x3 -> x4, Pallas kernels: 2.75 us -> 3.75 us  [the longest x1 1.05 us: shards(): pl.pallas_call(own_kernel, out_shape=(jax.ShapeDtypeStruct((kept, cout),...]
  transfers between devices with their start and end apart: 4 -> 5, of which waited for: 2 -> 4; matrix products, arithmetic and copies ran while one was open for 0% -> 0% of each run, Pallas kernels for 2% -> 3%
where the time goes in v6:
time: 121 us
  starting transfers between devices  50.7 us (42%)
  waiting for transfers between devices  36.3 us (30%)
  blocking collectives  25.8 us (21%)
  Pallas kernels  5.23 us (4%)
  local copies, waits for them, and re-layouts  1.88 us (2%)
    all_to_all x3, waiting for transfers between devices, exchange(): return lax.all_to_all(value, axes, 0, 0, tiled=True)  34.3 us
    all_to_all x3, starting transfers between devices, exchange(): return lax.all_to_all(value, axes, 0, 0, tiled=True)  31 us
    all_to_all x1, blocking collectives, exchange(): return lax.all_to_all(value, axes, 0, 0, tiled=True)  25.8 us
    ppermute x2, starting transfers between devices, passed_along(): lax.ppermute(value, axes, [(source, source + steps) for source in range(f...  19.7 us
  transfers between devices with their start and end apart: 5, of which 4 were waited for; matrix products, arithmetic and copies ran while one was open for 0% of the time, Pallas kernels for 3%

profile of v6, /device:TPU:1, one launch (start us, length us, event | category | flops | bytes accessed | tf_op | source)
XLA Modules:
  0.0 120.6 jit_solution(957182697343774268)
XLA Ops:
  0.6 16.1 %collective-permute-start = (bf16[4,64,128]{2,1,0:T(8,128)(2,1)}, bf16[4,64,128]{2,1,0:T(8,128)(2,1)S(1)}, u32[]{:S(2)}, u32[]{:S(2)}) collective-permute-start(bf16[4,64,128]{2,1,0:T(8,128)(2,1)} %bitcast.11), channel_id=1, source_target_pairs={{1,0},{2,1},{3,2},{4,3},{5,4},{6,5},{7,6},{8,7},{9,8},{10,9},{11,1... | collective-permute-start | bytes 196616 | tf_op jit(solution)/shard_map/ppermute | solution.py:22
  16.7 0.0 copy-start
  16.7 0.9 copy-done
  17.7 0.0 copy-start.3
  17.7 0.8 copy-done.3
  18.5 1.1 own.1
  19.5 0.0 copy-start.1
  19.6 5.7 %all-to-all-start = ((bf16[64,16,128]{2,1,0:T(8,128)(2,1)}), bf16[64,16,128]{2,1,0:T(8,128)(2,1)S(1)}, u32[]{:S(2)}, u32[]{:S(2)}) async-start(bf16[64,16,128]{2,1,0:T(8,128)(2,1)} %bitcast.2), calls=%async_computation | async-start | bytes 524288 | tf_op jit(solution)/shard_map/all_to_all | solution.py:26
  25.2 0.0 collective-permute-done.later_ref
  25.2 0.0 copy-done.1
  25.2 1.0 joined.1
  26.2 9.0 %all-to-all-done.first_ref = bf16[64,16,128]{2,1,0:T(8,128)(2,1)S(1)} async-done(((bf16[64,16,128]{2,1,0:T(8,128)(2,1)}), bf16[64,16,128]{2,1,0:T(8,128)(2,1)S(1)}, u32[]{:S(2)}, u32[]{:S(2)}) %all-to-all-start) | async-done | bytes 262176 | tf_op jit(solution)/shard_map/all_to_all | solution.py:26
  35.2 4.5 %all-to-all-start.1 = ((bf16[64,16,128]{2,1,0:T(8,128)(2,1)}), bf16[64,16,128]{2,1,0:T(8,128)(2,1)S(1)}, u32[]{:S(2)}, u32[]{:S(2)}) async-start(bf16[64,16,128]{2,1,0:T(8,128)(2,1)} %joined.1), calls=%async_computation.1 | async-start | bytes 524288 | tf_op jit(solution)/shard_map/all_to_all | solution.py:26
  39.8 0.0 copy-start.2
  39.8 3.7 %collective-permute-start.1 = (bf16[1,8,64,128]{3,2,1,0:T(8,128)(2,1)S(1)}, bf16[1,8,64,128]{3,2,1,0:T(8,128)(2,1)S(1)}, u32[]{:S(2)}, u32[]{:S(2)}) collective-permute-start(bf16[1,8,64,128]{3,2,1,0:T(8,128)(2,1)S(1)} %slice_bitcast_fusion), channel_id=1, source_target_pairs={{0,1},{1,2},{2,3},{3,4},{4,5},{5,6},{6,7},{7,8},{8,9},{9,10},{10,1... | collective-permute-start | bytes 393224 | tf_op jit(solution)/shard_map/ppermute | solution.py:22
  43.5 1.9 %collective-permute-done.1.rim_ref = bf16[1,8,64,128]{3,2,1,0:T(8,128)(2,1)S(1)} collective-permute-done((bf16[1,8,64,128]{3,2,1,0:T(8,128)(2,1)S(1)}, bf16[1,8,64,128]{3,2,1,0:T(8,128)(2,1)S(1)}, u32[]{:S(2)}, u32[]{:S(2)}) %collective-permute-start.1) | collective-permute-done | bytes 131104 | tf_op jit(solution)/shard_map/ppermute | solution.py:22
  45.4 4.5 %all-to-all-done.1.second_ref = bf16[64,16,128]{2,1,0:T(8,128)(2,1)S(1)} async-done(((bf16[64,16,128]{2,1,0:T(8,128)(2,1)}), bf16[64,16,128]{2,1,0:T(8,128)(2,1)S(1)}, u32[]{:S(2)}, u32[]{:S(2)}) %all-to-all-start.1) | async-done | bytes 262176 | tf_op jit(solution)/shard_map/all_to_all | solution.py:26
  49.8 0.7 copies.1
  50.6 0.0 copy-start.4
  50.6 20.8 %all-to-all-start.2 = ((bf16[16,32,128]{2,1,0:T(8,128)(2,1)}), bf16[16,32,128]{2,1,0:T(8,128)(2,1)S(1)}, u32[]{:S(2)}, u32[]{:S(2)}) async-start(bf16[16,32,128]{2,1,0:T(8,128)(2,1)} %copies.1), calls=%async_computation.2 | async-start | bytes 262144 | tf_op jit(solution)/shard_map/all_to_all | solution.py:26
  71.4 0.0 copy-done.2
  71.4 0.0 copy-done.4
  71.4 1.5 %finish.1 = (bf16[4,64,128]{2,1,0:T(8,128)(2,1)}, bf16[2,8,64,128]{3,2,1,0:T(8,128)(2,1)}) custom-call(bf16[1,8,64,128]{3,2,1,0:T(8,128)(2,1)S(1)} %collective-permute-done.1.rim_ref, bf16[2,8,64,128]{3,2,1,0:T(8,128)(2,1)S(1)} %bitcast.10, bf16[4,64,128]{2,1,0:T(8,128)(2,1)S(1)} %bitcast.13, bf16[4,64,128]{2,1,0:T(8,128)(2,1)S(1)} %collective-permute-done.later_ref, ...), custom_call_target="tpu_custom_call" | custom-call | flops 400000000 | bytes 1500000 | tf_op jit(solution)/shard_map/finish/pallas_call | solution.py:234
  72.9 20.9 %all-to-all-done.2 = bf16[16,32,128]{2,1,0:T(8,128)(2,1)S(1)} async-done(((bf16[16,32,128]{2,1,0:T(8,128)(2,1)}), bf16[16,32,128]{2,1,0:T(8,128)(2,1)S(1)}, u32[]{:S(2)}, u32[]{:S(2)}) %all-to-all-start.2) | async-done | bytes 131104 | tf_op jit(solution)/shard_map/all_to_all | solution.py:26
  93.8 0.1 broadcast_in_dim.14
  93.9 25.8 %all_to_all.20.chunks_ref = bf16[64,32,128]{2,1,0:T(8,128)(2,1)S(1)} all-to-all(bf16[64,32,128]{2,1,0:T(8,128)(2,1)S(1)} %broadcast_in_dim.14), channel_id=1, replica_groups=mesh['x'=4,'zh'=4,'y'=4,'zn'=4,'ze'=2,'c'=2] {'x','y','ze','c'}, dimensions={0} | all-to-all | bytes 1048576 | tf_op jit(solution)/shard_map/all_to_all | solution.py:26
  119.6 1.0 spread_out.1
  (2 shorter events, 0.0 us)
Async XLA Ops:
  0.6 24.6 %collective-permute-start = (bf16[4,64,128]{2,1,0:T(8,128)(2,1)}, bf16[4,64,128]{2,1,0:T(8,128)(2,1)S(1)}, u32[]{:S(2)}, u32[]{:S(2)}) collective-permute-start(bf16[4,64,128]{2,1,0:T(8,128)(2,1)} %bitcast.11), channel_id=1, source_target_pairs={{1,0},{2,1},{3,2},{4,3},{5,4},{6,5},{7,6},{8,7},{9,8},{10,9},{11,1... | collective-permute-start | bytes 196616 | tf_op jit(solution)/shard_map/ppermute | solution.py:22
  16.7 1.0 copy-start
  17.7 0.8 copy-start.3
  19.5 5.7 %copy-start.1 = (bf16[1,2,8,64,128]{4,3,2,1,0:T(8,128)(2,1)S(1)}, bf16[1,2,8,64,128]{4,3,2,1,0:T(8,128)(2,1)}, u32[]{:S(2)}) copy-start(bf16[1,2,8,64,128]{4,3,2,1,0:T(8,128)(2,1)} %param.3) | copy-start | bytes 786436
  19.6 15.7 %all-to-all-start = ((bf16[64,16,128]{2,1,0:T(8,128)(2,1)}), bf16[64,16,128]{2,1,0:T(8,128)(2,1)S(1)}, u32[]{:S(2)}, u32[]{:S(2)}) async-start(bf16[64,16,128]{2,1,0:T(8,128)(2,1)} %bitcast.2), calls=%async_computation | async-start | bytes 524288 | tf_op jit(solution)/shard_map/all_to_all | solution.py:26
  35.2 14.6 %all-to-all-start.1 = ((bf16[64,16,128]{2,1,0:T(8,128)(2,1)}), bf16[64,16,128]{2,1,0:T(8,128)(2,1)S(1)}, u32[]{:S(2)}, u32[]{:S(2)}) async-start(bf16[64,16,128]{2,1,0:T(8,128)(2,1)} %joined.1), calls=%async_computation.1 | async-start | bytes 524288 | tf_op jit(solution)/shard_map/all_to_all | solution.py:26
  39.8 31.6 %copy-start.2 = (bf16[3,3,3,64,128]{4,3,2,1,0:T(8,128)(2,1)S(1)}, bf16[3,3,3,64,128]{4,3,2,1,0:T(8,128)(2,1)}, u32[]{:S(2)}) copy-start(bf16[3,3,3,64,128]{4,3,2,1,0:T(8,128)(2,1)} %weight_ref.1) | copy-start | bytes 1327108
  39.8 5.6 %collective-permute-start.1 = (bf16[1,8,64,128]{3,2,1,0:T(8,128)(2,1)S(1)}, bf16[1,8,64,128]{3,2,1,0:T(8,128)(2,1)S(1)}, u32[]{:S(2)}, u32[]{:S(2)}) collective-permute-start(bf16[1,8,64,128]{3,2,1,0:T(8,128)(2,1)S(1)} %slice_bitcast_fusion), channel_id=1, source_target_pairs={{0,1},{1,2},{2,3},{3,4},{4,5},{5,6},{6,7},{7,8},{8,9},{9,10},{10,1... | collective-permute-start | bytes 393224 | tf_op jit(solution)/shard_map/ppermute | solution.py:22
  50.6 20.8 %copy-start.4 = (bf16[1,1,4,64,128]{4,3,2,1,0:T(8,128)(2,1)S(1)}, bf16[1,1,4,64,128]{4,3,2,1,0:T(8,128)(2,1)}, u32[]{:S(2)}) copy-start(bf16[1,1,4,64,128]{4,3,2,1,0:T(8,128)(2,1)} %param.5) | copy-start | bytes 196612
  50.6 43.2 %all-to-all-start.2 = ((bf16[16,32,128]{2,1,0:T(8,128)(2,1)}), bf16[16,32,128]{2,1,0:T(8,128)(2,1)S(1)}, u32[]{:S(2)}, u32[]{:S(2)}) async-start(bf16[16,32,128]{2,1,0:T(8,128)(2,1)} %copies.1), calls=%async_computation.2 | async-start | bytes 262144 | tf_op jit(solution)/shard_map/all_to_all | solution.py:26

commit v7 on v6

--- a/solution.py
+++ b/solution.py
@@ -104,7 +104,7 @@
     return even, odd
 
 
-def own_kernel(local_ref, grads_ref, head_ref, rest_ref, terms_ref):
+def own_kernel(local_ref, grads_ref, terms_ref, plane_ref):
     rows_out, pairs, cout = grads_ref.shape
     cin = local_ref.shape[3] // 2
     grads = with_next_pair(grads_ref[...].reshape(rows_out * pairs, cout), pairs)
@@ -112,29 +112,25 @@
         store_kernel_terms(
             terms_ref, plane * 9 * cin, local_ref[plane], grads, rows_out, pairs, cin, cout
         )
-    kept = head_ref.shape[0]
-    head_ref[...] = terms_ref[:kept]
-    rest_ref[...] = terms_ref[kept:]
-
-
-def joined_kernel(step, local_ref, later_ref, rest_ref, chunks_ref, scratch_ref):
+    plane_ref[0] = local_ref[1]
+
+
+def joined_kernel(local_ref, later_ref, terms_ref, chunks_ref, scratch_ref):
     rows_out, pairs, cout = later_ref.shape
     cin = local_ref.shape[3] // 2
     count, rows, _ = chunks_ref.shape
-    rest = rest_ref.shape[0]
-    total = rest + 9 * cin
+    total = 27 * cin
+    step = total // count
     later = with_next_pair(later_ref[...].reshape(rows_out * pairs, cout), pairs)
-    scratch_ref[:rest] = rest_ref[...].astype(jnp.float32)
-    store_kernel_terms(scratch_ref, rest, local_ref[1], later, rows_out, pairs, cin, cout)
+    store_kernel_terms(scratch_ref, 0, local_ref[1], later, rows_out, pairs, cin, cout)
+    scratch_ref[9 * cin : total] = terms_ref[...]
     scratch_ref[total:] = jnp.zeros((scratch_ref.shape[0] - total, cout), jnp.float32)
     for index in range(count):
         chunks_ref[index] = scratch_ref[index * step : index * step + rows].astype(jnp.bfloat16)
 
 
-def copies_kernel(first_ref, second_ref, copies_ref):
-    first = jnp.sum(first_ref[...].astype(jnp.float32), axis=0).astype(jnp.bfloat16)
-    second = jnp.sum(second_ref[...].astype(jnp.float32), axis=0).astype(jnp.bfloat16)
-    piece = jnp.concatenate([first, second], axis=0)
+def copies_kernel(chunks_ref, copies_ref):
+    piece = jnp.sum(chunks_ref[...].astype(jnp.float32), axis=0).astype(jnp.bfloat16)
     for index in range(copies_ref.shape[0]):
         copies_ref[index] = piece
 
@@ -166,20 +162,10 @@
                 grad_ref[plane, 2 * b + side] = rounded[b * pairs : (b + 1) * pairs]
 
 
-def spread_kernel(head, step, cin, factor, chunks_ref, grad_ref):
-    count = chunks_ref.shape[0]
-    ahead = 9 * cin
-    total = 27 * cin
-    for index in range(count):
-        block = chunks_ref[index].astype(jnp.float32) * factor
-        grad_ref[ahead + index * head : ahead + (index + 1) * head] = block[:head]
-        start = ahead + count * head + index * step
-        stop = start + step
-        below = min(max(total - start, 0), step)
-        if below:
-            grad_ref[start : start + below] = block[head : head + below]
-        if below < step:
-            grad_ref[start + below - total : stop - total] = block[head + below : head + step]
+def spread_kernel(step, factor, chunks_ref, grad_ref):
+    for index in range(chunks_ref.shape[0]):
+        block = chunks_ref[index].astype(jnp.float32)[:step]
+        grad_ref[index * step : (index + 1) * step] = block * factor
 
 
 def shards(volume, weight, cotangent):
@@ -190,45 +176,42 @@
     total = 27 * cin
     cells = rows_out * pairs
     count = math.prod(lax.axis_size(axis) for axis in SLAB)
-    head = 18 * cin // count // 16 * 16
-    step = total // count - head
+    step = total // count
     rows = -(-step // 16) * 16
     devices = math.prod(lax.axis_size(axis) for axis in DP + SPACE)
     factor = 1.0 / math.sqrt(devices * cells)
 
     later = passed_along(grads, SPACE, -1)
-    rim = passed_along(local[1:2], SPACE, 1)
-    kept = count * head
-    leaving, rest = pl.pallas_call(
+    terms, plane = pl.pallas_call(
         own_kernel,
         out_shape=(
-            jax.ShapeDtypeStruct((kept, cout), jnp.bfloat16),
-            jax.ShapeDtypeStruct((18 * cin - kept, cout), jnp.bfloat16),
+            jax.ShapeDtypeStruct((18 * cin, cout), jnp.float32),
+            jax.ShapeDtypeStruct((1, *local.shape[1:]), jnp.bfloat16),
         ),
-        scratch_shapes=[pltpu.VMEM((18 * cin, cout), jnp.bfloat16)],
-        cost_estimate=pl.CostEstimate(flops=100_000_000, bytes_accessed=600_000, transcendentals=0),
+        cost_estimate=pl.CostEstimate(flops=300_000_000, bytes_accessed=2_000_000, transcendentals=0),
         compiler_params=pltpu.CompilerParams(vmem_limit_bytes=VMEM_BYTES),
         name="own",
     )(local, grads)
-    first = exchange(leaving.reshape(count, head, cout), SLAB)
     chunks = pl.pallas_call(
-        functools.partial(joined_kernel, step),
+        joined_kernel,
         out_shape=jax.ShapeDtypeStruct((count, rows, cout), jnp.bfloat16),
-        scratch_shapes=[pltpu.VMEM((count * step + 16, cout), jnp.float32)],
-        cost_estimate=pl.CostEstimate(flops=40_000_000_000, bytes_accessed=600_000, transcendentals=0),
+        scratch_shapes=[pltpu.VMEM((total + 16, cout), jnp.float32)],
+        cost_estimate=pl.CostEstimate(flops=60_000_000, bytes_accessed=1_000_000, transcendentals=0),
         compiler_params=pltpu.CompilerParams(vmem_limit_bytes=VMEM_BYTES),
         name="joined",
-    )(local, later, rest)
-    second = exchange(chunks, SLAB)
-    first, second, rim = lax.optimization_barrier((first, second, rim))
+    )(local, later, terms)
     lines = math.prod(lax.axis_size(axis) for axis in LINE)
     copies = pl.pallas_call(
         copies_kernel,
-        out_shape=jax.ShapeDtypeStruct((lines, head + rows, cout), jnp.bfloat16),
+        out_shape=jax.ShapeDtypeStruct((lines, rows, cout), jnp.bfloat16),
         cost_estimate=pl.CostEstimate(flops=500_000, bytes_accessed=700_000, transcendentals=0),
         compiler_params=pltpu.CompilerParams(vmem_limit_bytes=VMEM_BYTES),
         name="copies",
-    )(first, second)
+    )(exchange(chunks, SLAB))
+    copies, plane, later, local, grads = lax.optimization_barrier(
+        (copies, plane, later, local, grads)
+    )
+    rim = passed_along(plane, SPACE, 1)
     piece = jnp.sum(exchange(copies, LINE).astype(jnp.float32), axis=0)
 
     output, grad_volume = pl.pallas_call(
@@ -242,10 +225,10 @@
         name="finish",
     )(rim, local, grads, later, weight)
     piece, output, grad_volume = lax.optimization_barrier((piece, output, grad_volume))
-    copies = jnp.broadcast_to(piece.astype(jnp.bfloat16)[None], (count, head + rows, cout))
+    copies = jnp.broadcast_to(piece.astype(jnp.bfloat16)[None], (count, rows, cout))
     gathered = exchange(copies, SLAB)
     grad_weight = pl.pallas_call(
-        functools.partial(spread_kernel, head, step, cin, factor),
+        functools.partial(spread_kernel, step, factor),
         out_shape=jax.ShapeDtypeStruct((total, cout), jnp.float32),
         compiler_params=pltpu.CompilerParams(vmem_limit_bytes=VMEM_BYTES),
         name="spread_out",

time: 121 us -> 109 us (0.901)
  waiting for transfers between devices: 36.3 us -> 21.7 us
  blocking collectives: 25.8 us -> 37.9 us
  starting transfers between devices: 50.7 us -> 42.3 us
  Pallas kernels: 5.23 us -> 3.76 us
    all_to_all x3 -> x1, waiting for transfers between devices: 34.3 us -> 15.8 us  [exchange(): return lax.all_to_all(value, axes, 0, 0, tiled=True)]
    all_to_all x1 -> x2, blocking collectives: 25.8 us -> 37.9 us  [exchange(): return lax.all_to_all(value, axes, 0, 0, tiled=True)]
    all_to_all x3 -> x1, starting transfers between devices: 31 us -> 23.7 us  [exchange(): return lax.all_to_all(value, axes, 0, 0, tiled=True)]
    ppermute x2, waiting for transfers between devices: 1.93 us -> 5.9 us  [passed_along(): lax.ppermute(value, axes, [(source, source + steps) for source in range(f...]
    pallas_call x4, Pallas kernels: 3.75 us -> 2.29 us  [the longest x1 0.98 us: shards(): pl.pallas_call(functools.partial(spread_kernel, step, factor), out_shape=...]
  transfers between devices with their start and end apart: 5 -> 3, of which waited for: 4 -> 2; matrix products, arithmetic and copies ran while one was open for 0% -> 0% of each run, Pallas kernels for 3% -> 2%
where the time goes in v7:
time: 109 us; the launch traced here: 108 us
  starting transfers between devices  42.3 us (39%)
  blocking collectives  37.9 us (35%)
  waiting for transfers between devices  21.7 us (20%)
  Pallas kernels  3.76 us (3%)
  local copies, waits for them, and re-layouts  1.87 us (2%)
    all_to_all x2, blocking collectives, exchange(): return lax.all_to_all(value, axes, 0, 0, tiled=True)  37.9 us
    all_to_all x1, starting transfers between devices, exchange(): return lax.all_to_all(value, axes, 0, 0, tiled=True)  23.7 us
    ppermute x2, starting transfers between devices, passed_along(): lax.ppermute(value, axes, [(source, source + steps) for source in range(f...  18.6 us
    all_to_all x1, waiting for transfers between devices, exchange(): return lax.all_to_all(value, axes, 0, 0, tiled=True)  15.8 us
    ppermute x2, waiting for transfers between devices, passed_along(): lax.ppermute(value, axes, [(source, source + steps) for source in range(f...  5.9 us
  transfers between devices with their start and end apart: 3, of which 2 were waited for; matrix products, arithmetic and copies ran while one was open for 0% of the time, Pallas kernels for 2%

profile of v7, /device:TPU:1, one launch (start us, length us, event | category | flops | bytes accessed | tf_op | source)
XLA Modules:
  0.0 108.2 jit_solution(6540237203722796888)
XLA Ops:
  0.6 16.1 %collective-permute-start = (bf16[4,64,128]{2,1,0:T(8,128)(2,1)}, bf16[4,64,128]{2,1,0:T(8,128)(2,1)S(1)}, u32[]{:S(2)}, u32[]{:S(2)}) collective-permute-start(bf16[4,64,128]{2,1,0:T(8,128)(2,1)} %bitcast.8), channel_id=1, source_target_pairs={{1,0},{2,1},{3,2},{4,3},{5,4},{6,5},{7,6},{8,7},{9,8},{10,9},{11,1... | collective-permute-start | bytes 196616 | tf_op jit(solution)/shard_map/ppermute | solution.py:22
  16.7 0.0 copy-start
  16.7 0.9 copy-done
  17.7 0.0 copy-start.3
  17.7 0.8 copy-done.3
  18.5 0.3 own.1
  18.8 0.0 collective-permute-done.later_ref
  18.8 0.3 joined.1
  19.1 18.2 %all_to_all.15.chunks_ref = bf16[64,32,128]{2,1,0:T(8,128)(2,1)S(1)} all-to-all(bf16[64,32,128]{2,1,0:T(8,128)(2,1)S(1)} %joined.1), channel_id=1, replica_groups=mesh['x'=4,'zh'=4,'y'=4,'zn'=4,'ze'=2,'c'=2] {'x','y','ze','c'}, dimensions={0} | all-to-all | bytes 1048576 | tf_op jit(solution)/shard_map/all_to_all | solution.py:26
  37.3 0.0 copy-start.2
  37.3 0.0 copy-start.4
  37.3 0.7 copies.1
  38.0 0.0 copy-start.1
  38.0 23.7 %all-to-all-start.1 = ((bf16[16,32,128]{2,1,0:T(8,128)(2,1)}), bf16[16,32,128]{2,1,0:T(8,128)(2,1)S(1)}, u32[]{:S(2)}, u32[]{:S(2)}) async-start(bf16[16,32,128]{2,1,0:T(8,128)(2,1)} %copies.1), calls=%async_computation.1 | async-start | bytes 262144 | tf_op jit(solution)/shard_map/all_to_all | solution.py:26
  61.7 2.5 %collective-permute-start.1 = (bf16[1,8,64,128]{3,2,1,0:T(8,128)(2,1)S(1)}, bf16[1,8,64,128]{3,2,1,0:T(8,128)(2,1)S(1)}, u32[]{:S(2)}, u32[]{:S(2)}) collective-permute-start(bf16[1,8,64,128]{3,2,1,0:T(8,128)(2,1)S(1)} %get-tuple-element.18), channel_id=1, source_target_pairs={{0,1},{1,2},{2,3},{3,4},{4,5},{5,6},{6,7},{7,8},{8,9},{9,10},{10,1... | collective-permute-start | bytes 393224 | tf_op jit(solution)/shard_map/ppermute | solution.py:22
  64.2 5.9 %collective-permute-done.1.rim_ref = bf16[1,8,64,128]{3,2,1,0:T(8,128)(2,1)S(1)} collective-permute-done((bf16[1,8,64,128]{3,2,1,0:T(8,128)(2,1)S(1)}, bf16[1,8,64,128]{3,2,1,0:T(8,128)(2,1)S(1)}, u32[]{:S(2)}, u32[]{:S(2)}) %collective-permute-start.1) | collective-permute-done | bytes 131104 | tf_op jit(solution)/shard_map/ppermute | solution.py:22
  70.1 0.0 copy-done.2
  70.1 0.0 copy-done.4
  70.1 0.0 copy-done.1
  70.2 1.5 %finish.1 = (bf16[4,64,128]{2,1,0:T(8,128)(2,1)}, bf16[2,8,64,128]{3,2,1,0:T(8,128)(2,1)}) custom-call(bf16[1,8,64,128]{3,2,1,0:T(8,128)(2,1)S(1)} %collective-permute-done.1.rim_ref, bf16[2,8,64,128]{3,2,1,0:T(8,128)(2,1)S(1)} %bitcast.7, bf16[4,64,128]{2,1,0:T(8,128)(2,1)S(1)} %bitcast.10, bf16[4,64,128]{2,1,0:T(8,128)(2,1)S(1)} %collective-permute-done.later_ref, ...), custom_call_target="tpu_custom_call" | custom-call | flops 400000000 | bytes 1500000 | tf_op jit(solution)/shard_map/finish/pallas_call | solution.py:217
  71.6 15.8 %all-to-all-done.1 = bf16[16,32,128]{2,1,0:T(8,128)(2,1)S(1)} async-done(((bf16[16,32,128]{2,1,0:T(8,128)(2,1)}), bf16[16,32,128]{2,1,0:T(8,128)(2,1)S(1)}, u32[]{:S(2)}, u32[]{:S(2)}) %all-to-all-start.1) | async-done | bytes 131104 | tf_op jit(solution)/shard_map/all_to_all | solution.py:26
  87.4 0.1 broadcast_in_dim.14
  87.5 19.7 %all_to_all.16.chunks_ref = bf16[64,32,128]{2,1,0:T(8,128)(2,1)S(1)} all-to-all(bf16[64,32,128]{2,1,0:T(8,128)(2,1)S(1)} %broadcast_in_dim.14), channel_id=1, replica_groups=mesh['x'=4,'zh'=4,'y'=4,'zn'=4,'ze'=2,'c'=2] {'x','y','ze','c'}, dimensions={0} | all-to-all | bytes 1048576 | tf_op jit(solution)/shard_map/all_to_all | solution.py:26
  107.2 1.0 spread_out.1
  (1 shorter events, 0.0 us)
Async XLA Ops:
  0.6 18.2 %collective-permute-start = (bf16[4,64,128]{2,1,0:T(8,128)(2,1)}, bf16[4,64,128]{2,1,0:T(8,128)(2,1)S(1)}, u32[]{:S(2)}, u32[]{:S(2)}) collective-permute-start(bf16[4,64,128]{2,1,0:T(8,128)(2,1)} %bitcast.8), channel_id=1, source_target_pairs={{1,0},{2,1},{3,2},{4,3},{5,4},{6,5},{7,6},{8,7},{9,8},{10,9},{11,1... | collective-permute-start | bytes 196616 | tf_op jit(solution)/shard_map/ppermute | solution.py:22
  16.7 1.0 copy-start
  17.7 0.8 copy-start.3
  37.3 32.9 %copy-start.2 = (bf16[3,3,3,64,128]{4,3,2,1,0:T(8,128)(2,1)S(1)}, bf16[3,3,3,64,128]{4,3,2,1,0:T(8,128)(2,1)}, u32[]{:S(2)}) copy-start(bf16[3,3,3,64,128]{4,3,2,1,0:T(8,128)(2,1)} %weight_ref.1) | copy-start | bytes 1327108
  37.3 32.9 %copy-start.4 = (bf16[1,1,4,64,128]{4,3,2,1,0:T(8,128)(2,1)S(1)}, bf16[1,1,4,64,128]{4,3,2,1,0:T(8,128)(2,1)}, u32[]{:S(2)}) copy-start(bf16[1,1,4,64,128]{4,3,2,1,0:T(8,128)(2,1)} %param.5) | copy-start | bytes 196612
  38.0 32.1 %copy-start.1 = (bf16[1,2,8,64,128]{4,3,2,1,0:T(8,128)(2,1)S(1)}, bf16[1,2,8,64,128]{4,3,2,1,0:T(8,128)(2,1)}, u32[]{:S(2)}) copy-start(bf16[1,2,8,64,128]{4,3,2,1,0:T(8,128)(2,1)} %param.3) | copy-start | bytes 786436
  38.0 49.3 %all-to-all-start.1 = ((bf16[16,32,128]{2,1,0:T(8,128)(2,1)}), bf16[16,32,128]{2,1,0:T(8,128)(2,1)S(1)}, u32[]{:S(2)}, u32[]{:S(2)}) async-start(bf16[16,32,128]{2,1,0:T(8,128)(2,1)} %copies.1), calls=%async_computation.1 | async-start | bytes 262144 | tf_op jit(solution)/shard_map/all_to_all | solution.py:26
  61.7 8.4 %collective-permute-start.1 = (bf16[1,8,64,128]{3,2,1,0:T(8,128)(2,1)S(1)}, bf16[1,8,64,128]{3,2,1,0:T(8,128)(2,1)S(1)}, u32[]{:S(2)}, u32[]{:S(2)}) collective-permute-start(bf16[1,8,64,128]{3,2,1,0:T(8,128)(2,1)S(1)} %get-tuple-element.18), channel_id=1, source_target_pairs={{0,1},{1,2},{2,3},{3,4},{4,5},{5,6},{6,7},{7,8},{8,9},{9,10},{10,1... | collective-permute-start | bytes 393224 | tf_op jit(solution)/shard_map/ppermute | solution.py:22

commit v8 on v7

--- a/solution.py
+++ b/solution.py
@@ -10,7 +10,7 @@
 
 DP = ("x", "zh")
 SPACE = ("y", "zn", "ze", "c")
-SLAB = ("x", "y", "ze", "c")
+SLAB = ("x", "y", "ze")
 LINE = ("zh", "zn")
 SIZES = (4, 4, 4, 4, 2, 2)
 VMEM_BYTES = 16 << 20
@@ -115,18 +115,27 @@
     plane_ref[0] = local_ref[1]
 
 
-def joined_kernel(local_ref, later_ref, terms_ref, chunks_ref, scratch_ref):
+def joined_kernel(core_ref, local_ref, later_ref, terms_ref, kept_ref, sent_ref, scratch_ref):
     rows_out, pairs, cout = later_ref.shape
     cin = local_ref.shape[3] // 2
-    count, rows, _ = chunks_ref.shape
+    count, rows, _ = kept_ref.shape
     total = 27 * cin
-    step = total // count
+    step = total // (2 * count)
     later = with_next_pair(later_ref[...].reshape(rows_out * pairs, cout), pairs)
     store_kernel_terms(scratch_ref, 0, local_ref[1], later, rows_out, pairs, cin, cout)
     scratch_ref[9 * cin : total] = terms_ref[...]
     scratch_ref[total:] = jnp.zeros((scratch_ref.shape[0] - total, cout), jnp.float32)
+    first = core_ref[0] == 0
     for index in range(count):
-        chunks_ref[index] = scratch_ref[index * step : index * step + rows].astype(jnp.bfloat16)
+        start = 2 * index * step
+        even = scratch_ref[start : start + rows]
+        odd = scratch_ref[start + step : start + step + rows]
+        kept_ref[index] = jnp.where(first, even, odd)
+        sent_ref[index] = jnp.where(first, odd, even)
+
+
+def merge_kernel(kept_ref, other_ref, chunks_ref):
+    chunks_ref[...] = (kept_ref[...] + other_ref[...]).astype(jnp.bfloat16)
 
 
 def copies_kernel(chunks_ref, copies_ref):
@@ -162,10 +171,18 @@
                 grad_ref[plane, 2 * b + side] = rounded[b * pairs : (b + 1) * pairs]
 
 
-def spread_kernel(step, factor, chunks_ref, grad_ref):
-    for index in range(chunks_ref.shape[0]):
-        block = chunks_ref[index].astype(jnp.float32)[:step]
-        grad_ref[index * step : (index + 1) * step] = block * factor
+def spread_kernel(step, factor, core_ref, own_ref, other_ref, grad_ref):
+    first = core_ref[0] == 0
+    for index in range(own_ref.shape[0]):
+        own = own_ref[index].astype(jnp.float32)[:step] * factor
+        other = other_ref[index].astype(jnp.float32)[:step] * factor
+        start = 2 * index * step
+        grad_ref[start : start + step] = jnp.where(first, own, other)
+        grad_ref[start + step : start + 2 * step] = jnp.where(first, other, own)
+
+
+def swapped(value):
+    return lax.ppermute(value, "c", [(0, 1), (1, 0)])
 
 
 def shards(volume, weight, cotangent):
@@ -176,7 +193,7 @@
     total = 27 * cin
     cells = rows_out * pairs
     count = math.prod(lax.axis_size(axis) for axis in SLAB)
-    step = total // count
+    step = total // (2 * count)
     rows = -(-step // 16) * 16
     devices = math.prod(lax.axis_size(axis) for axis in DP + SPACE)
     factor = 1.0 / math.sqrt(devices * cells)
@@ -192,14 +209,28 @@
         compiler_params=pltpu.CompilerParams(vmem_limit_bytes=VMEM_BYTES),
         name="own",
     )(local, grads)
-    chunks = pl.pallas_call(
+    core = jnp.full((1,), lax.axis_index("c"), jnp.int32)
+    in_vmem = pl.BlockSpec(memory_space=pltpu.VMEM)
+    in_smem = pl.BlockSpec(memory_space=pltpu.SMEM)
+    kept, sent = pl.pallas_call(
         joined_kernel,
-        out_shape=jax.ShapeDtypeStruct((count, rows, cout), jnp.bfloat16),
+        in_specs=[in_smem, in_vmem, in_vmem, in_vmem],
+        out_shape=(
+            jax.ShapeDtypeStruct((count, rows, cout), jnp.float32),
+            jax.ShapeDtypeStruct((count, rows, cout), jnp.float32),
+        ),
         scratch_shapes=[pltpu.VMEM((total + 16, cout), jnp.float32)],
         cost_estimate=pl.CostEstimate(flops=60_000_000, bytes_accessed=1_000_000, transcendentals=0),
         compiler_params=pltpu.CompilerParams(vmem_limit_bytes=VMEM_BYTES),
         name="joined",
-    )(local, later, terms)
+    )(core, local, later, terms)
+    chunks = pl.pallas_call(
+        merge_kernel,
+        out_shape=jax.ShapeDtypeStruct((count, rows, cout), jnp.bfloat16),
+        cost_estimate=pl.CostEstimate(flops=500_000, bytes_accessed=1_000_000, transcendentals=0),
+        compiler_params=pltpu.CompilerParams(vmem_limit_bytes=VMEM_BYTES),
+        name="merge",
+    )(kept, swapped(sent))
     lines = math.prod(lax.axis_size(axis) for axis in LINE)
     copies = pl.pallas_call(
         copies_kernel,
@@ -229,10 +260,11 @@
     gathered = exchange(copies, SLAB)
     grad_weight = pl.pallas_call(
         functools.partial(spread_kernel, step, factor),
+        in_specs=[in_smem, in_vmem, in_vmem],
         out_shape=jax.ShapeDtypeStruct((total, cout), jnp.float32),
         compiler_params=pltpu.CompilerParams(vmem_limit_bytes=VMEM_BYTES),
         name="spread_out",
-    )(gathered)
+    )(core, gathered, swapped(gathered))
     return (output[None, None], grad_volume[None], grad_weight.reshape(weight.shape))
 
 

time: 109 us -> 109 us (level)
  starting transfers between devices: 42.3 us -> 55.6 us
  blocking collectives: 37.9 us -> 25.8 us
  waiting for transfers between devices: 21.7 us -> 20.4 us
    all_to_all x2, blocking collectives: 37.9 us -> 25.8 us  [exchange(): return lax.all_to_all(value, axes, 0, 0, tiled=True)]
    ppermute x0 -> x2, starting transfers between devices: none -> 11.7 us  [swapped(): return lax.ppermute(value, 'c', [(0, 1), (1, 0)])]
    all_to_all x1, waiting for transfers between devices: 15.8 us -> 9.83 us  [exchange(): return lax.all_to_all(value, axes, 0, 0, tiled=True)]
    ppermute x0 -> x2, waiting for transfers between devices: none -> 3.02 us  [swapped(): return lax.ppermute(value, 'c', [(0, 1), (1, 0)])]
    ppermute x2, waiting for transfers between devices: 5.9 us -> 7.57 us  [passed_along(): lax.ppermute(value, axes, [(source, source + steps) for source in range(f...]
    ppermute x2, starting transfers between devices: 18.6 us -> 19.8 us  [passed_along(): lax.ppermute(value, axes, [(source, source + steps) for source in range(f...]
  transfers between devices with their start and end apart: 3 -> 5, of which waited for: 2 -> 4; matrix products, arithmetic and copies ran while one was open for 0% -> 0% of each run, Pallas kernels for 2% -> 2%
where the time goes in v8:
time: 109 us; the launch traced here: 108 us
  starting transfers between devices  55.6 us (51%)
  blocking collectives  25.8 us (24%)
  waiting for transfers between devices  20.4 us (19%)
  Pallas kernels  3.84 us (4%)
  local copies, waits for them, and re-layouts  1.84 us (2%)
    all_to_all x2, blocking collectives, exchange(): return lax.all_to_all(value, axes, 0, 0, tiled=True)  25.8 us
    all_to_all x1, starting transfers between devices, exchange(): return lax.all_to_all(value, axes, 0, 0, tiled=True)  24.1 us
    ppermute x2, starting transfers between devices, passed_along(): lax.ppermute(value, axes, [(source, source + steps) for source in range(f...  19.8 us
    ppermute x2, starting transfers between devices, swapped(): return lax.ppermute(value, 'c', [(0, 1), (1, 0)])  11.7 us
    all_to_all x1, waiting for transfers between devices, exchange(): return lax.all_to_all(value, axes, 0, 0, tiled=True)  9.83 us
    ppermute x2, waiting for transfers between devices, passed_along(): lax.ppermute(value, axes, [(source, source + steps) for source in range(f...  7.57 us
    ppermute x2, waiting for transfers between devices, swapped(): return lax.ppermute(value, 'c', [(0, 1), (1, 0)])  3.02 us
  transfers between devices with their start and end apart: 5, of which 4 were waited for; matrix products, arithmetic and copies ran while one was open for 0% of the time, Pallas kernels for 2%

profile of v8, /device:TPU:1, one launch (start us, length us, event | category | flops | bytes accessed | tf_op | source)
XLA Modules:
  0.0 108.2 jit_solution(7318024591606731735)
XLA Ops:
  0.6 16.1 %collective-permute-start = (bf16[4,64,128]{2,1,0:T(8,128)(2,1)}, bf16[4,64,128]{2,1,0:T(8,128)(2,1)S(1)}, u32[]{:S(2)}, u32[]{:S(2)}) collective-permute-start(bf16[4,64,128]{2,1,0:T(8,128)(2,1)} %bitcast.9), channel_id=1, source_target_pairs={{1,0},{2,1},{3,2},{4,3},{5,4},{6,5},{7,6},{8,7},{9,8},{10,9},{11,1... | collective-permute-start | bytes 196616 | tf_op jit(solution)/shard_map/ppermute | solution.py:22
  16.7 0.0 copy-start
  16.7 0.9 copy-done
  17.7 0.0 copy-start.3
  17.7 0.8 copy-done.3
  18.5 0.3 own.1
  18.8 0.0 collective-permute-done.later_ref
  18.8 0.3 joined.1
  19.1 1.9 %collective-permute-start.1 = (f32[32,32,128]{2,1,0:T(8,128)S(1)}, f32[32,32,128]{2,1,0:T(8,128)S(1)}, u32[]{:S(2)}, u32[]{:S(2)}) collective-permute-start(f32[32,32,128]{2,1,0:T(8,128)S(1)} %get-tuple-element.19), channel_id=1, source_target_pairs={{0,1},{1,0},{2,3},{3,2},{4,5},{5,4},{6,7},{7,6},{8,9},{9,8},{10,11... | collective-permute-start | bytes 1572872 | tf_op jit(solution)/shard_map/ppermute | solution.py:185
  21.1 1.9 %collective-permute-done.1.other_ref = f32[32,32,128]{2,1,0:T(8,128)S(1)} collective-permute-done((f32[32,32,128]{2,1,0:T(8,128)S(1)}, f32[32,32,128]{2,1,0:T(8,128)S(1)}, u32[]{:S(2)}, u32[]{:S(2)}) %collective-permute-start.1) | collective-permute-done | bytes 524320 | tf_op jit(solution)/shard_map/ppermute | solution.py:185
  23.0 0.0 copy-start.2
  23.0 13.6 %all_to_all.15.chunks_ref = bf16[32,32,128]{2,1,0:T(8,128)(2,1)S(1)} all-to-all(bf16[32,32,128]{2,1,0:T(8,128)(2,1)S(1)} %merge.1), channel_id=1, replica_groups=mesh['x'=4,'zh'=4,'y'=4,'zn'=4,'ze'=2,'c'=2] {'x','y','ze'}, dimensions={0} | all-to-all | bytes 524288 | tf_op jit(solution)/shard_map/all_to_all | solution.py:26
  36.6 0.0 copy-start.1
  36.6 0.7 copies.1
  37.3 0.0 copy-start.4
  37.3 24.1 %all-to-all-start.1 = ((bf16[16,32,128]{2,1,0:T(8,128)(2,1)}), bf16[16,32,128]{2,1,0:T(8,128)(2,1)S(1)}, u32[]{:S(2)}, u32[]{:S(2)}) async-start(bf16[16,32,128]{2,1,0:T(8,128)(2,1)} %copies.1), calls=%async_computation.1 | async-start | bytes 262144 | tf_op jit(solution)/shard_map/all_to_all | solution.py:26
  61.4 3.7 %collective-permute-start.2 = (bf16[1,8,64,128]{3,2,1,0:T(8,128)(2,1)S(1)}, bf16[1,8,64,128]{3,2,1,0:T(8,128)(2,1)S(1)}, u32[]{:S(2)}, u32[]{:S(2)}) collective-permute-start(bf16[1,8,64,128]{3,2,1,0:T(8,128)(2,1)S(1)} %get-tuple-element.22), channel_id=1, source_target_pairs={{0,1},{1,2},{2,3},{3,4},{4,5},{5,6},{6,7},{7,8},{8,9},{9,10},{10,1... | collective-permute-start | bytes 393224 | tf_op jit(solution)/shard_map/ppermute | solution.py:22
  65.1 7.6 %collective-permute-done.2.rim_ref = bf16[1,8,64,128]{3,2,1,0:T(8,128)(2,1)S(1)} collective-permute-done((bf16[1,8,64,128]{3,2,1,0:T(8,128)(2,1)S(1)}, bf16[1,8,64,128]{3,2,1,0:T(8,128)(2,1)S(1)}, u32[]{:S(2)}, u32[]{:S(2)}) %collective-permute-start.2) | collective-permute-done | bytes 131104 | tf_op jit(solution)/shard_map/ppermute | solution.py:22
  72.7 0.0 copy-done.2
  72.7 0.0 copy-done.1
  72.7 0.0 copy-done.4
  72.7 1.5 %finish.1 = (bf16[4,64,128]{2,1,0:T(8,128)(2,1)}, bf16[2,8,64,128]{3,2,1,0:T(8,128)(2,1)}) custom-call(bf16[1,8,64,128]{3,2,1,0:T(8,128)(2,1)S(1)} %collective-permute-done.2.rim_ref, bf16[2,8,64,128]{3,2,1,0:T(8,128)(2,1)S(1)} %bitcast.8, bf16[4,64,128]{2,1,0:T(8,128)(2,1)S(1)} %bitcast.11, bf16[4,64,128]{2,1,0:T(8,128)(2,1)S(1)} %collective-permute-done.later_ref, ...), custom_call_target="tpu_custom_call" | custom-call | flops 400000000 | bytes 1500000 | tf_op jit(solution)/shard_map/finish/pallas_call | solution.py:248
  74.2 9.8 %all-to-all-done.1 = bf16[16,32,128]{2,1,0:T(8,128)(2,1)S(1)} async-done(((bf16[16,32,128]{2,1,0:T(8,128)(2,1)}), bf16[16,32,128]{2,1,0:T(8,128)(2,1)S(1)}, u32[]{:S(2)}, u32[]{:S(2)}) %all-to-all-start.1) | async-done | bytes 131104 | tf_op jit(solution)/shard_map/all_to_all | solution.py:26
  84.1 12.2 %all_to_all.16.own_ref = bf16[32,32,128]{2,1,0:T(8,128)(2,1)S(1)} all-to-all(bf16[32,32,128]{2,1,0:T(8,128)(2,1)S(1)} %broadcast_in_dim.18), channel_id=1, replica_groups=mesh['x'=4,'zh'=4,'y'=4,'zn'=4,'ze'=2,'c'=2] {'x','y','ze'}, dimensions={0} | all-to-all | bytes 524288 | tf_op jit(solution)/shard_map/all_to_all | solution.py:26
  96.3 9.8 %collective-permute-start.3 = (bf16[32,32,128]{2,1,0:T(8,128)(2,1)S(1)}, bf16[32,32,128]{2,1,0:T(8,128)(2,1)S(1)}, u32[]{:S(2)}, u32[]{:S(2)}) collective-permute-start(bf16[32,32,128]{2,1,0:T(8,128)(2,1)S(1)} %all_to_all.16.own_ref), channel_id=1, source_target_pairs={{0,1},{1,0},{2,3},{3,2},{4,5},{5,4},{6,7},{7,6},{8,9},{9,8},{10,11... | collective-permute-start | bytes 786440 | tf_op jit(solution)/shard_map/ppermute | solution.py:185
  106.1 1.1 %collective-permute-done.3.other_ref = bf16[32,32,128]{2,1,0:T(8,128)(2,1)S(1)} collective-permute-done((bf16[32,32,128]{2,1,0:T(8,128)(2,1)S(1)}, bf16[32,32,128]{2,1,0:T(8,128)(2,1)S(1)}, u32[]{:S(2)}, u32[]{:S(2)}) %collective-permute-start.3) | collective-permute-done | bytes 262176 | tf_op jit(solution)/shard_map/ppermute | solution.py:185
  107.2 1.0 spread_out.1
  (3 shorter events, 0.1 us)
Async XLA Ops:
  0.6 18.2 %collective-permute-start = (bf16[4,64,128]{2,1,0:T(8,128)(2,1)}, bf16[4,64,128]{2,1,0:T(8,128)(2,1)S(1)}, u32[]{:S(2)}, u32[]{:S(2)}) collective-permute-start(bf16[4,64,128]{2,1,0:T(8,128)(2,1)} %bitcast.9), channel_id=1, source_target_pairs={{1,0},{2,1},{3,2},{4,3},{5,4},{6,5},{7,6},{8,7},{9,8},{10,9},{11,1... | collective-permute-start | bytes 196616 | tf_op jit(solution)/shard_map/ppermute | solution.py:22
  16.7 1.0 copy-start
  17.7 0.8 copy-start.3
  19.1 3.8 %collective-permute-start.1 = (f32[32,32,128]{2,1,0:T(8,128)S(1)}, f32[32,32,128]{2,1,0:T(8,128)S(1)}, u32[]{:S(2)}, u32[]{:S(2)}) collective-permute-start(f32[32,32,128]{2,1,0:T(8,128)S(1)} %get-tuple-element.19), channel_id=1, source_target_pairs={{0,1},{1,0},{2,3},{3,2},{4,5},{5,4},{6,7},{7,6},{8,9},{9,8},{10,11... | collective-permute-start | bytes 1572872 | tf_op jit(solution)/shard_map/ppermute | solution.py:185
  23.0 49.7 %copy-start.2 = (bf16[3,3,3,64,128]{4,3,2,1,0:T(8,128)(2,1)S(1)}, bf16[3,3,3,64,128]{4,3,2,1,0:T(8,128)(2,1)}, u32[]{:S(2)}) copy-start(bf16[3,3,3,64,128]{4,3,2,1,0:T(8,128)(2,1)} %weight_ref.1) | copy-start | bytes 1327108
  36.6 36.2 %copy-start.1 = (bf16[1,2,8,64,128]{4,3,2,1,0:T(8,128)(2,1)S(1)}, bf16[1,2,8,64,128]{4,3,2,1,0:T(8,128)(2,1)}, u32[]{:S(2)}) copy-start(bf16[1,2,8,64,128]{4,3,2,1,0:T(8,128)(2,1)} %param.3) | copy-start | bytes 786436
  37.3 35.5 %copy-start.4 = (bf16[1,1,4,64,128]{4,3,2,1,0:T(8,128)(2,1)S(1)}, bf16[1,1,4,64,128]{4,3,2,1,0:T(8,128)(2,1)}, u32[]{:S(2)}) copy-start(bf16[1,1,4,64,128]{4,3,2,1,0:T(8,128)(2,1)} %param.5) | copy-start | bytes 196612
  37.3 46.8 %all-to-all-start.1 = ((bf16[16,32,128]{2,1,0:T(8,128)(2,1)}), bf16[16,32,128]{2,1,0:T(8,128)(2,1)S(1)}, u32[]{:S(2)}, u32[]{:S(2)}) async-start(bf16[16,32,128]{2,1,0:T(8,128)(2,1)} %copies.1), calls=%async_computation.1 | async-start | bytes 262144 | tf_op jit(solution)/shard_map/all_to_all | solution.py:26
  61.4 11.3 %collective-permute-start.2 = (bf16[1,8,64,128]{3,2,1,0:T(8,128)(2,1)S(1)}, bf16[1,8,64,128]{3,2,1,0:T(8,128)(2,1)S(1)}, u32[]{:S(2)}, u32[]{:S(2)}) collective-permute-start(bf16[1,8,64,128]{3,2,1,0:T(8,128)(2,1)S(1)} %get-tuple-element.22), channel_id=1, source_target_pairs={{0,1},{1,2},{2,3},{3,4},{4,5},{5,6},{6,7},{7,8},{8,9},{9,10},{10,1... | collective-permute-start | bytes 393224 | tf_op jit(solution)/shard_map/ppermute | solution.py:22
  96.3 10.9 %collective-permute-start.3 = (bf16[32,32,128]{2,1,0:T(8,128)(2,1)S(1)}, bf16[32,32,128]{2,1,0:T(8,128)(2,1)S(1)}, u32[]{:S(2)}, u32[]{:S(2)}) collective-permute-start(bf16[32,32,128]{2,1,0:T(8,128)(2,1)S(1)} %all_to_all.16.own_ref), channel_id=1, source_target_pairs={{0,1},{1,0},{2,3},{3,2},{4,5},{5,4},{6,7},{7,6},{8,9},{9,8},{10,11... | collective-permute-start | bytes 786440 | tf_op jit(solution)/shard_map/ppermute | solution.py:185

commit v9 on v8

--- a/solution.py
+++ b/solution.py
@@ -9,10 +9,10 @@
 from jax.sharding import PartitionSpec as P
 
 DP = ("x", "zh")
-SPACE = ("y", "zn", "ze", "c")
-SLAB = ("x", "y", "ze")
-LINE = ("zh", "zn")
-SIZES = (4, 4, 4, 4, 2, 2)
+SPACE = ("y", "zp", "zq", "ze", "c")
+SLAB = ("x", "y", "zq", "ze")
+LINE = ("zh", "zp")
+SIZES = (4, 4, 4, 2, 2, 2, 2)
 VMEM_BYTES = 16 << 20
 
 
@@ -120,7 +120,7 @@
     cin = local_ref.shape[3] // 2
     count, rows, _ = kept_ref.shape
     total = 27 * cin
-    step = total // (2 * count)
+    step = -(-total // (2 * count))
     later = with_next_pair(later_ref[...].reshape(rows_out * pairs, cout), pairs)
     store_kernel_terms(scratch_ref, 0, local_ref[1], later, rows_out, pairs, cin, cout)
     scratch_ref[9 * cin : total] = terms_ref[...]
@@ -174,11 +174,15 @@
 def spread_kernel(step, factor, core_ref, own_ref, other_ref, grad_ref):
     first = core_ref[0] == 0
     for index in range(own_ref.shape[0]):
-        own = own_ref[index].astype(jnp.float32)[:step] * factor
-        other = other_ref[index].astype(jnp.float32)[:step] * factor
-        start = 2 * index * step
-        grad_ref[start : start + step] = jnp.where(first, own, other)
-        grad_ref[start + step : start + 2 * step] = jnp.where(first, other, own)
+        own = own_ref[index].astype(jnp.float32) * factor
+        other = other_ref[index].astype(jnp.float32) * factor
+        for start, block in (
+            (2 * index * step, jnp.where(first, own, other)),
+            ((2 * index + 1) * step, jnp.where(first, other, own)),
+        ):
+            valid = min(step, grad_ref.shape[0] - start)
+            if valid > 0:
+                grad_ref[start : start + valid] = block[:valid]
 
 
 def swapped(value):
@@ -193,7 +197,7 @@
     total = 27 * cin
     cells = rows_out * pairs
     count = math.prod(lax.axis_size(axis) for axis in SLAB)
-    step = total // (2 * count)
+    step = -(-total // (2 * count))
     rows = -(-step // 16) * 16
     devices = math.prod(lax.axis_size(axis) for axis in DP + SPACE)
     factor = 1.0 / math.sqrt(devices * cells)
@@ -219,7 +223,7 @@
             jax.ShapeDtypeStruct((count, rows, cout), jnp.float32),
             jax.ShapeDtypeStruct((count, rows, cout), jnp.float32),
         ),
-        scratch_shapes=[pltpu.VMEM((total + 16, cout), jnp.float32)],
+        scratch_shapes=[pltpu.VMEM((2 * count * step + 16, cout), jnp.float32)],
         cost_estimate=pl.CostEstimate(flops=60_000_000, bytes_accessed=1_000_000, transcendentals=0),
         compiler_params=pltpu.CompilerParams(vmem_limit_bytes=VMEM_BYTES),
         name="joined",

time: 109 us -> 111 us (1.018)
  blocking collectives: 25.8 us -> 32.4 us
  starting transfers between devices: 55.6 us -> 53.2 us
  waiting for transfers between devices: 20.4 us -> 18.7 us
    all_to_all x2, blocking collectives: 25.8 us -> 32.4 us  [exchange(): return lax.all_to_all(value, axes, 0, 0, tiled=True)]
    ppermute x2, waiting for transfers between devices: 7.57 us -> 2.73 us  [passed_along(): lax.ppermute(value, axes, [(source, source + steps) for source in range(f...]
    ppermute x2, starting transfers between devices: 11.7 us -> 7.58 us  [swapped(): return lax.ppermute(value, 'c', [(0, 1), (1, 0)])]
    all_to_all x1, waiting for transfers between devices: 9.83 us -> 12.9 us  [exchange(): return lax.all_to_all(value, axes, 0, 0, tiled=True)]
where the time goes in v9:
time: 111 us
  starting transfers between devices  53.2 us (48%)
  blocking collectives  32.4 us (29%)
  waiting for transfers between devices  18.7 us (17%)
  Pallas kernels  3.83 us (3%)
  local copies, waits for them, and re-layouts  1.83 us (2%)
    all_to_all x2, blocking collectives, exchange(): return lax.all_to_all(value, axes, 0, 0, tiled=True)  32.4 us
    all_to_all x1, starting transfers between devices, exchange(): return lax.all_to_all(value, axes, 0, 0, tiled=True)  25.2 us
    ppermute x2, starting transfers between devices, passed_along(): lax.ppermute(value, axes, [(source, source + steps) for source in range(f...  20.5 us
    all_to_all x1, waiting for transfers between devices, exchange(): return lax.all_to_all(value, axes, 0, 0, tiled=True)  12.9 us
    ppermute x2, starting transfers between devices, swapped(): return lax.ppermute(value, 'c', [(0, 1), (1, 0)])  7.58 us
    ppermute x2, waiting for transfers between devices, swapped(): return lax.ppermute(value, 'c', [(0, 1), (1, 0)])  3.02 us
    ppermute x2, waiting for transfers between devices, passed_along(): lax.ppermute(value, axes, [(source, source + steps) for source in range(f...  2.73 us
  transfers between devices with their start and end apart: 5, of which 4 were waited for; matrix products, arithmetic and copies ran while one was open for 0% of the time, Pallas kernels for 2%

profile of v9, /device:TPU:1, one launch (start us, length us, event | category | flops | bytes accessed | tf_op | source)
XLA Modules:
  0.0 110.7 jit_solution(12005163988192935593)
XLA Ops:
  0.6 16.1 %collective-permute-start = (bf16[4,64,128]{2,1,0:T(8,128)(2,1)}, bf16[4,64,128]{2,1,0:T(8,128)(2,1)S(1)}, u32[]{:S(2)}, u32[]{:S(2)}) collective-permute-start(bf16[4,64,128]{2,1,0:T(8,128)(2,1)} %bitcast.9), channel_id=1, source_target_pairs={{1,0},{2,1},{3,2},{4,3},{5,4},{6,5},{7,6},{8,7},{9,8},{10,9},{11,1... | collective-permute-start | bytes 196616 | tf_op jit(solution)/shard_map/ppermute | solution.py:22
  16.7 0.0 copy-start
  16.7 0.9 copy-done
  17.7 0.0 copy-start.3
  17.7 0.8 copy-done.3
  18.5 0.3 own.1
  18.8 0.0 collective-permute-done.later_ref
  18.8 0.3 joined.1
  19.1 1.9 %collective-permute-start.1 = (f32[64,16,128]{2,1,0:T(8,128)S(1)}, f32[64,16,128]{2,1,0:T(8,128)S(1)}, u32[]{:S(2)}, u32[]{:S(2)}) collective-permute-start(f32[64,16,128]{2,1,0:T(8,128)S(1)} %get-tuple-element.19), channel_id=1, source_target_pairs={{0,1},{1,0},{2,3},{3,2},{4,5},{5,4},{6,7},{7,6},{8,9},{9,8},{10,11... | collective-permute-start | bytes 1572872 | tf_op jit(solution)/shard_map/ppermute | solution.py:189
  21.1 1.9 %collective-permute-done.1.other_ref = f32[64,16,128]{2,1,0:T(8,128)S(1)} collective-permute-done((f32[64,16,128]{2,1,0:T(8,128)S(1)}, f32[64,16,128]{2,1,0:T(8,128)S(1)}, u32[]{:S(2)}, u32[]{:S(2)}) %collective-permute-start.1) | collective-permute-done | bytes 524320 | tf_op jit(solution)/shard_map/ppermute | solution.py:189
  23.0 0.0 copy-start.2
  23.0 16.6 %all_to_all.15.chunks_ref = bf16[64,16,128]{2,1,0:T(8,128)(2,1)S(1)} all-to-all(bf16[64,16,128]{2,1,0:T(8,128)(2,1)S(1)} %merge.1), channel_id=1, replica_groups=mesh['x'=4,'zh'=4,'y'=4,'zp'=2,'zq'=2,'ze'=2,'c'=2] {'x','y','zq','ze'}, dimensions={0} | all-to-all | bytes 524288 | tf_op jit(solution)/shard_map/all_to_all | solution.py:26
  39.6 0.0 copy-start.1
  39.6 0.7 copies.1
  40.3 0.0 copy-start.4
  40.3 25.2 %all-to-all-start.1 = ((bf16[8,16,128]{2,1,0:T(8,128)(2,1)}), bf16[8,16,128]{2,1,0:T(8,128)(2,1)S(1)}, u32[]{:S(2)}, u32[]{:S(2)}) async-start(bf16[8,16,128]{2,1,0:T(8,128)(2,1)} %copies.1), calls=%async_computation.1 | async-start | bytes 65536 | tf_op jit(solution)/shard_map/all_to_all | solution.py:26
  65.5 4.4 %collective-permute-start.2 = (bf16[1,8,64,128]{3,2,1,0:T(8,128)(2,1)S(1)}, bf16[1,8,64,128]{3,2,1,0:T(8,128)(2,1)S(1)}, u32[]{:S(2)}, u32[]{:S(2)}) collective-permute-start(bf16[1,8,64,128]{3,2,1,0:T(8,128)(2,1)S(1)} %get-tuple-element.22), channel_id=1, source_target_pairs={{0,1},{1,2},{2,3},{3,4},{4,5},{5,6},{6,7},{7,8},{8,9},{9,10},{10,1... | collective-permute-start | bytes 393224 | tf_op jit(solution)/shard_map/ppermute | solution.py:22
  69.9 2.7 %collective-permute-done.2.rim_ref = bf16[1,8,64,128]{3,2,1,0:T(8,128)(2,1)S(1)} collective-permute-done((bf16[1,8,64,128]{3,2,1,0:T(8,128)(2,1)S(1)}, bf16[1,8,64,128]{3,2,1,0:T(8,128)(2,1)S(1)}, u32[]{:S(2)}, u32[]{:S(2)}) %collective-permute-start.2) | collective-permute-done | bytes 131104 | tf_op jit(solution)/shard_map/ppermute | solution.py:22
  72.6 0.0 copy-done.2
  72.6 0.0 copy-done.1
  72.6 0.0 copy-done.4
  72.6 1.5 %finish.1 = (bf16[4,64,128]{2,1,0:T(8,128)(2,1)}, bf16[2,8,64,128]{3,2,1,0:T(8,128)(2,1)}) custom-call(bf16[1,8,64,128]{3,2,1,0:T(8,128)(2,1)S(1)} %collective-permute-done.2.rim_ref, bf16[2,8,64,128]{3,2,1,0:T(8,128)(2,1)S(1)} %bitcast.8, bf16[4,64,128]{2,1,0:T(8,128)(2,1)S(1)} %bitcast.11, bf16[4,64,128]{2,1,0:T(8,128)(2,1)S(1)} %collective-permute-done.later_ref, ...), custom_call_target="tpu_custom_call" | custom-call | flops 400000000 | bytes 1500000 | tf_op jit(solution)/shard_map/finish/pallas_call | solution.py:252
  74.1 12.9 %all-to-all-done.1 = bf16[8,16,128]{2,1,0:T(8,128)(2,1)S(1)} async-done(((bf16[8,16,128]{2,1,0:T(8,128)(2,1)}), bf16[8,16,128]{2,1,0:T(8,128)(2,1)S(1)}, u32[]{:S(2)}, u32[]{:S(2)}) %all-to-all-start.1) | async-done | bytes 32800 | tf_op jit(solution)/shard_map/all_to_all | solution.py:26
  87.0 15.8 %all_to_all.16.own_ref = bf16[64,16,128]{2,1,0:T(8,128)(2,1)S(1)} all-to-all(bf16[64,16,128]{2,1,0:T(8,128)(2,1)S(1)} %broadcast_in_dim.18), channel_id=1, replica_groups=mesh['x'=4,'zh'=4,'y'=4,'zp'=2,'zq'=2,'ze'=2,'c'=2] {'x','y','zq','ze'}, dimensions={0} | all-to-all | bytes 524288 | tf_op jit(solution)/shard_map/all_to_all | solution.py:26
  102.8 5.7 %collective-permute-start.3 = (bf16[64,16,128]{2,1,0:T(8,128)(2,1)S(1)}, bf16[64,16,128]{2,1,0:T(8,128)(2,1)S(1)}, u32[]{:S(2)}, u32[]{:S(2)}) collective-permute-start(bf16[64,16,128]{2,1,0:T(8,128)(2,1)S(1)} %all_to_all.16.own_ref), channel_id=1, source_target_pairs={{0,1},{1,0},{2,3},{3,2},{4,5},{5,4},{6,7},{7,6},{8,9},{9,8},{10,11... | collective-permute-start | bytes 786440 | tf_op jit(solution)/shard_map/ppermute | solution.py:189
  108.5 1.1 %collective-permute-done.3.other_ref = bf16[64,16,128]{2,1,0:T(8,128)(2,1)S(1)} collective-permute-done((bf16[64,16,128]{2,1,0:T(8,128)(2,1)S(1)}, bf16[64,16,128]{2,1,0:T(8,128)(2,1)S(1)}, u32[]{:S(2)}, u32[]{:S(2)}) %collective-permute-start.3) | collective-permute-done | bytes 262176 | tf_op jit(solution)/shard_map/ppermute | solution.py:189
  109.6 1.0 spread_out.1
  (3 shorter events, 0.1 us)
Async XLA Ops:
  0.6 18.2 %collective-permute-start = (bf16[4,64,128]{2,1,0:T(8,128)(2,1)}, bf16[4,64,128]{2,1,0:T(8,128)(2,1)S(1)}, u32[]{:S(2)}, u32[]{:S(2)}) collective-permute-start(bf16[4,64,128]{2,1,0:T(8,128)(2,1)} %bitcast.9), channel_id=1, source_target_pairs={{1,0},{2,1},{3,2},{4,3},{5,4},{6,5},{7,6},{8,7},{9,8},{10,9},{11,1... | collective-permute-start | bytes 196616 | tf_op jit(solution)/shard_map/ppermute | solution.py:22
  16.7 1.0 copy-start
  17.7 0.8 copy-start.3
  19.1 3.8 %collective-permute-start.1 = (f32[64,16,128]{2,1,0:T(8,128)S(1)}, f32[64,16,128]{2,1,0:T(8,128)S(1)}, u32[]{:S(2)}, u32[]{:S(2)}) collective-permute-start(f32[64,16,128]{2,1,0:T(8,128)S(1)} %get-tuple-element.19), channel_id=1, source_target_pairs={{0,1},{1,0},{2,3},{3,2},{4,5},{5,4},{6,7},{7,6},{8,9},{9,8},{10,11... | collective-permute-start | bytes 1572872 | tf_op jit(solution)/shard_map/ppermute | solution.py:189
  23.0 49.6 %copy-start.2 = (bf16[3,3,3,64,128]{4,3,2,1,0:T(8,128)(2,1)S(1)}, bf16[3,3,3,64,128]{4,3,2,1,0:T(8,128)(2,1)}, u32[]{:S(2)}) copy-start(bf16[3,3,3,64,128]{4,3,2,1,0:T(8,128)(2,1)} %weight_ref.1) | copy-start | bytes 1327108
  39.6 33.0 %copy-start.1 = (bf16[1,2,8,64,128]{4,3,2,1,0:T(8,128)(2,1)S(1)}, bf16[1,2,8,64,128]{4,3,2,1,0:T(8,128)(2,1)}, u32[]{:S(2)}) copy-start(bf16[1,2,8,64,128]{4,3,2,1,0:T(8,128)(2,1)} %param.3) | copy-start | bytes 786436
  40.3 32.3 %copy-start.4 = (bf16[1,1,4,64,128]{4,3,2,1,0:T(8,128)(2,1)S(1)}, bf16[1,1,4,64,128]{4,3,2,1,0:T(8,128)(2,1)}, u32[]{:S(2)}) copy-start(bf16[1,1,4,64,128]{4,3,2,1,0:T(8,128)(2,1)} %param.5) | copy-start | bytes 196612
  40.3 46.7 %all-to-all-start.1 = ((bf16[8,16,128]{2,1,0:T(8,128)(2,1)}), bf16[8,16,128]{2,1,0:T(8,128)(2,1)S(1)}, u32[]{:S(2)}, u32[]{:S(2)}) async-start(bf16[8,16,128]{2,1,0:T(8,128)(2,1)} %copies.1), calls=%async_computation.1 | async-start | bytes 65536 | tf_op jit(solution)/shard_map/all_to_all | solution.py:26
  65.5 7.1 %collective-permute-start.2 = (bf16[1,8,64,128]{3,2,1,0:T(8,128)(2,1)S(1)}, bf16[1,8,64,128]{3,2,1,0:T(8,128)(2,1)S(1)}, u32[]{:S(2)}, u32[]{:S(2)}) collective-permute-start(bf16[1,8,64,128]{3,2,1,0:T(8,128)(2,1)S(1)} %get-tuple-element.22), channel_id=1, source_target_pairs={{0,1},{1,2},{2,3},{3,4},{4,5},{5,6},{6,7},{7,8},{8,9},{9,10},{10,1... | collective-permute-start | bytes 393224 | tf_op jit(solution)/shard_map/ppermute | solution.py:22
  102.8 6.8 %collective-permute-start.3 = (bf16[64,16,128]{2,1,0:T(8,128)(2,1)S(1)}, bf16[64,16,128]{2,1,0:T(8,128)(2,1)S(1)}, u32[]{:S(2)}, u32[]{:S(2)}) collective-permute-start(bf16[64,16,128]{2,1,0:T(8,128)(2,1)S(1)} %all_to_all.16.own_ref), channel_id=1, source_target_pairs={{0,1},{1,0},{2,3},{3,2},{4,5},{5,4},{6,7},{7,6},{8,9},{9,8},{10,11... | collective-permute-start | bytes 786440 | tf_op jit(solution)/shard_map/ppermute | solution.py:189

commit v10 on v7

--- a/solution.py
+++ b/solution.py
@@ -22,6 +22,10 @@
     return lax.ppermute(value, axes, [(source, source + steps) for source in range(first, last)])
 
 
+def sent(value, pairs):
+    return lax.ppermute(value, SPACE, pairs)
+
+
 def exchange(value, axes):
     return lax.all_to_all(value, axes, 0, 0, tiled=True)
 
@@ -70,19 +74,22 @@
     )
 
 
-def store_kernel_terms(terms_ref, base, plane, grads, rows_out, pairs, cin, cout):
+def kernel_terms(plane, grads, rows_out, pairs):
     even, odd = plane_rows(plane, rows_out)
     kept = (rows_out - 1) * pairs
-    products = (
+    return (
         kernel_dot(odd[:kept], grads[pairs:]),
         kernel_dot(even, grads),
         kernel_dot(odd, grads),
     )
+
+
+def store_kernel_terms(terms_ref, base, products, cin, cout):
     for height_tap in range(3):
         product = products[height_tap]
         start = base + height_tap * 3 * cin
-        terms_ref[start : start + cin] = product[cin:, cout:].astype(terms_ref.dtype)
-        terms_ref[start + cin : start + 3 * cin] = product[:, :cout].astype(terms_ref.dtype)
+        terms_ref[start : start + cin] = product[cin:, cout:]
+        terms_ref[start + cin : start + 3 * cin] = product[:, :cout]
 
 
 def forward_terms(plane, weight, depth_tap, rows_out, pairs):
@@ -109,20 +116,25 @@
     cin = local_ref.shape[3] // 2
     grads = with_next_pair(grads_ref[...].reshape(rows_out * pairs, cout), pairs)
     for plane in range(2):
-        store_kernel_terms(
-            terms_ref, plane * 9 * cin, local_ref[plane], grads, rows_out, pairs, cin, cout
-        )
+        products = kernel_terms(local_ref[plane], grads, rows_out, pairs)
+        store_kernel_terms(terms_ref, plane * 9 * cin, products, cin, cout)
     plane_ref[0] = local_ref[1]
 
 
-def joined_kernel(local_ref, later_ref, terms_ref, chunks_ref, scratch_ref):
+def joined_kernel(
+    local_ref, later_ref, far_plane_ref, far_grads_ref, terms_ref, chunks_ref, scratch_ref
+):
     rows_out, pairs, cout = later_ref.shape
     cin = local_ref.shape[3] // 2
     count, rows, _ = chunks_ref.shape
     total = 27 * cin
     step = total // count
     later = with_next_pair(later_ref[...].reshape(rows_out * pairs, cout), pairs)
-    store_kernel_terms(scratch_ref, 0, local_ref[1], later, rows_out, pairs, cin, cout)
+    far = with_next_pair(far_grads_ref[...].reshape(rows_out * pairs, cout), pairs)
+    near_terms = kernel_terms(local_ref[1], later, rows_out, pairs)
+    far_terms = kernel_terms(far_plane_ref[0], far, rows_out, pairs)
+    products = [near + other for near, other in zip(near_terms, far_terms)]
+    store_kernel_terms(scratch_ref, 0, products, cin, cout)
     scratch_ref[9 * cin : total] = terms_ref[...]
     scratch_ref[total:] = jnp.zeros((scratch_ref.shape[0] - total, cout), jnp.float32)
     for index in range(count):
@@ -136,12 +148,12 @@
 
 
 def finish_kernel(
-    rim_ref, local_ref, grads_ref, later_ref, weight_ref, output_ref, grad_ref
+    rim_ref, local_ref, grads_ref, later_ref, after_ref, weight_ref, output_ref, grad_ref
 ):
     rows_out, pairs, cout = later_ref.shape
     cells = rows_out * pairs
     grads = with_next_pair(grads_ref[...].reshape(cells, cout), pairs)
-    later = with_next_pair(later_ref[...].reshape(cells, cout), pairs)
+    later = with_next_pair((later_ref[...] + after_ref[...]).reshape(cells, cout), pairs)
     total = (
         forward_terms(rim_ref[0], weight_ref, 0, rows_out, pairs)
         + forward_terms(local_ref[0], weight_ref, 1, rows_out, pairs)
@@ -181,7 +193,12 @@
     devices = math.prod(lax.axis_size(axis) for axis in DP + SPACE)
     factor = 1.0 / math.sqrt(devices * cells)
 
-    later = passed_along(grads, SPACE, -1)
+    places = math.prod(lax.axis_size(axis) for axis in SPACE)
+    run = places // lax.axis_size("y")
+    bends = range(run, places, run)
+    far_grads = sent(grads, [(place, place + run // 2) for place in bends])
+    far_plane = sent(local[1:2], [(place - 1, place + run // 2) for place in bends])
+    later = sent(grads, [(place, place - 1) for place in range(1, places) if place % run])
     terms, plane = pl.pallas_call(
         own_kernel,
         out_shape=(
@@ -199,7 +216,7 @@
         cost_estimate=pl.CostEstimate(flops=60_000_000, bytes_accessed=1_000_000, transcendentals=0),
         compiler_params=pltpu.CompilerParams(vmem_limit_bytes=VMEM_BYTES),
         name="joined",
-    )(local, later, terms)
+    )(local, later, far_plane, far_grads, terms)
     lines = math.prod(lax.axis_size(axis) for axis in LINE)
     copies = pl.pallas_call(
         copies_kernel,
@@ -212,6 +229,7 @@
         (copies, plane, later, local, grads)
     )
     rim = passed_along(plane, SPACE, 1)
+    after = sent(grads, [(place, place - 1) for place in bends])
     piece = jnp.sum(exchange(copies, LINE).astype(jnp.float32), axis=0)
 
     output, grad_volume = pl.pallas_call(
@@ -223,7 +241,7 @@
         cost_estimate=pl.CostEstimate(flops=400_000_000, bytes_accessed=1_500_000, transcendentals=0),
         compiler_params=pltpu.CompilerParams(vmem_limit_bytes=VMEM_BYTES),
         name="finish",
-    )(rim, local, grads, later, weight)
+    )(rim, local, grads, later, after, weight)
     piece, output, grad_volume = lax.optimization_barrier((piece, output, grad_volume))
     copies = jnp.broadcast_to(piece.astype(jnp.bfloat16)[None], (count, rows, cout))
     gathered = exchange(copies, SLAB)

time: 109 us -> 108 us (level)
  starting transfers between devices: 42.3 us -> 44.1 us
  blocking collectives: 37.9 us -> 36.5 us
    ppermute x0 -> x4, starting transfers between devices: none -> 18.1 us  [sent(): return lax.ppermute(value, SPACE, pairs)]
    ppermute x2 -> x1, starting transfers between devices: 18.6 us -> 2.53 us  [passed_along(): lax.ppermute(value, axes, [(source, source + steps) for source in range(f...]
    all_to_all x2, blocking collectives: 37.9 us -> 36.5 us  [exchange(): return lax.all_to_all(value, axes, 0, 0, tiled=True)]
    ppermute x2 -> x1, waiting for transfers between devices: 5.9 us -> 5.21 us  [passed_along(): lax.ppermute(value, axes, [(source, source + steps) for source in range(f...]
  transfers between devices with their start and end apart: 3 -> 6, of which waited for: 2 -> 2; matrix products, arithmetic and copies ran while one was open for 0% -> 0% of each run, Pallas kernels for 2% -> 2%
where the time goes in v10:
time: 108 us
  starting transfers between devices  44.1 us (41%)
  blocking collectives  36.5 us (34%)
  waiting for transfers between devices  21 us (19%)
  Pallas kernels  3.83 us (4%)
  local copies, waits for them, and re-layouts  1.9 us (2%)
    all_to_all x2, blocking collectives, exchange(): return lax.all_to_all(value, axes, 0, 0, tiled=True)  36.5 us
    all_to_all x1, starting transfers between devices, exchange(): return lax.all_to_all(value, axes, 0, 0, tiled=True)  23.5 us
    ppermute x4, starting transfers between devices, sent(): return lax.ppermute(value, SPACE, pairs)  18.1 us
    all_to_all x1, waiting for transfers between devices, exchange(): return lax.all_to_all(value, axes, 0, 0, tiled=True)  15.8 us
    ppermute x1, waiting for transfers between devices, passed_along(): lax.ppermute(value, axes, [(source, source + steps) for source in range(f...  5.21 us
    ppermute x1, starting transfers between devices, passed_along(): lax.ppermute(value, axes, [(source, source + steps) for source in range(f...  2.53 us
  transfers between devices with their start and end apart: 6, of which 2 were waited for; matrix products, arithmetic and copies ran while one was open for 0% of the time, Pallas kernels for 2%

profile of v10, /device:TPU:1, one launch (start us, length us, event | category | flops | bytes accessed | tf_op | source)
XLA Modules:
  0.0 108.0 jit_solution(6088587963542250456)
XLA Ops:
  0.6 0.0 copy-start
  0.6 1.0 slice_bitcast_fusion
  1.6 0.7 collective-permute-start.1
  2.3 0.7 collective-permute-start.2
  3.0 16.1 %collective-permute-start = (bf16[4,64,128]{2,1,0:T(8,128)(2,1)}, bf16[4,64,128]{2,1,0:T(8,128)(2,1)S(1)}, u32[]{:S(2)}, u32[]{:S(2)}) collective-permute-start(bf16[4,64,128]{2,1,0:T(8,128)(2,1)} %bitcast.11), channel_id=1, source_target_pairs={{1,0},{2,1},{3,2},{4,3},{5,4},{6,5},{7,6},{8,7},{9,8},{10,9},{11,1... | collective-permute-start | bytes 196616 | tf_op jit(solution)/shard_map/ppermute | solution.py:26
  19.0 0.0 copy-done
  19.1 0.0 copy-start.2
  19.1 0.8 copy-done.2
  19.9 0.3 own.1
  20.2 0.0 collective-permute-done.2.far_grads_ref
  20.2 0.0 collective-permute-done.later_ref
  20.2 0.0 collective-permute-done.1.far_plane_ref
  20.2 0.3 joined.1
  20.6 16.7 %all_to_all.15.chunks_ref = bf16[64,32,128]{2,1,0:T(8,128)(2,1)S(1)} all-to-all(bf16[64,32,128]{2,1,0:T(8,128)(2,1)S(1)} %joined.1), channel_id=1, replica_groups=mesh['x'=4,'zh'=4,'y'=4,'zn'=4,'ze'=2,'c'=2] {'x','y','ze','c'}, dimensions={0} | all-to-all | bytes 1048576 | tf_op jit(solution)/shard_map/all_to_all | solution.py:30
  37.3 0.0 copy-start.1
  37.3 0.7 copies.1
  38.1 0.0 copy-start.3
  38.1 23.5 %all-to-all-start.1 = ((bf16[16,32,128]{2,1,0:T(8,128)(2,1)}), bf16[16,32,128]{2,1,0:T(8,128)(2,1)S(1)}, u32[]{:S(2)}, u32[]{:S(2)}) async-start(bf16[16,32,128]{2,1,0:T(8,128)(2,1)} %copies.1), calls=%async_computation.1 | async-start | bytes 262144 | tf_op jit(solution)/shard_map/all_to_all | solution.py:30
  61.6 2.5 %collective-permute-start.3 = (bf16[1,8,64,128]{3,2,1,0:T(8,128)(2,1)S(1)}, bf16[1,8,64,128]{3,2,1,0:T(8,128)(2,1)S(1)}, u32[]{:S(2)}, u32[]{:S(2)}) collective-permute-start(bf16[1,8,64,128]{3,2,1,0:T(8,128)(2,1)S(1)} %get-tuple-element.18), channel_id=1, source_target_pairs={{0,1},{1,2},{2,3},{3,4},{4,5},{5,6},{6,7},{7,8},{8,9},{9,10},{10,1... | collective-permute-start | bytes 393224 | tf_op jit(solution)/shard_map/ppermute | solution.py:22
  64.1 0.0 copy-done.3
  64.1 0.7 collective-permute-start.4
  64.8 0.0 collective-permute-done.4.after_ref
  64.8 5.2 %collective-permute-done.3.rim_ref = bf16[1,8,64,128]{3,2,1,0:T(8,128)(2,1)S(1)} collective-permute-done((bf16[1,8,64,128]{3,2,1,0:T(8,128)(2,1)S(1)}, bf16[1,8,64,128]{3,2,1,0:T(8,128)(2,1)S(1)}, u32[]{:S(2)}, u32[]{:S(2)}) %collective-permute-start.3) | collective-permute-done | bytes 131104 | tf_op jit(solution)/shard_map/ppermute | solution.py:22
  70.0 0.0 copy-done.1
  70.0 1.5 %finish.1 = (bf16[4,64,128]{2,1,0:T(8,128)(2,1)}, bf16[2,8,64,128]{3,2,1,0:T(8,128)(2,1)}) custom-call(bf16[1,8,64,128]{3,2,1,0:T(8,128)(2,1)S(1)} %collective-permute-done.3.rim_ref, bf16[2,8,64,128]{3,2,1,0:T(8,128)(2,1)S(1)} %bitcast.9, bf16[4,64,128]{2,1,0:T(8,128)(2,1)S(1)} %bitcast.14, bf16[4,64,128]{2,1,0:T(8,128)(2,1)S(1)} %collective-permute-done.later_ref, ...), custom_call_target="tpu_custom_call" | custom-call | flops 400000000 | bytes 1500000 | tf_op jit(solution)/shard_map/finish/pallas_call | solution.py:235
  71.5 15.8 %all-to-all-done.1 = bf16[16,32,128]{2,1,0:T(8,128)(2,1)S(1)} async-done(((bf16[16,32,128]{2,1,0:T(8,128)(2,1)}), bf16[16,32,128]{2,1,0:T(8,128)(2,1)S(1)}, u32[]{:S(2)}, u32[]{:S(2)}) %all-to-all-start.1) | async-done | bytes 131104 | tf_op jit(solution)/shard_map/all_to_all | solution.py:30
  87.3 0.1 broadcast_in_dim.14
  87.3 19.7 %all_to_all.16.chunks_ref = bf16[64,32,128]{2,1,0:T(8,128)(2,1)S(1)} all-to-all(bf16[64,32,128]{2,1,0:T(8,128)(2,1)S(1)} %broadcast_in_dim.14), channel_id=1, replica_groups=mesh['x'=4,'zh'=4,'y'=4,'zn'=4,'ze'=2,'c'=2] {'x','y','ze','c'}, dimensions={0} | all-to-all | bytes 1048576 | tf_op jit(solution)/shard_map/all_to_all | solution.py:30
  107.1 1.0 spread_out.1
  (1 shorter events, 0.0 us)
Async XLA Ops:
  0.6 18.4 %copy-start = (bf16[1,2,8,64,128]{4,3,2,1,0:T(8,128)(2,1)S(1)}, bf16[1,2,8,64,128]{4,3,2,1,0:T(8,128)(2,1)}, u32[]{:S(2)}) copy-start(bf16[1,2,8,64,128]{4,3,2,1,0:T(8,128)(2,1)} %param.3) | copy-start | bytes 786436
  1.6 18.6 %collective-permute-start.1 = (bf16[1,8,64,128]{3,2,1,0:T(8,128)(2,1)S(1)}, bf16[1,8,64,128]{3,2,1,0:T(8,128)(2,1)S(1)}, u32[]{:S(2)}, u32[]{:S(2)}) collective-permute-start(bf16[1,8,64,128]{3,2,1,0:T(8,128)(2,1)S(1)} %slice_bitcast_fusion), channel_id=1, source_target_pairs={{15,24},{31,40},{47,56},{79,88},{95,104},{111,120},{143,152},{159,... | collective-permute-start | bytes 393224 | tf_op jit(solution)/shard_map/ppermute | solution.py:26
  2.3 17.9 %collective-permute-start.2 = (bf16[4,64,128]{2,1,0:T(8,128)(2,1)}, bf16[4,64,128]{2,1,0:T(8,128)(2,1)S(1)}, u32[]{:S(2)}, u32[]{:S(2)}) collective-permute-start(bf16[4,64,128]{2,1,0:T(8,128)(2,1)} %bitcast.10), channel_id=1, source_target_pairs={{16,24},{32,40},{48,56},{80,88},{96,104},{112,120},{144,152},{160,... | collective-permute-start | bytes 196616 | tf_op jit(solution)/shard_map/ppermute | solution.py:26
  3.0 17.2 %collective-permute-start = (bf16[4,64,128]{2,1,0:T(8,128)(2,1)}, bf16[4,64,128]{2,1,0:T(8,128)(2,1)S(1)}, u32[]{:S(2)}, u32[]{:S(2)}) collective-permute-start(bf16[4,64,128]{2,1,0:T(8,128)(2,1)} %bitcast.11), channel_id=1, source_target_pairs={{1,0},{2,1},{3,2},{4,3},{5,4},{6,5},{7,6},{8,7},{9,8},{10,9},{11,1... | collective-permute-start | bytes 196616 | tf_op jit(solution)/shard_map/ppermute | solution.py:26
  19.1 0.8 copy-start.2
  37.3 32.7 %copy-start.1 = (bf16[3,3,3,64,128]{4,3,2,1,0:T(8,128)(2,1)S(1)}, bf16[3,3,3,64,128]{4,3,2,1,0:T(8,128)(2,1)}, u32[]{:S(2)}) copy-start(bf16[3,3,3,64,128]{4,3,2,1,0:T(8,128)(2,1)} %weight_ref.1) | copy-start | bytes 1327108
  38.1 26.0 %copy-start.3 = (bf16[1,1,4,64,128]{4,3,2,1,0:T(8,128)(2,1)S(1)}, bf16[1,1,4,64,128]{4,3,2,1,0:T(8,128)(2,1)}, u32[]{:S(2)}) copy-start(bf16[1,1,4,64,128]{4,3,2,1,0:T(8,128)(2,1)} %param.5) | copy-start | bytes 196612
  38.1 49.2 %all-to-all-start.1 = ((bf16[16,32,128]{2,1,0:T(8,128)(2,1)}), bf16[16,32,128]{2,1,0:T(8,128)(2,1)S(1)}, u32[]{:S(2)}, u32[]{:S(2)}) async-start(bf16[16,32,128]{2,1,0:T(8,128)(2,1)} %copies.1), calls=%async_computation.1 | async-start | bytes 262144 | tf_op jit(solution)/shard_map/all_to_all | solution.py:30
  61.6 8.4 %collective-permute-start.3 = (bf16[1,8,64,128]{3,2,1,0:T(8,128)(2,1)S(1)}, bf16[1,8,64,128]{3,2,1,0:T(8,128)(2,1)S(1)}, u32[]{:S(2)}, u32[]{:S(2)}) collective-permute-start(bf16[1,8,64,128]{3,2,1,0:T(8,128)(2,1)S(1)} %get-tuple-element.18), channel_id=1, source_target_pairs={{0,1},{1,2},{2,3},{3,4},{4,5},{5,6},{6,7},{7,8},{8,9},{9,10},{10,1... | collective-permute-start | bytes 393224 | tf_op jit(solution)/shard_map/ppermute | solution.py:22
  64.1 0.7 collective-permute-start.4

commit v11 on v7

--- a/solution.py
+++ b/solution.py
@@ -10,8 +10,8 @@
 
 DP = ("x", "zh")
 SPACE = ("y", "zn", "ze", "c")
-SLAB = ("x", "y", "ze", "c")
-LINE = ("zh", "zn")
+SLAB = ("c", "ze", "y", "x")
+LINE = ("zn", "zh")
 SIZES = (4, 4, 4, 4, 2, 2)
 VMEM_BYTES = 16 << 20
 

time: 109 us -> 107 us (0.982)
  waiting for transfers between devices: 21.7 us -> 18.5 us
  blocking collectives: 37.9 us -> 39.6 us
    all_to_all x1, waiting for transfers between devices: 15.8 us -> 11.2 us  [exchange(): return lax.all_to_all(value, axes, 0, 0, tiled=True)]
    all_to_all x2, blocking collectives: 37.9 us -> 39.6 us  [exchange(): return lax.all_to_all(value, axes, 0, 0, tiled=True)]
    ppermute x2, waiting for transfers between devices: 5.9 us -> 7.21 us  [passed_along(): lax.ppermute(value, axes, [(source, source + steps) for source in range(f...]
where the time goes in v11:
time: 107 us
  starting transfers between devices  42.7 us (40%)
  blocking collectives  39.6 us (37%)
  waiting for transfers between devices  18.5 us (17%)
  Pallas kernels  3.76 us (4%)
  local copies, waits for them, and re-layouts  1.87 us (2%)
    all_to_all x2, blocking collectives, exchange(): return lax.all_to_all(value, axes, 0, 0, tiled=True)  39.6 us
    all_to_all x1, starting transfers between devices, exchange(): return lax.all_to_all(value, axes, 0, 0, tiled=True)  23.7 us
    ppermute x2, starting transfers between devices, passed_along(): lax.ppermute(value, axes, [(source, source + steps) for source in range(f...  19 us
    all_to_all x1, waiting for transfers between devices, exchange(): return lax.all_to_all(value, axes, 0, 0, tiled=True)  11.2 us
    ppermute x2, waiting for transfers between devices, passed_along(): lax.ppermute(value, axes, [(source, source + steps) for source in range(f...  7.21 us
  transfers between devices with their start and end apart: 3, of which 2 were waited for; matrix products, arithmetic and copies ran while one was open for 0% of the time, Pallas kernels for 2%

profile of v11, /device:TPU:1, one launch (start us, length us, event | category | flops | bytes accessed | tf_op | source)
XLA Modules:
  0.0 107.1 jit_solution(7948200690069753020)
XLA Ops:
  0.6 16.1 %collective-permute-start = (bf16[4,64,128]{2,1,0:T(8,128)(2,1)}, bf16[4,64,128]{2,1,0:T(8,128)(2,1)S(1)}, u32[]{:S(2)}, u32[]{:S(2)}) collective-permute-start(bf16[4,64,128]{2,1,0:T(8,128)(2,1)} %bitcast.8), channel_id=1, source_target_pairs={{1,0},{2,1},{3,2},{4,3},{5,4},{6,5},{7,6},{8,7},{9,8},{10,9},{11,1... | collective-permute-start | bytes 196616 | tf_op jit(solution)/shard_map/ppermute | solution.py:22
  16.7 0.0 copy-start
  16.7 0.9 copy-done
  17.7 0.0 copy-start.3
  17.7 0.8 copy-done.3
  18.5 0.3 own.1
  18.8 0.0 collective-permute-done.later_ref
  18.8 0.3 joined.1
  19.1 18.1 %all_to_all.15.chunks_ref = bf16[64,32,128]{2,1,0:T(8,128)(2,1)S(1)} all-to-all(bf16[64,32,128]{2,1,0:T(8,128)(2,1)S(1)} %joined.1), channel_id=1, replica_groups=mesh['x'=4,'zh'=4,'y'=4,'zn'=4,'ze'=2,'c'=2] {'c','ze','y','x'}, dimensions={0} | all-to-all | bytes 1048576 | tf_op jit(solution)/shard_map/all_to_all | solution.py:26
  37.2 0.0 copy-start.2
  37.2 0.0 copy-start.4
  37.2 0.7 copies.1
  37.9 0.0 copy-start.1
  37.9 23.7 %all-to-all-start.1 = ((bf16[16,32,128]{2,1,0:T(8,128)(2,1)}), bf16[16,32,128]{2,1,0:T(8,128)(2,1)S(1)}, u32[]{:S(2)}, u32[]{:S(2)}) async-start(bf16[16,32,128]{2,1,0:T(8,128)(2,1)} %copies.1), calls=%async_computation.1 | async-start | bytes 262144 | tf_op jit(solution)/shard_map/all_to_all | solution.py:26
  61.6 2.9 %collective-permute-start.1 = (bf16[1,8,64,128]{3,2,1,0:T(8,128)(2,1)S(1)}, bf16[1,8,64,128]{3,2,1,0:T(8,128)(2,1)S(1)}, u32[]{:S(2)}, u32[]{:S(2)}) collective-permute-start(bf16[1,8,64,128]{3,2,1,0:T(8,128)(2,1)S(1)} %get-tuple-element.18), channel_id=1, source_target_pairs={{0,1},{1,2},{2,3},{3,4},{4,5},{5,6},{6,7},{7,8},{8,9},{9,10},{10,1... | collective-permute-start | bytes 393224 | tf_op jit(solution)/shard_map/ppermute | solution.py:22
  64.5 7.2 %collective-permute-done.1.rim_ref = bf16[1,8,64,128]{3,2,1,0:T(8,128)(2,1)S(1)} collective-permute-done((bf16[1,8,64,128]{3,2,1,0:T(8,128)(2,1)S(1)}, bf16[1,8,64,128]{3,2,1,0:T(8,128)(2,1)S(1)}, u32[]{:S(2)}, u32[]{:S(2)}) %collective-permute-start.1) | collective-permute-done | bytes 131104 | tf_op jit(solution)/shard_map/ppermute | solution.py:22
  71.7 0.0 copy-done.2
  71.7 0.0 copy-done.4
  71.7 0.0 copy-done.1
  71.7 1.5 %finish.1 = (bf16[4,64,128]{2,1,0:T(8,128)(2,1)}, bf16[2,8,64,128]{3,2,1,0:T(8,128)(2,1)}) custom-call(bf16[1,8,64,128]{3,2,1,0:T(8,128)(2,1)S(1)} %collective-permute-done.1.rim_ref, bf16[2,8,64,128]{3,2,1,0:T(8,128)(2,1)S(1)} %bitcast.7, bf16[4,64,128]{2,1,0:T(8,128)(2,1)S(1)} %bitcast.10, bf16[4,64,128]{2,1,0:T(8,128)(2,1)S(1)} %collective-permute-done.later_ref, ...), custom_call_target="tpu_custom_call" | custom-call | flops 400000000 | bytes 1500000 | tf_op jit(solution)/shard_map/finish/pallas_call | solution.py:217
  73.2 11.2 %all-to-all-done.1 = bf16[16,32,128]{2,1,0:T(8,128)(2,1)S(1)} async-done(((bf16[16,32,128]{2,1,0:T(8,128)(2,1)}), bf16[16,32,128]{2,1,0:T(8,128)(2,1)S(1)}, u32[]{:S(2)}, u32[]{:S(2)}) %all-to-all-start.1) | async-done | bytes 131104 | tf_op jit(solution)/shard_map/all_to_all | solution.py:26
  84.5 0.1 broadcast_in_dim.14
  84.6 21.6 %all_to_all.16.chunks_ref = bf16[64,32,128]{2,1,0:T(8,128)(2,1)S(1)} all-to-all(bf16[64,32,128]{2,1,0:T(8,128)(2,1)S(1)} %broadcast_in_dim.14), channel_id=1, replica_groups=mesh['x'=4,'zh'=4,'y'=4,'zn'=4,'ze'=2,'c'=2] {'c','ze','y','x'}, dimensions={0} | all-to-all | bytes 1048576 | tf_op jit(solution)/shard_map/all_to_all | solution.py:26
  106.1 1.0 spread_out.1
  (1 shorter events, 0.0 us)
Async XLA Ops:
  0.6 18.2 %collective-permute-start = (bf16[4,64,128]{2,1,0:T(8,128)(2,1)}, bf16[4,64,128]{2,1,0:T(8,128)(2,1)S(1)}, u32[]{:S(2)}, u32[]{:S(2)}) collective-permute-start(bf16[4,64,128]{2,1,0:T(8,128)(2,1)} %bitcast.8), channel_id=1, source_target_pairs={{1,0},{2,1},{3,2},{4,3},{5,4},{6,5},{7,6},{8,7},{9,8},{10,9},{11,1... | collective-permute-start | bytes 196616 | tf_op jit(solution)/shard_map/ppermute | solution.py:22
  16.7 1.0 copy-start
  17.7 0.8 copy-start.3
  37.2 34.6 %copy-start.2 = (bf16[3,3,3,64,128]{4,3,2,1,0:T(8,128)(2,1)S(1)}, bf16[3,3,3,64,128]{4,3,2,1,0:T(8,128)(2,1)}, u32[]{:S(2)}) copy-start(bf16[3,3,3,64,128]{4,3,2,1,0:T(8,128)(2,1)} %weight_ref.1) | copy-start | bytes 1327108
  37.2 34.6 %copy-start.4 = (bf16[1,1,4,64,128]{4,3,2,1,0:T(8,128)(2,1)S(1)}, bf16[1,1,4,64,128]{4,3,2,1,0:T(8,128)(2,1)}, u32[]{:S(2)}) copy-start(bf16[1,1,4,64,128]{4,3,2,1,0:T(8,128)(2,1)} %param.5) | copy-start | bytes 196612
  37.9 33.8 %copy-start.1 = (bf16[1,2,8,64,128]{4,3,2,1,0:T(8,128)(2,1)S(1)}, bf16[1,2,8,64,128]{4,3,2,1,0:T(8,128)(2,1)}, u32[]{:S(2)}) copy-start(bf16[1,2,8,64,128]{4,3,2,1,0:T(8,128)(2,1)} %param.3) | copy-start | bytes 786436
  37.9 46.6 %all-to-all-start.1 = ((bf16[16,32,128]{2,1,0:T(8,128)(2,1)}), bf16[16,32,128]{2,1,0:T(8,128)(2,1)S(1)}, u32[]{:S(2)}, u32[]{:S(2)}) async-start(bf16[16,32,128]{2,1,0:T(8,128)(2,1)} %copies.1), calls=%async_computation.1 | async-start | bytes 262144 | tf_op jit(solution)/shard_map/all_to_all | solution.py:26
  61.6 10.2 %collective-permute-start.1 = (bf16[1,8,64,128]{3,2,1,0:T(8,128)(2,1)S(1)}, bf16[1,8,64,128]{3,2,1,0:T(8,128)(2,1)S(1)}, u32[]{:S(2)}, u32[]{:S(2)}) collective-permute-start(bf16[1,8,64,128]{3,2,1,0:T(8,128)(2,1)S(1)} %get-tuple-element.18), channel_id=1, source_target_pairs={{0,1},{1,2},{2,3},{3,4},{4,5},{5,6},{6,7},{7,8},{8,9},{9,10},{10,1... | collective-permute-start | bytes 393224 | tf_op jit(solution)/shard_map/ppermute | solution.py:22

commit v12 on v10

--- a/solution.py
+++ b/solution.py
@@ -10,8 +10,8 @@
 
 DP = ("x", "zh")
 SPACE = ("y", "zn", "ze", "c")
-SLAB = ("x", "y", "ze", "c")
-LINE = ("zh", "zn")
+SLAB = ("c", "ze", "y", "x")
+LINE = ("zn", "zh")
 SIZES = (4, 4, 4, 4, 2, 2)
 VMEM_BYTES = 16 << 20
 

time: 108 us -> 107 us (level)
  waiting for transfers between devices: 21 us -> 17.8 us
  blocking collectives: 36.5 us -> 38.2 us
    all_to_all x1, waiting for transfers between devices: 15.8 us -> 11.2 us  [exchange(): return lax.all_to_all(value, axes, 0, 0, tiled=True)]
    all_to_all x2, blocking collectives: 36.5 us -> 38.2 us  [exchange(): return lax.all_to_all(value, axes, 0, 0, tiled=True)]
    ppermute x1, waiting for transfers between devices: 5.21 us -> 6.52 us  [passed_along(): lax.ppermute(value, axes, [(source, source + steps) for source in range(f...]
where the time goes in v12:
time: 107 us
  starting transfers between devices  44.5 us (42%)
  blocking collectives  38.2 us (36%)
  waiting for transfers between devices  17.8 us (17%)
  Pallas kernels  3.83 us (4%)
  local copies, waits for them, and re-layouts  1.9 us (2%)
    all_to_all x2, blocking collectives, exchange(): return lax.all_to_all(value, axes, 0, 0, tiled=True)  38.2 us
    all_to_all x1, starting transfers between devices, exchange(): return lax.all_to_all(value, axes, 0, 0, tiled=True)  23.5 us
    ppermute x4, starting transfers between devices, sent(): return lax.ppermute(value, SPACE, pairs)  18.1 us
    all_to_all x1, waiting for transfers between devices, exchange(): return lax.all_to_all(value, axes, 0, 0, tiled=True)  11.2 us
    ppermute x1, waiting for transfers between devices, passed_along(): lax.ppermute(value, axes, [(source, source + steps) for source in range(f...  6.52 us
    ppermute x1, starting transfers between devices, passed_along(): lax.ppermute(value, axes, [(source, source + steps) for source in range(f...  2.94 us
  transfers between devices with their start and end apart: 6, of which 2 were waited for; matrix products, arithmetic and copies ran while one was open for 0% of the time, Pallas kernels for 2%

profile of v12, /device:TPU:1, one launch (start us, length us, event | category | flops | bytes accessed | tf_op | source)
XLA Modules:
  0.0 107.0 jit_solution(5453093432531169102)
XLA Ops:
  0.6 0.0 copy-start
  0.6 1.0 slice_bitcast_fusion
  1.6 0.7 collective-permute-start.1
  2.3 0.7 collective-permute-start.2
  3.0 16.1 %collective-permute-start = (bf16[4,64,128]{2,1,0:T(8,128)(2,1)}, bf16[4,64,128]{2,1,0:T(8,128)(2,1)S(1)}, u32[]{:S(2)}, u32[]{:S(2)}) collective-permute-start(bf16[4,64,128]{2,1,0:T(8,128)(2,1)} %bitcast.11), channel_id=1, source_target_pairs={{1,0},{2,1},{3,2},{4,3},{5,4},{6,5},{7,6},{8,7},{9,8},{10,9},{11,1... | collective-permute-start | bytes 196616 | tf_op jit(solution)/shard_map/ppermute | solution.py:26
  19.0 0.0 copy-done
  19.1 0.0 copy-start.2
  19.1 0.8 copy-done.2
  19.9 0.3 own.1
  20.2 0.0 collective-permute-done.2.far_grads_ref
  20.2 0.0 collective-permute-done.later_ref
  20.2 0.0 collective-permute-done.1.far_plane_ref
  20.2 0.3 joined.1
  20.6 16.6 %all_to_all.15.chunks_ref = bf16[64,32,128]{2,1,0:T(8,128)(2,1)S(1)} all-to-all(bf16[64,32,128]{2,1,0:T(8,128)(2,1)S(1)} %joined.1), channel_id=1, replica_groups=mesh['x'=4,'zh'=4,'y'=4,'zn'=4,'ze'=2,'c'=2] {'c','ze','y','x'}, dimensions={0} | all-to-all | bytes 1048576 | tf_op jit(solution)/shard_map/all_to_all | solution.py:30
  37.2 0.0 copy-start.1
  37.2 0.7 copies.1
  37.9 0.0 copy-start.3
  37.9 23.5 %all-to-all-start.1 = ((bf16[16,32,128]{2,1,0:T(8,128)(2,1)}), bf16[16,32,128]{2,1,0:T(8,128)(2,1)S(1)}, u32[]{:S(2)}, u32[]{:S(2)}) async-start(bf16[16,32,128]{2,1,0:T(8,128)(2,1)} %copies.1), calls=%async_computation.1 | async-start | bytes 262144 | tf_op jit(solution)/shard_map/all_to_all | solution.py:30
  61.4 2.9 %collective-permute-start.3 = (bf16[1,8,64,128]{3,2,1,0:T(8,128)(2,1)S(1)}, bf16[1,8,64,128]{3,2,1,0:T(8,128)(2,1)S(1)}, u32[]{:S(2)}, u32[]{:S(2)}) collective-permute-start(bf16[1,8,64,128]{3,2,1,0:T(8,128)(2,1)S(1)} %get-tuple-element.18), channel_id=1, source_target_pairs={{0,1},{1,2},{2,3},{3,4},{4,5},{5,6},{6,7},{7,8},{8,9},{9,10},{10,1... | collective-permute-start | bytes 393224 | tf_op jit(solution)/shard_map/ppermute | solution.py:22
  64.4 0.0 copy-done.3
  64.4 0.7 collective-permute-start.4
  65.1 0.0 collective-permute-done.4.after_ref
  65.1 6.5 %collective-permute-done.3.rim_ref = bf16[1,8,64,128]{3,2,1,0:T(8,128)(2,1)S(1)} collective-permute-done((bf16[1,8,64,128]{3,2,1,0:T(8,128)(2,1)S(1)}, bf16[1,8,64,128]{3,2,1,0:T(8,128)(2,1)S(1)}, u32[]{:S(2)}, u32[]{:S(2)}) %collective-permute-start.3) | collective-permute-done | bytes 131104 | tf_op jit(solution)/shard_map/ppermute | solution.py:22
  71.6 0.0 copy-done.1
  71.6 1.5 %finish.1 = (bf16[4,64,128]{2,1,0:T(8,128)(2,1)}, bf16[2,8,64,128]{3,2,1,0:T(8,128)(2,1)}) custom-call(bf16[1,8,64,128]{3,2,1,0:T(8,128)(2,1)S(1)} %collective-permute-done.3.rim_ref, bf16[2,8,64,128]{3,2,1,0:T(8,128)(2,1)S(1)} %bitcast.9, bf16[4,64,128]{2,1,0:T(8,128)(2,1)S(1)} %bitcast.14, bf16[4,64,128]{2,1,0:T(8,128)(2,1)S(1)} %collective-permute-done.later_ref, ...), custom_call_target="tpu_custom_call" | custom-call | flops 400000000 | bytes 1500000 | tf_op jit(solution)/shard_map/finish/pallas_call | solution.py:235
  73.1 11.2 %all-to-all-done.1 = bf16[16,32,128]{2,1,0:T(8,128)(2,1)S(1)} async-done(((bf16[16,32,128]{2,1,0:T(8,128)(2,1)}), bf16[16,32,128]{2,1,0:T(8,128)(2,1)S(1)}, u32[]{:S(2)}, u32[]{:S(2)}) %all-to-all-start.1) | async-done | bytes 131104 | tf_op jit(solution)/shard_map/all_to_all | solution.py:30
  84.3 0.1 broadcast_in_dim.14
  84.4 21.6 %all_to_all.16.chunks_ref = bf16[64,32,128]{2,1,0:T(8,128)(2,1)S(1)} all-to-all(bf16[64,32,128]{2,1,0:T(8,128)(2,1)S(1)} %broadcast_in_dim.14), channel_id=1, replica_groups=mesh['x'=4,'zh'=4,'y'=4,'zn'=4,'ze'=2,'c'=2] {'c','ze','y','x'}, dimensions={0} | all-to-all | bytes 1048576 | tf_op jit(solution)/shard_map/all_to_all | solution.py:30
  106.0 1.0 spread_out.1
  (1 shorter events, 0.0 us)
Async XLA Ops:
  0.6 18.4 %copy-start = (bf16[1,2,8,64,128]{4,3,2,1,0:T(8,128)(2,1)S(1)}, bf16[1,2,8,64,128]{4,3,2,1,0:T(8,128)(2,1)}, u32[]{:S(2)}) copy-start(bf16[1,2,8,64,128]{4,3,2,1,0:T(8,128)(2,1)} %param.3) | copy-start | bytes 786436
  1.6 18.6 %collective-permute-start.1 = (bf16[1,8,64,128]{3,2,1,0:T(8,128)(2,1)S(1)}, bf16[1,8,64,128]{3,2,1,0:T(8,128)(2,1)S(1)}, u32[]{:S(2)}, u32[]{:S(2)}) collective-permute-start(bf16[1,8,64,128]{3,2,1,0:T(8,128)(2,1)S(1)} %slice_bitcast_fusion), channel_id=1, source_target_pairs={{15,24},{31,40},{47,56},{79,88},{95,104},{111,120},{143,152},{159,... | collective-permute-start | bytes 393224 | tf_op jit(solution)/shard_map/ppermute | solution.py:26
  2.3 17.9 %collective-permute-start.2 = (bf16[4,64,128]{2,1,0:T(8,128)(2,1)}, bf16[4,64,128]{2,1,0:T(8,128)(2,1)S(1)}, u32[]{:S(2)}, u32[]{:S(2)}) collective-permute-start(bf16[4,64,128]{2,1,0:T(8,128)(2,1)} %bitcast.10), channel_id=1, source_target_pairs={{16,24},{32,40},{48,56},{80,88},{96,104},{112,120},{144,152},{160,... | collective-permute-start | bytes 196616 | tf_op jit(solution)/shard_map/ppermute | solution.py:26
  3.0 17.2 %collective-permute-start = (bf16[4,64,128]{2,1,0:T(8,128)(2,1)}, bf16[4,64,128]{2,1,0:T(8,128)(2,1)S(1)}, u32[]{:S(2)}, u32[]{:S(2)}) collective-permute-start(bf16[4,64,128]{2,1,0:T(8,128)(2,1)} %bitcast.11), channel_id=1, source_target_pairs={{1,0},{2,1},{3,2},{4,3},{5,4},{6,5},{7,6},{8,7},{9,8},{10,9},{11,1... | collective-permute-start | bytes 196616 | tf_op jit(solution)/shard_map/ppermute | solution.py:26
  19.1 0.8 copy-start.2
  37.2 34.4 %copy-start.1 = (bf16[3,3,3,64,128]{4,3,2,1,0:T(8,128)(2,1)S(1)}, bf16[3,3,3,64,128]{4,3,2,1,0:T(8,128)(2,1)}, u32[]{:S(2)}) copy-start(bf16[3,3,3,64,128]{4,3,2,1,0:T(8,128)(2,1)} %weight_ref.1) | copy-start | bytes 1327108
  37.9 26.4 %copy-start.3 = (bf16[1,1,4,64,128]{4,3,2,1,0:T(8,128)(2,1)S(1)}, bf16[1,1,4,64,128]{4,3,2,1,0:T(8,128)(2,1)}, u32[]{:S(2)}) copy-start(bf16[1,1,4,64,128]{4,3,2,1,0:T(8,128)(2,1)} %param.5) | copy-start | bytes 196612
  37.9 46.4 %all-to-all-start.1 = ((bf16[16,32,128]{2,1,0:T(8,128)(2,1)}), bf16[16,32,128]{2,1,0:T(8,128)(2,1)S(1)}, u32[]{:S(2)}, u32[]{:S(2)}) async-start(bf16[16,32,128]{2,1,0:T(8,128)(2,1)} %copies.1), calls=%async_computation.1 | async-start | bytes 262144 | tf_op jit(solution)/shard_map/all_to_all | solution.py:30
  61.4 10.2 %collective-permute-start.3 = (bf16[1,8,64,128]{3,2,1,0:T(8,128)(2,1)S(1)}, bf16[1,8,64,128]{3,2,1,0:T(8,128)(2,1)S(1)}, u32[]{:S(2)}, u32[]{:S(2)}) collective-permute-start(bf16[1,8,64,128]{3,2,1,0:T(8,128)(2,1)S(1)} %get-tuple-element.18), channel_id=1, source_target_pairs={{0,1},{1,2},{2,3},{3,4},{4,5},{5,6},{6,7},{7,8},{8,9},{9,10},{10,1... | collective-permute-start | bytes 393224 | tf_op jit(solution)/shard_map/ppermute | solution.py:22
  64.4 0.7 collective-permute-start.4

commit v13 on v11

--- a/solution.py
+++ b/solution.py
@@ -227,8 +227,12 @@
     piece, output, grad_volume = lax.optimization_barrier((piece, output, grad_volume))
     copies = jnp.broadcast_to(piece.astype(jnp.bfloat16)[None], (count, rows, cout))
     gathered = exchange(copies, SLAB)
+    parts = 4
     grad_weight = pl.pallas_call(
         functools.partial(spread_kernel, step, factor),
+        grid=(parts,),
+        in_specs=[pl.BlockSpec((count // parts, rows, cout), lambda part: (part, 0, 0))],
+        out_specs=pl.BlockSpec((total // parts, cout), lambda part: (part, 0)),
         out_shape=jax.ShapeDtypeStruct((total, cout), jnp.float32),
         compiler_params=pltpu.CompilerParams(vmem_limit_bytes=VMEM_BYTES),
         name="spread_out",

time: 107 us -> 108 us (level)
  no operation moved by 1% of the time
where the time goes in v13:
time: 108 us
  starting transfers between devices  42.7 us (40%)
  blocking collectives  39.6 us (37%)
  waiting for transfers between devices  18.5 us (17%)
  Pallas kernels  4.26 us (4%)
  local copies, waits for them, and re-layouts  1.87 us (2%)
    all_to_all x2, blocking collectives, exchange(): return lax.all_to_all(value, axes, 0, 0, tiled=True)  39.6 us
    all_to_all x1, starting transfers between devices, exchange(): return lax.all_to_all(value, axes, 0, 0, tiled=True)  23.7 us
    ppermute x2, starting transfers between devices, passed_along(): lax.ppermute(value, axes, [(source, source + steps) for source in range(f...  19 us
    all_to_all x1, waiting for transfers between devices, exchange(): return lax.all_to_all(value, axes, 0, 0, tiled=True)  11.2 us
    ppermute x2, waiting for transfers between devices, passed_along(): lax.ppermute(value, axes, [(source, source + steps) for source in range(f...  7.21 us
  transfers between devices with their start and end apart: 3, of which 2 were waited for; matrix products, arithmetic and copies ran while one was open for 0% of the time, Pallas kernels for 2%

profile of v13, /device:TPU:1, one launch (start us, length us, event | category | flops | bytes accessed | tf_op | source)
XLA Modules:
  0.0 107.6 jit_solution(11012310936352409075)
XLA Ops:
  0.6 16.1 %collective-permute-start = (bf16[4,64,128]{2,1,0:T(8,128)(2,1)}, bf16[4,64,128]{2,1,0:T(8,128)(2,1)S(1)}, u32[]{:S(2)}, u32[]{:S(2)}) collective-permute-start(bf16[4,64,128]{2,1,0:T(8,128)(2,1)} %bitcast.8), channel_id=1, source_target_pairs={{1,0},{2,1},{3,2},{4,3},{5,4},{6,5},{7,6},{8,7},{9,8},{10,9},{11,1... | collective-permute-start | bytes 196616 | tf_op jit(solution)/shard_map/ppermute | solution.py:22
  16.7 0.0 copy-start
  16.7 0.9 copy-done
  17.7 0.0 copy-start.3
  17.7 0.8 copy-done.3
  18.5 0.3 own.1
  18.8 0.0 collective-permute-done.later_ref
  18.8 0.3 joined.1
  19.1 18.1 %all_to_all.15.chunks_ref = bf16[64,32,128]{2,1,0:T(8,128)(2,1)S(1)} all-to-all(bf16[64,32,128]{2,1,0:T(8,128)(2,1)S(1)} %joined.1), channel_id=1, replica_groups=mesh['x'=4,'zh'=4,'y'=4,'zn'=4,'ze'=2,'c'=2] {'c','ze','y','x'}, dimensions={0} | all-to-all | bytes 1048576 | tf_op jit(solution)/shard_map/all_to_all | solution.py:26
  37.2 0.0 copy-start.2
  37.2 0.0 copy-start.4
  37.2 0.7 copies.1
  37.9 0.0 copy-start.1
  37.9 23.7 %all-to-all-start.1 = ((bf16[16,32,128]{2,1,0:T(8,128)(2,1)}), bf16[16,32,128]{2,1,0:T(8,128)(2,1)S(1)}, u32[]{:S(2)}, u32[]{:S(2)}) async-start(bf16[16,32,128]{2,1,0:T(8,128)(2,1)} %copies.1), calls=%async_computation.1 | async-start | bytes 262144 | tf_op jit(solution)/shard_map/all_to_all | solution.py:26
  61.6 2.9 %collective-permute-start.1 = (bf16[1,8,64,128]{3,2,1,0:T(8,128)(2,1)S(1)}, bf16[1,8,64,128]{3,2,1,0:T(8,128)(2,1)S(1)}, u32[]{:S(2)}, u32[]{:S(2)}) collective-permute-start(bf16[1,8,64,128]{3,2,1,0:T(8,128)(2,1)S(1)} %get-tuple-element.18), channel_id=1, source_target_pairs={{0,1},{1,2},{2,3},{3,4},{4,5},{5,6},{6,7},{7,8},{8,9},{9,10},{10,1... | collective-permute-start | bytes 393224 | tf_op jit(solution)/shard_map/ppermute | solution.py:22
  64.5 7.2 %collective-permute-done.1.rim_ref = bf16[1,8,64,128]{3,2,1,0:T(8,128)(2,1)S(1)} collective-permute-done((bf16[1,8,64,128]{3,2,1,0:T(8,128)(2,1)S(1)}, bf16[1,8,64,128]{3,2,1,0:T(8,128)(2,1)S(1)}, u32[]{:S(2)}, u32[]{:S(2)}) %collective-permute-start.1) | collective-permute-done | bytes 131104 | tf_op jit(solution)/shard_map/ppermute | solution.py:22
  71.7 0.0 copy-done.2
  71.7 0.0 copy-done.4
  71.7 0.0 copy-done.1
  71.7 1.5 %finish.1 = (bf16[4,64,128]{2,1,0:T(8,128)(2,1)}, bf16[2,8,64,128]{3,2,1,0:T(8,128)(2,1)}) custom-call(bf16[1,8,64,128]{3,2,1,0:T(8,128)(2,1)S(1)} %collective-permute-done.1.rim_ref, bf16[2,8,64,128]{3,2,1,0:T(8,128)(2,1)S(1)} %bitcast.7, bf16[4,64,128]{2,1,0:T(8,128)(2,1)S(1)} %bitcast.10, bf16[4,64,128]{2,1,0:T(8,128)(2,1)S(1)} %collective-permute-done.later_ref, ...), custom_call_target="tpu_custom_call" | custom-call | flops 400000000 | bytes 1500000 | tf_op jit(solution)/shard_map/finish/pallas_call | solution.py:217
  73.2 11.2 %all-to-all-done.1 = bf16[16,32,128]{2,1,0:T(8,128)(2,1)S(1)} async-done(((bf16[16,32,128]{2,1,0:T(8,128)(2,1)}), bf16[16,32,128]{2,1,0:T(8,128)(2,1)S(1)}, u32[]{:S(2)}, u32[]{:S(2)}) %all-to-all-start.1) | async-done | bytes 131104 | tf_op jit(solution)/shard_map/all_to_all | solution.py:26
  84.5 0.1 broadcast_in_dim.14
  84.6 21.6 %all_to_all.16.chunks_ref = bf16[64,32,128]{2,1,0:T(8,128)(2,1)S(1)} all-to-all(bf16[64,32,128]{2,1,0:T(8,128)(2,1)S(1)} %broadcast_in_dim.14), channel_id=1, replica_groups=mesh['x'=4,'zh'=4,'y'=4,'zn'=4,'ze'=2,'c'=2] {'c','ze','y','x'}, dimensions={0} | all-to-all | bytes 1048576 | tf_op jit(solution)/shard_map/all_to_all | solution.py:26
  106.1 1.5 %spread_out.1 = f32[1728,128]{1,0:T(8,128)} custom-call(bf16[64,32,128]{2,1,0:T(8,128)(2,1)S(1)} %all_to_all.16.chunks_ref), custom_call_target="tpu_custom_call" | custom-call | tf_op jit(solution)/shard_map/spread_out/pallas_call | solution.py:231
  (1 shorter events, 0.0 us)
Async XLA Ops:
  0.6 18.2 %collective-permute-start = (bf16[4,64,128]{2,1,0:T(8,128)(2,1)}, bf16[4,64,128]{2,1,0:T(8,128)(2,1)S(1)}, u32[]{:S(2)}, u32[]{:S(2)}) collective-permute-start(bf16[4,64,128]{2,1,0:T(8,128)(2,1)} %bitcast.8), channel_id=1, source_target_pairs={{1,0},{2,1},{3,2},{4,3},{5,4},{6,5},{7,6},{8,7},{9,8},{10,9},{11,1... | collective-permute-start | bytes 196616 | tf_op jit(solution)/shard_map/ppermute | solution.py:22
  16.7 1.0 copy-start
  17.7 0.8 copy-start.3
  37.2 34.6 %copy-start.2 = (bf16[3,3,3,64,128]{4,3,2,1,0:T(8,128)(2,1)S(1)}, bf16[3,3,3,64,128]{4,3,2,1,0:T(8,128)(2,1)}, u32[]{:S(2)}) copy-start(bf16[3,3,3,64,128]{4,3,2,1,0:T(8,128)(2,1)} %weight_ref.1) | copy-start | bytes 1327108
  37.2 34.6 %copy-start.4 = (bf16[1,1,4,64,128]{4,3,2,1,0:T(8,128)(2,1)S(1)}, bf16[1,1,4,64,128]{4,3,2,1,0:T(8,128)(2,1)}, u32[]{:S(2)}) copy-start(bf16[1,1,4,64,128]{4,3,2,1,0:T(8,128)(2,1)} %param.5) | copy-start | bytes 196612
  37.9 33.8 %copy-start.1 = (bf16[1,2,8,64,128]{4,3,2,1,0:T(8,128)(2,1)S(1)}, bf16[1,2,8,64,128]{4,3,2,1,0:T(8,128)(2,1)}, u32[]{:S(2)}) copy-start(bf16[1,2,8,64,128]{4,3,2,1,0:T(8,128)(2,1)} %param.3) | copy-start | bytes 786436
  37.9 46.6 %all-to-all-start.1 = ((bf16[16,32,128]{2,1,0:T(8,128)(2,1)}), bf16[16,32,128]{2,1,0:T(8,128)(2,1)S(1)}, u32[]{:S(2)}, u32[]{:S(2)}) async-start(bf16[16,32,128]{2,1,0:T(8,128)(2,1)} %copies.1), calls=%async_computation.1 | async-start | bytes 262144 | tf_op jit(solution)/shard_map/all_to_all | solution.py:26
  61.6 10.2 %collective-permute-start.1 = (bf16[1,8,64,128]{3,2,1,0:T(8,128)(2,1)S(1)}, bf16[1,8,64,128]{3,2,1,0:T(8,128)(2,1)S(1)}, u32[]{:S(2)}, u32[]{:S(2)}) collective-permute-start(bf16[1,8,64,128]{3,2,1,0:T(8,128)(2,1)S(1)} %get-tuple-element.18), channel_id=1, source_target_pairs={{0,1},{1,2},{2,3},{3,4},{4,5},{5,6},{6,7},{7,8},{8,9},{9,10},{10,1... | collective-permute-start | bytes 393224 | tf_op jit(solution)/shard_map/ppermute | solution.py:22
